TPU v7x, 128 devices: a whole 4x4x4 slice. The times are simulated.
128 devices in a mesh: grp: 16 (over y, x_lo, core), tp: 8 (over x_hi, z).
Axes of the slice: x: 4 (x_hi: 2, x_lo: 2; x = x_hi * 2 + x_lo), y: 4, z: 4, core: 2. Of those that a mesh axis runs over, the one named last changes fastest.
Arguments:
- targets: int32 [256], replicated, may hold values from 0 to 31, as said below
- prompt_lens: int32 [256], replicated, may hold values from 1 to 512, 65536 in all
- prompt_kv: bfloat16 [256, 8, 512, 256], P('grp', 'tp'), may hold values from -14 to 14
- cache_pool: bfloat16 [16, 8, 224, 2, 64, 256], P('grp', 'tp'), may hold values from -14 to 14
- block_table: int32 [16, 2, 64, 6], P('grp'), may hold values from 0 to 223, as said below
- cache_lens: int32 [16, 2, 64], P('grp'), may hold values from 1 to 384
- queries: bfloat16 [16, 8, 80, 2048], P('grp', 'tp'), may hold values from -11 to 11
- new_kv: bfloat16 [16, 8, 80, 2, 256], P('grp', 'tp'), may hold values from -14 to 14
Outputs:
- context: bfloat16 [16, 8, 80, 2048], P('grp', 'tp')
- landed: bfloat16 [16, 8, 16, 2, 512, 256], P('grp', 'tp')
Inputs may be any that keep to these rules, and one draw needn't show every extreme that they name: `targets`: value v sends the prompt to decode group v % 2 of serving group v // 2. Each prefill group sends exactly 2 or none of its prompts to each serving group, every serving group receives 16 prompts in all, and one decode group receives up to 16, some decode group exactly 16. `block_table`: for the rows of one decode group, the pages at entries c < ceil(cache_lens / 64) are all distinct; other entries name some page and are not read.
All inputs are finite; a program needn't handle non-finite values.
Results may differ from a plain program's by a relative error of at most 0.0019.
Values may be sent and summed in bfloat16 or wider, within the bound.
No kernel may reach another device: no remote copies, remote signals or barrier semaphores. Data moves between devices by JAX's collectives and lax.ppermute only.
A program may use at most 256 MiB of HBM per device.

v0:
```python
import functools
import math

import jax
import jax.numpy as jnp
import numpy as np
from jax import lax
from jax.experimental import pallas as pl
from jax.experimental.pallas import tpu as pltpu
from jax.sharding import PartitionSpec as P

CHUNK = 32
PROMPT_CHUNKS = 16
OWN_CHUNKS = 256
HOME = 512
X, YA, YB, Z, CORE = 1, 2, 4, 8, 16
ORDERS = ((X, Z, YB, YA), (YA, YB, Z, X), (YB, YA, X, Z), (Z, X, YA, YB))
DEAL = (2, 0, 1, 3, 2, 0, 1, 2, 3, 0, 1, 2, 0, 1, 3, 2)
SHARES = tuple(sum(1 << k for k, part in enumerate(DEAL) if part == q) for q in range(4))
ROOM = ((40, 40, 48, 36), (48, 44, 48, 48), (64, 52, 48, 52), (72, 72, 68, 60))
MIB = 1024 * 1024
SMALL = 4096


def region(phase, part):
    before = [room for rooms in ROOM[:phase] for room in rooms] + list(ROOM[phase][:part])
    return HOME + sum(before)


def space_of(phases):
    return HOME + sum(room for rooms in ROOM[:phases] for room in rooms)


def flipped(group, mask):
    x, core, y = (group >> 1) & 1, group & 1, group >> 2
    if mask & X:
        x ^= 1
    if mask & YA:
        y ^= 1
    if mask & YB:
        y = 3 - y
    if mask & CORE:
        core ^= 1
    return (y << 2) | (x << 1) | core


def hop(value, axis):
    if axis == Z:
        return lax.ppermute(value, "tp", [(t, t ^ 1) for t in range(lax.axis_size("tp"))])
    return lax.ppermute(value, "grp", [(g, flipped(g, axis)) for g in range(lax.axis_size("grp"))])


def node_of(group, parity):
    y = group >> 2
    return (
        ((group >> 1) & 1)
        | (((y ^ (y >> 1)) & 1) << 1)
        | (((y >> 1) & 1) << 2)
        | (parity << 3)
        | ((group & 1) << 4)
    )


def bits_set(word):
    word = word - ((word >> 1) & 0x5555)
    word = (word & 0x3333) + ((word >> 2) & 0x3333)
    word = (word + (word >> 4)) & 0x0F0F
    return (word + (word >> 8)) & 0x1F


def turned(share, by):
    return ((share | (share << 16)) >> by) & 0xFFFF


def below(k):
    return (1 << k) - 1


def plan_kernel(where_ref, targets_ref, lens_ref, const_ref, slots_ref, land_ref):
    me, mine, group = where_ref[0], where_ref[1], where_ref[2]
    row_t = jnp.concatenate([targets_ref[...], targets_ref[...]], axis=1)
    row_l = jnp.concatenate([lens_ref[...], lens_ref[...]], axis=1)
    items = row_t.shape[1]
    prompts = items // 2

    def upright(row):
        down = lax.broadcasted_iota(jnp.int32, (prompts, prompts), 0)
        along = lax.broadcasted_iota(jnp.int32, (prompts, prompts), 1)
        column = jnp.sum(jnp.where(down == along, row[:, :prompts], 0), axis=1, keepdims=True)
        return jnp.concatenate([column, column], axis=0)

    def derive(targets, item):
        prompt = item & (prompts - 1)
        parity = item >> 8
        start = node_of(prompt >> 4, parity)
        end = node_of(targets >> 1, targets & 1)
        start = (start & 15) | (end & CORE)
        return prompt, parity, start, start ^ end

    col_t, col_l = upright(row_t), upright(row_l)
    item = lax.broadcasted_iota(jnp.int32, (items, 1), 0)
    prompt, parity, start, ways = derive(col_t, item)
    chunks = (col_l + (CHUNK - 1)) >> 5
    turn = (prompt * 5) & 15
    routed, bit, sender, share, room = (const_ref[k : k + 1, :] for k in range(5))
    lane = lax.broadcasted_iota(jnp.int32, (1, 64), 1)
    weight = bits_set(turned(share, turn) & below(chunks))
    crosses = (ways & bit) != 0
    at_home = (ways & routed) == 0
    listed = crosses & ((start ^ (ways & routed)) == (me ^ sender)) & (lane < 32)
    landing = (col_t == mine) & (((lane == 32) & (parity == 0)) | ((lane == 33) & (parity == 1)))

    def exact(values):
        return values.astype(jnp.float32).astype(jnp.bfloat16)

    def dot(left, right):
        return jnp.dot(left, right, preferred_element_type=jnp.float32)

    down = lax.broadcasted_iota(jnp.int32, (items, items), 0)
    along = lax.broadcasted_iota(jnp.int32, (items, items), 1)
    amount = jnp.where(listed, weight, jnp.where(landing, 1, 0))
    place = dot(exact(jnp.where(along < down, 1, 0)), exact(amount)).astype(jnp.int32)

    everyone = exact(jnp.where(crosses & (lane < 16), weight, 0))
    row_item = lax.broadcasted_iota(jnp.int32, (1, items), 1)
    _, _, row_start, row_ways = derive(row_t, row_item)
    nodes = lax.broadcasted_iota(jnp.int32, (32, 1), 0)
    need = jnp.zeros((1, 64), jnp.float32)
    for done in sorted({sum(order[:p]) for order in ORDERS for p in range(4)}):
        present = exact(jnp.where(nodes == (row_start ^ (row_ways & done)), 1, 0))
        held = jnp.max(dot(present, everyone), axis=0, keepdims=True)
        need = jnp.where(routed == done, held, need)
    over = (need.astype(jnp.int32) > room) & (lane < 16)
    over = jnp.max(jnp.where(over, 1, 0), axis=1, keepdims=True)

    bases = [[jnp.zeros_like(ways)] * 4]
    for p in range(4):
        came = []
        for q in range(4):
            k = 16 + 4 * p + q
            moved = (ways & ORDERS[q][p]) != 0
            came.append(jnp.where(moved, region(p, q) + place[:, k : k + 1], bases[p][q]))
        bases.append(came)

    unit = lax.broadcasted_iota(jnp.int32, (HOME, 1), 0)
    local, k = unit >> 4, unit & 15
    unit_prompt = jnp.where(local < 16, 16 * group + local, 16 * (group ^ 1) + local - 16)
    unit_item = unit_prompt + prompts * ((me >> 3) & 1)
    told = jnp.where(listed & at_home, jnp.minimum(place, 250), 255)
    told = jnp.where(lane == 63, chunks, told)
    told = dot(exact(jnp.where(row_item == unit_item, 1, 0)), exact(told)).astype(jnp.int32)
    mine_of = turned(share, (unit_prompt * 5) & 15)
    dealt = (((mine_of >> k) & 1) != 0) & (k < told[:, 63:64]) & (told < 255)
    unit_place = jnp.where(dealt, told + bits_set(mine_of & below(k)), -1)

    slot = lax.broadcasted_iota(jnp.int32, (1, 128), 1)

    def sources(p, q):
        c = 4 * p + q
        found = jnp.where(unit_place[:, c : c + 1] == slot, unit, 0)
        if p:
            first = jnp.where(listed[:, c : c + 1] & jnp.logical_not(at_home[:, c : c + 1]), place[:, c : c + 1], 1 << 20)
            offset = slot - first
            inside = (offset >= 0) & (offset < weight[:, c : c + 1])
            found += jnp.where(inside, jnp.minimum(offset + bases[p][q], space_of(p) - 1), 0)
        return jnp.sum(found, axis=0, keepdims=True)

    slots_ref[...] = jnp.concatenate([sources(p, q) for p in range(4) for q in range(4)], axis=0)

    rank = jnp.where(parity == 0, place[:, 32:33], place[:, 33:34])
    lands = (col_t == mine) & (rank == slot)

    def landed(value, which):
        return jnp.sum(jnp.where(lands & (parity == which), value, 0), axis=0, keepdims=True)

    own = (prompt & 15) * PROMPT_CHUNKS
    own += jnp.where(((prompt >> 4) & 1) == (me >> 4), 0, OWN_CHUNKS)
    length = landed(col_l, 0)
    live = (length + (CHUNK - 1)) >> 5
    by = landed(turn, 0)
    rows = []
    for j in range(2):
        stays = landed(jnp.where((ways & 15) == 0, 1, 0), j)
        home = landed(own, j)
        held = [landed(bases[4][q], j) for q in range(4)]
        parts = [turned(jnp.full_like(by, SHARES[q]), by) for q in range(4)]
        for k in range(PROMPT_CHUNKS):
            source = jnp.zeros_like(by)
            for q in range(4):
                source += ((parts[q] >> k) & 1) * (held[q] + bits_set(parts[q] & ((1 << k) - 1)))
            source = jnp.where(stays != 0, home + k, jnp.minimum(source, space_of(4) - 1))
            rows.append(jnp.where(k < live, source, 0))
    rows += [length, jnp.broadcast_to(over, (1, 128)), jnp.zeros((6, 128), jnp.int32)]
    land_ref[...] = jnp.concatenate(rows, axis=0)


LENGTH, OVER = 32, 33


def plan(targets, prompt_lens, group, member):
    const = np.zeros((8, 64), np.int32)
    for p in range(4):
        for q, order in enumerate(ORDERS):
            for first, sender in ((0, 0), (16, order[p])):
                const[:5, first + 4 * p + q] = (sum(order[:p]), order[p], sender, SHARES[q], ROOM[p][q])
    where = jnp.stack([node_of(group, member % 2), 2 * group + member % 2, group]).astype(jnp.int32)
    vmem = pl.BlockSpec(memory_space=pltpu.VMEM)
    return pl.pallas_call(
        plan_kernel,
        out_shape=(
            jax.ShapeDtypeStruct((16, 128), jnp.int32),
            jax.ShapeDtypeStruct((40, 128), jnp.int32),
        ),
        in_specs=[pl.BlockSpec(memory_space=pltpu.SMEM), vmem, vmem, vmem],
        out_specs=(vmem, vmem),
        compiler_params=pltpu.CompilerParams(vmem_limit_bytes=24 * MIB),
        cost_estimate=cost(SMALL),
        name="plan",
    )(where, targets.reshape(1, -1), prompt_lens.reshape(1, -1), jnp.asarray(const))


def fetch(pairs, sems):
    copies = [
        pltpu.make_async_copy(source, target, sems.at[k]) for k, (source, target) in enumerate(pairs)
    ]
    for copy in copies:
        copy.start()
    return copies


def gather_chunks(table_ref, row, out_ref, pick):
    batch = 4

    def body(s, carry):
        first = s * batch
        held = [pick(table_ref[row, first + b]) for b in range(batch)]
        for b in range(batch):
            out_ref[first + b] = held[b]
        return carry

    lax.fori_loop(0, out_ref.shape[0] // batch, body, 0, unroll=2)


SMEM = pl.BlockSpec(memory_space=pltpu.SMEM)
ANY = pl.BlockSpec(memory_space=pl.ANY)
VMEM = pl.BlockSpec(memory_space=pltpu.VMEM)


def chunks_of(count):
    return jax.ShapeDtypeStruct((count, CHUNK, 256), jnp.bfloat16)


def cost(bytes_accessed, flops=0):
    return pl.CostEstimate(flops=flops, bytes_accessed=bytes_accessed, transcendentals=0)


def space_pairs(homes, boxes, space):
    pairs = [(home, space.at[pl.ds(OWN_CHUNKS * k, OWN_CHUNKS)]) for k, home in enumerate(homes)]
    for k, box in enumerate(boxes):
        pairs.append((box, space.at[pl.ds(region(k // 4, k % 4), box.shape[0])]))
    return pairs


def pack_kernel(phase, table_ref, kv_ref, other_ref, *rest):
    given = 4 * phase
    boxes, outs, space, sems = rest[:given], rest[given : given + 4], rest[given + 4], rest[given + 5]
    for copy in fetch(space_pairs((kv_ref, other_ref), boxes, space), sems):
        copy.wait()
    for q in range(4):
        gather_chunks(table_ref, given + q, outs[q], lambda i: space[i])


def pack_lists(phase, table, kv, other, boxes):
    return pl.pallas_call(
        functools.partial(pack_kernel, phase),
        out_shape=tuple(chunks_of(room) for room in ROOM[phase]),
        in_specs=[SMEM, ANY, ANY] + [ANY] * len(boxes),
        out_specs=(VMEM,) * 4,
        scratch_shapes=[
            pltpu.VMEM((space_of(phase), CHUNK, 256), jnp.bfloat16),
            pltpu.SemaphoreType.DMA((2 + len(boxes),)),
        ],
        compiler_params=pltpu.CompilerParams(vmem_limit_bytes=32 * MIB),
        cost_estimate=cost(SMALL),
        name="pack_lists",
    )(table, kv, other, *boxes)


def attend_row(query, first, second, own, length):
    scaling = 1.0 / math.sqrt(query.shape[1])
    upper = lax.broadcasted_iota(jnp.int32, query.shape, 0) < 8
    zero = jnp.zeros_like(query)
    wide = jnp.concatenate([jnp.where(upper, query, zero), jnp.where(upper, zero, query)], axis=1)
    keys = jnp.concatenate([first[:, :128], second[:, :128]], axis=1)
    values = jnp.concatenate([first[:, 128:], second[:, 128:]], axis=1)
    scores = (
        lax.dot_general(wide, keys, (((1,), (1,)), ((), ())), preferred_element_type=jnp.float32)
        * scaling
    )
    own = own.astype(jnp.float32)
    own_key = jnp.where(upper, own[0:1, :128], own[1:2, :128])
    own_value = jnp.where(upper, own[0:1, 128:], own[1:2, 128:])
    own_score = jnp.sum(query.astype(jnp.float32) * own_key, axis=1, keepdims=True) * scaling
    live = lax.broadcasted_iota(jnp.int32, scores.shape, 1) < length
    scores = jnp.where(live, scores, -jnp.inf)
    row_max = jnp.maximum(jnp.max(scores, axis=1, keepdims=True), own_score)
    weights = jnp.where(live, jnp.exp(scores - row_max), 0.0)
    own_weight = jnp.exp(own_score - row_max)
    denominator = jnp.sum(weights, axis=1, keepdims=True) + own_weight
    both = jnp.dot(weights.astype(jnp.bfloat16), values, preferred_element_type=jnp.float32)
    mixture = jnp.where(upper, both[:, :128], both[:, 128:])
    mixture += own_weight.astype(jnp.bfloat16).astype(jnp.float32) * own_value
    return (mixture / denominator).astype(jnp.bfloat16)


TOGETHER = 4
DEPTH = 4 * TOGETHER


def running_kernel(first, half_ref, pages_ref, lens_ref, query_ref, own_ref, pool_ref, out_ref, held, sems):
    rows = out_ref.shape[0]
    all_rows = lens_ref.shape[0] // 2
    max_pages = held.shape[1]
    start = half_ref[0] * all_rows + first
    held[...] = jnp.zeros_like(held)

    def each_page(row, action):
        slot = row % DEPTH
        count = (lens_ref[start + row] + 63) // 64
        for c in range(max_pages):

            @pl.when(c < count)
            def _():
                page = pages_ref[(start + row) * max_pages + c]
                action(pltpu.make_async_copy(pool_ref.at[page], held.at[slot, c], sems.at[slot, c]))

    def begin(group):
        for r in range(TOGETHER):
            each_page(group * TOGETHER + r, lambda copy: copy.start())

    ahead = DEPTH // TOGETHER - 1
    for group in range(ahead):
        begin(group)

    def body(group, carry):
        @pl.when(group + ahead < rows // TOGETHER)
        def _():
            begin(group + ahead)

        for r in range(TOGETHER):
            each_page(group * TOGETHER + r, lambda copy: copy.wait())
        results = []
        for r in range(TOGETHER):
            row = group * TOGETHER + r
            slot = row % DEPTH
            blocks = [held[slot, :, j].reshape(max_pages * 64, 256) for j in range(2)]
            results.append(
                attend_row(query_ref[first + row], *blocks, own_ref[first + row], lens_ref[start + row])
            )
        for r in range(TOGETHER):
            out_ref[group * TOGETHER + r] = results[r]
        return carry

    lax.fori_loop(0, rows // TOGETHER, body, 0)


def running_rows(first, count, half, pages, lens, queries, own, pool):
    max_pages = pages.shape[-1]
    return pl.pallas_call(
        functools.partial(running_kernel, first),
        out_shape=jax.ShapeDtypeStruct((count, 16, 128), jnp.bfloat16),
        in_specs=[SMEM, SMEM, SMEM, VMEM, VMEM, pl.BlockSpec(memory_space=pltpu.HBM)],
        out_specs=VMEM,
        scratch_shapes=[
            pltpu.VMEM((DEPTH, max_pages) + pool.shape[1:], jnp.bfloat16),
            pltpu.SemaphoreType.DMA((DEPTH, max_pages)),
        ],
        compiler_params=pltpu.CompilerParams(vmem_limit_bytes=48 * MIB),
        cost_estimate=cost(SMALL),
        name="running_rows",
    )(half, pages.reshape(-1), lens.reshape(-1), queries, own, pool)


RING = 4


def land_kernel(first, land_ref, query_ref, own_ref, kv_ref, other_ref, *rest):
    boxes, rest = rest[:16], rest[16:]
    out_ref, landed_ref, block, sems, space, box_sems = rest
    slots = out_ref.shape[0]
    for copy in fetch(space_pairs((kv_ref, other_ref), boxes, space), box_sems):
        copy.wait()

    def write(slot):
        turn = slot % RING
        return pltpu.make_async_copy(block.at[turn], landed_ref.at[slot], sems.at[turn])

    def assemble(slot):
        turn = slot % RING
        length = land_ref[LENGTH, slot]
        count = (length + (CHUNK - 1)) // CHUNK
        for j in range(2):

            def copy(k, carry):
                held = [space[land_ref[PROMPT_CHUNKS * j + 4 * k + b, slot]] for b in range(4)]
                for b in range(4):
                    block[turn, j, 4 * k + b] = held[b]
                return carry

            def clear(k, carry):
                block[turn, j, k] = jnp.zeros((CHUNK, 256), jnp.bfloat16)
                return carry

            lax.fori_loop(0, (count + 3) // 4, copy, 0)
            lax.fori_loop(count, PROMPT_CHUNKS, clear, 0)

            @pl.when(count > 0)
            def _():
                last = count - 1
                row = last * CHUNK + lax.broadcasted_iota(jnp.int32, (CHUNK, 256), 0)
                zero = jnp.zeros((CHUNK, 256), jnp.bfloat16)
                block[turn, j, last] = jnp.where(row < length, block[turn, j, last], zero)

    def body(pair, carry):
        both = (2 * pair, 2 * pair + 1)
        for slot in both:

            @pl.when(slot >= RING)
            def _():
                write(slot).wait()

            assemble(slot)
            write(slot).start()
        results = []
        for slot in both:
            blocks = [block[slot % RING, j].reshape(PROMPT_CHUNKS * CHUNK, 256) for j in range(2)]
            results.append(
                attend_row(query_ref[first + slot], *blocks, own_ref[first + slot], land_ref[LENGTH, slot])
            )
        for slot, result in zip(both, results):
            out_ref[slot] = result
        return carry

    lax.fori_loop(0, slots // 2, body, 0)
    for slot in range(slots - RING, slots):
        write(slot).wait()


def land_rows(first, slots, land, queries, own, kv, other, boxes):
    return pl.pallas_call(
        functools.partial(land_kernel, first),
        out_shape=(
            jax.ShapeDtypeStruct((slots, 16, 128), jnp.bfloat16),
            jax.ShapeDtypeStruct((slots, 2, PROMPT_CHUNKS, CHUNK, 256), jnp.bfloat16),
        ),
        in_specs=[SMEM, VMEM, VMEM, ANY, ANY] + [ANY] * 16,
        out_specs=(VMEM, ANY),
        scratch_shapes=[
            pltpu.VMEM((RING, 2, PROMPT_CHUNKS, CHUNK, 256), jnp.bfloat16),
            pltpu.SemaphoreType.DMA((RING,)),
            pltpu.VMEM((space_of(4), CHUNK, 256), jnp.bfloat16),
            pltpu.SemaphoreType.DMA((18,)),
        ],
        compiler_params=pltpu.CompilerParams(vmem_limit_bytes=40 * MIB),
        cost_estimate=cost(SMALL),
        name="land_rows",
    )(land, queries, own, kv, other, *boxes)


def routed(table, land, kv, other, half, pages, lens, queries, own, pool):
    running = pages.shape[1]
    rows = queries.shape[0]
    quarter = running // 4
    boxes, contexts = [], []
    for phase in range(4):
        lists = pack_lists(phase, table, kv, other, boxes)
        ready, _ = lax.optimization_barrier((half, lists))
        context = running_rows(phase * quarter, quarter, ready, pages, lens, queries, own, pool)
        sent = [hop(value, order[phase]) for value, order in zip(lists, ORDERS)]
        table, land, sent, context = lax.optimization_barrier((table, land, sent, context))
        boxes, contexts = boxes + sent, contexts + [context]
    handed, landed = land_rows(running, rows - running, land, queries, own, kv, other, boxes)
    return join(*contexts), join(handed), landed


def join(*contexts):
    return jnp.concatenate([c.reshape(c.shape[0], -1) for c in contexts], axis=0)


def earlier_matches(labels, block_len, kind_count):
    onehot = (labels[:, None] == jnp.arange(kind_count, dtype=jnp.int32)[None, :]).astype(jnp.int32)
    blocks = onehot.reshape(labels.shape[0] // block_len, block_len, kind_count)
    before = jnp.cumsum(blocks, axis=1) - blocks
    return jnp.sum(before * blocks, axis=2).reshape(labels.shape[0])


def lookup(matches):
    prompt_ids = jnp.arange(matches.shape[1], dtype=jnp.int32)
    row_index = jnp.sum(jnp.where(matches, prompt_ids[None, :], 0), axis=1)
    return (row_index, jnp.any(matches, axis=1))


def pick_rows(table_rows, row_index, is_valid):
    picked = jnp.take(table_rows, row_index, axis=0)
    mask_shape = (is_valid.shape[0],) + (1,) * (picked.ndim - 1)
    return jnp.where(is_valid.reshape(mask_shape), picked, jnp.zeros_like(picked))


def any_fill(targets, prompt_lens, kv, queries, own):
    prompt_kv = kv.reshape(16, 1, 512, 256)
    groups = lax.axis_size("grp")
    group_id = lax.axis_index("grp")
    half_id = lax.axis_index("tp") % 2
    block_len = prompt_kv.shape[0]
    prompt_count = targets.shape[0]
    span_len = prompt_kv.shape[2]
    capacity = max(2, block_len // groups)
    source = jnp.arange(prompt_count, dtype=jnp.int32) // block_len
    arrival = earlier_matches(targets, prompt_count, 2 * groups)
    slot_ids = jnp.arange(block_len, dtype=jnp.int32)
    land_match = (targets[None, :] == 2 * group_id + half_id) & (
        arrival[None, :] == slot_ids[:, None]
    )
    land_len = jnp.sum(jnp.where(land_match, prompt_lens[None, :], 0), axis=1)
    land_live = jnp.arange(span_len, dtype=jnp.int32)[None, :] < land_len[:, None]
    land_index, land_valid = lookup(land_match)
    outgoing = source == group_id
    dest_ids = jnp.arange(groups, dtype=jnp.int32)
    cap_ids = jnp.arange(capacity, dtype=jnp.int32)
    partner = hop(prompt_kv, Z)
    pair_kv = jnp.where(
        half_id == 0,
        jnp.concatenate([prompt_kv, partner], axis=1),
        jnp.concatenate([partner, prompt_kv], axis=1),
    )
    within = earlier_matches(targets, block_len, 2 * groups)
    send_match = (
        outgoing[None, None, :]
        & (targets[None, None, :] == (2 * dest_ids + half_id)[:, None, None])
        & (within[None, None, :] == cap_ids[None, :, None])
    )
    send_index, send_valid = lookup(send_match.reshape(groups * capacity, prompt_count))
    send_index = jnp.where(send_valid, send_index - group_id * block_len, 0)
    outbox = pick_rows(pair_kv, send_index, send_valid)
    outbox = outbox.reshape((groups, capacity) + outbox.shape[1:])
    inbound = lax.all_to_all(outbox, "grp", split_axis=0, concat_axis=0, tiled=True)
    inbound = inbound.reshape((groups * capacity,) + inbound.shape[2:])
    entry_ids = source * capacity + within
    landed = pick_rows(inbound, jnp.take(entry_ids, land_index), land_valid)
    landed = jnp.where(land_live[:, None, :, None], landed, jnp.zeros_like(landed))
    handed = jnp.stack(
        [
            attend_row(queries[s], landed[s, 0], landed[s, 1], own[s], land_len[s])
            for s in range(block_len)
        ]
    )
    return join(handed), landed.reshape(block_len, 2, PROMPT_CHUNKS, CHUNK, 256)


def local(targets, prompt_lens, prompt_kv, cache_pool, block_table, cache_lens, queries, new_kv):
    group = lax.axis_index("grp")
    member = lax.axis_index("tp")
    kv = prompt_kv.reshape(OWN_CHUNKS, CHUNK, 256)
    other = hop(kv, CORE)
    table, land = plan(targets, prompt_lens, group, member)
    half = (member % 2).astype(jnp.int32).reshape(1)
    rows = queries.shape[2]
    running = block_table.shape[2]
    by_head = queries.reshape(rows, 16, 128)
    own = new_kv[0, 0]
    decoded, handed, landed = routed(
        table, land, kv, other, half, block_table[0], cache_lens[0], by_head, own, cache_pool[0, 0]
    )

    def again(carry):
        return (*any_fill(targets, prompt_lens, kv, by_head[running:], own[running:]), jnp.zeros((), jnp.int32))

    handed, landed, _ = lax.while_loop(lambda carry: carry[2] > 0, again, (handed, landed, land[OVER, 0]))
    return (
        jnp.concatenate([decoded, handed], axis=0).reshape(1, 1, rows, queries.shape[3]),
        landed.reshape(1, 1, 16, 2, 512, 256),
    )


def solution(mesh):
    placed = (
        P(),
        P(),
        P("grp", "tp", None, None),
        P("grp", "tp", None, None, None, None),
        P("grp", None, None, None),
        P("grp", None, None),
        P("grp", "tp", None, None),
        P("grp", "tp", None, None, None),
    )
    return jax.shard_map(
        local,
        mesh=mesh,
        in_specs=placed,
        out_specs=(P("grp", "tp", None, None), P("grp", "tp", None, None, None, None)),
        check_vma=False,
    )
```

profile of v0, /device:TPU:16, one launch (start us, length us, event | category | flops | bytes accessed | tf_op | source)
XLA Modules:
  0.0 143.8 jit_solution(6968680156654260751)
XLA Ops:
  0.7 0.1 collective-permute-start.1
  0.8 0.1 pad_add_fusion.where_ref
  0.8 0.7 copy-done
  1.5 9.3 %plan.1 = (s32[16,128]{1,0:T(8,128)S(1)}, s32[40,128]{1,0:T(8,128)S(1)}) custom-call(s32[3]{0:T(128)S(1)} %pad_add_fusion.where_ref, s32[1,256]{1,0:T(1,128)} %bitcast.533, s32[1,256]{1,0:T(1,128)} %bitcast.537, s32[8,64]{1,0:T(8,128)S(1)} %copy-done), custom_call_target="tpu_custom_call" | custom-call | bytes 4096 | tf_op jit(solution)/shard_map/plan/pallas_call | solution.py:208
  10.8 5.8 %pack_lists.4 = (bf16[40,32,256]{2,1,0:T(8,128)(2,1)}, bf16[40,32,256]{2,1,0:T(8,128)(2,1)}, bf16[48,32,256]{2,1,0:T(8,128)(2,1)S(1)}, bf16[36,32,256]{2,1,0:T(8,128)(2,1)}) custom-call(s32[16,128]{1,0:T(8,128)S(1)} %get-tuple-element.125.table_ref, bf16[256,32,256]{2,1,0:T(8,128)(2,1)} %bitcast.493, bf16[256,32,256]{2,1,0:T(8,128)(2,1)} %collective-permute-done.1.other_ref), custom_call_target="tpu_custom_call" | custom-call | bytes 4096 | tf_op jit(solution)/shard_map/pack_lists/pallas_call | solution.py:274
  16.7 0.5 collective-permute-start.4
  17.2 1.5 %collective-permute-start.2 = (bf16[40,32,256]{2,1,0:T(8,128)(2,1)}, bf16[40,32,256]{2,1,0:T(8,128)(2,1)S(1)}, u32[]{:S(2)}, u32[]{:S(2)}) collective-permute-start(bf16[40,32,256]{2,1,0:T(8,128)(2,1)} %get-tuple-element.95), channel_id=1, source_target_pairs={{0,16},{8,24},{16,0},{24,8},{32,48},{40,56},{48,32},{56,40},{64,80... | collective-permute-start | bytes 1966088 | tf_op jit(solution)/shard_map/ppermute | solution.py:50
  18.7 1.1 collective-permute-start.3
  19.8 1.9 %collective-permute-start.5 = (bf16[36,32,256]{2,1,0:T(8,128)(2,1)}, bf16[36,32,256]{2,1,0:T(8,128)(2,1)S(1)}, u32[]{:S(2)}, u32[]{:S(2)}) collective-permute-start(bf16[36,32,256]{2,1,0:T(8,128)(2,1)} %get-tuple-element.98), channel_id=1, source_target_pairs={{0,1},{1,0},{2,3},{3,2},{4,5},{5,4},{6,7},{7,6},{8,9},{9,8},{10,11... | collective-permute-start | bytes 1769480 | tf_op jit(solution)/shard_map/ppermute | solution.py:49
  21.7 0.8 copy.52
  22.5 0.7 copy.35
  23.2 1.0 reshape_squeeze.4.pages_ref
  24.2 0.1 reshape_squeeze.5.lens_ref
  24.3 8.4 %running_rows.4 = bf16[16,16,128]{2,1,0:T(8,128)(2,1)S(1)} custom-call(s32[1]{0:T(128)} %bitcast.180.half_ref, s32[768]{0:T(1024)S(1)} %reshape_squeeze.4.pages_ref, s32[128]{0:T(128)S(1)} %reshape_squeeze.5.lens_ref, bf16[80,16,128]{2,1,0:T(8,128)(2,1)} %bitcast.502, bf16[80,2,256]{2,1,0:T(2,128)(2,1)} %bitcast.511, bf16[224,2,64,256]{3,2,1,0:T(8,128)(2,1)} %bitcast.498), custom_call_target="tpu_custom_call" | custom-call | bytes 4096 | tf_op jit(solution)/shard_map/running_rows/pallas_call | solution.py:369
  32.7 0.0 copy-start.2
  32.7 2.4 %collective-permute-done.5.rest_3_ = bf16[36,32,256]{2,1,0:T(8,128)(2,1)S(1)} collective-permute-done((bf16[36,32,256]{2,1,0:T(8,128)(2,1)}, bf16[36,32,256]{2,1,0:T(8,128)(2,1)S(1)}, u32[]{:S(2)}, u32[]{:S(2)}) %collective-permute-start.5) | collective-permute-done | bytes 589856 | tf_op jit(solution)/shard_map/ppermute | solution.py:49
  35.2 0.3 collective-permute-done.3.rest_1_
  35.5 1.2 collective-permute-done.4.rest_2_
  36.7 4.7 %pack_lists.5 = (bf16[48,32,256]{2,1,0:T(8,128)(2,1)S(1)}, bf16[44,32,256]{2,1,0:T(8,128)(2,1)S(1)}, bf16[48,32,256]{2,1,0:T(8,128)(2,1)S(1)}, bf16[48,32,256]{2,1,0:T(8,128)(2,1)S(1)}) custom-call(s32[16,128]{1,0:T(8,128)S(1)} %get-tuple-element.125.table_ref, bf16[256,32,256]{2,1,0:T(8,128)(2,1)} %bitcast.494, ...), custom_call_target="tpu_custom_call" | custom-call | bytes 4096 | tf_op jit(solution)/shard_map/pack_lists/pallas_call | solution.py:274
  41.4 2.0 %collective-permute-start.6 = (bf16[48,32,256]{2,1,0:T(8,128)(2,1)S(1)}, bf16[48,32,256]{2,1,0:T(8,128)(2,1)S(1)}, u32[]{:S(2)}, u32[]{:S(2)}) collective-permute-start(bf16[48,32,256]{2,1,0:T(8,128)(2,1)S(1)} %get-tuple-element.107), channel_id=1, source_target_pairs={{0,1},{1,0},{2,3},{3,2},{4,5},{5,4},{6,7},{7,6},{8,9},{9,8},{10,11... | collective-permute-start | bytes 2359304 | tf_op jit(solution)/shard_map/ppermute | solution.py:49
  43.4 2.5 %collective-permute-start.8 = (bf16[48,32,256]{2,1,0:T(8,128)(2,1)S(1)}, bf16[48,32,256]{2,1,0:T(8,128)(2,1)S(1)}, u32[]{:S(2)}, u32[]{:S(2)}) collective-permute-start(bf16[48,32,256]{2,1,0:T(8,128)(2,1)S(1)} %get-tuple-element.109), channel_id=1, source_target_pairs={{0,32},{8,40},{16,48},{24,56},{32,0},{40,8},{48,16},{56,24},{64,96... | collective-permute-start | bytes 2359304 | tf_op jit(solution)/shard_map/ppermute | solution.py:50
  45.9 1.5 %collective-permute-start.9 = (bf16[48,32,256]{2,1,0:T(8,128)(2,1)S(1)}, bf16[48,32,256]{2,1,0:T(8,128)(2,1)S(1)}, u32[]{:S(2)}, u32[]{:S(2)}) collective-permute-start(bf16[48,32,256]{2,1,0:T(8,128)(2,1)S(1)} %get-tuple-element.110), channel_id=1, source_target_pairs={{0,16},{8,24},{16,0},{24,8},{32,48},{40,56},{48,32},{56,40},{64,80... | collective-permute-start | bytes 2359304 | tf_op jit(solution)/shard_map/ppermute | solution.py:50
  47.4 8.0 %running_rows.5 = bf16[16,16,128]{2,1,0:T(8,128)(2,1)S(1)} custom-call(s32[1]{0:T(128)} %bitcast.180.half_ref, s32[768]{0:T(1024)S(1)} %reshape_squeeze.4.pages_ref, s32[128]{0:T(128)S(1)} %reshape_squeeze.5.lens_ref, bf16[80,16,128]{2,1,0:T(8,128)(2,1)S(1)} %bitcast.504, bf16[80,2,256]{2,1,0:T(2,128)(2,1)S(1)} %bitcast.513, bf16[224,2,64,256]{3,2,1,0:T(8,128)(2,1)} %bitcast.499), custom_call_target="tpu_custom_call" | custom-call | bytes 4096 | tf_op jit(solution)/shard_map/running_rows/pallas_call | solution.py:369
  55.5 8.8 %collective-permute-done.7.rest_5_ = bf16[44,32,256]{2,1,0:T(8,128)(2,1)S(1)} collective-permute-done((bf16[44,32,256]{2,1,0:T(8,128)(2,1)S(1)}, bf16[44,32,256]{2,1,0:T(8,128)(2,1)S(1)}, u32[]{:S(2)}, u32[]{:S(2)}) %collective-permute-start.7) | collective-permute-done | bytes 720928 | tf_op jit(solution)/shard_map/ppermute | solution.py:50
  64.3 0.2 collective-permute-done.9.rest_7_
  64.5 4.9 %pack_lists.6 = (bf16[64,32,256]{2,1,0:T(8,128)(2,1)S(1)}, bf16[52,32,256]{2,1,0:T(8,128)(2,1)S(1)}, bf16[48,32,256]{2,1,0:T(8,128)(2,1)S(1)}, bf16[52,32,256]{2,1,0:T(8,128)(2,1)S(1)}) custom-call(s32[16,128]{1,0:T(8,128)S(1)} %get-tuple-element.125.table_ref, bf16[256,32,256]{2,1,0:T(8,128)(2,1)} %bitcast.495, ...), custom_call_target="tpu_custom_call" | custom-call | bytes 4096 | tf_op jit(solution)/shard_map/pack_lists/pallas_call | solution.py:274
  69.4 0.2 collective-permute-start.10
  69.6 0.6 collective-permute-start.11
  70.1 1.7 %collective-permute-start.13 = (bf16[52,32,256]{2,1,0:T(8,128)(2,1)S(1)}, bf16[52,32,256]{2,1,0:T(8,128)(2,1)S(1)}, u32[]{:S(2)}, u32[]{:S(2)}) collective-permute-start(bf16[52,32,256]{2,1,0:T(8,128)(2,1)S(1)} %get-tuple-element.122), channel_id=1, source_target_pairs={{0,32},{8,40},{16,48},{24,56},{32,0},{40,8},{48,16},{56,24},{64,96... | collective-permute-start | bytes 2555912 | tf_op jit(solution)/shard_map/ppermute | solution.py:50
  71.8 0.5 collective-permute-start.12
  72.3 0.5 slice.763
  72.9 8.0 %running_rows.6 = bf16[16,16,128]{2,1,0:T(8,128)(2,1)S(1)} custom-call(s32[1]{0:T(128)} %bitcast.180.half_ref, s32[768]{0:T(1024)S(1)} %reshape_squeeze.4.pages_ref, s32[128]{0:T(128)S(1)} %reshape_squeeze.5.lens_ref, bf16[80,16,128]{2,1,0:T(8,128)(2,1)S(1)} %bitcast.505, bf16[80,2,256]{2,1,0:T(2,128)(2,1)S(1)} %bitcast.514, bf16[224,2,64,256]{3,2,1,0:T(8,128)(2,1)} %bitcast.500), custom_call_target="tpu_custom_call" | custom-call | bytes 4096 | tf_op jit(solution)/shard_map/running_rows/pallas_call | solution.py:369
  80.9 8.0 %collective-permute-done.12.rest_10_ = bf16[48,32,256]{2,1,0:T(8,128)(2,1)S(1)} collective-permute-done((bf16[48,32,256]{2,1,0:T(8,128)(2,1)S(1)}, bf16[48,32,256]{2,1,0:T(8,128)(2,1)S(1)}, u32[]{:S(2)}, u32[]{:S(2)}) %collective-permute-start.12) | collective-permute-done | bytes 786464 | tf_op jit(solution)/shard_map/ppermute | solution.py:50
  88.9 0.3 collective-permute-done.13.rest_11_
  89.2 3.6 %collective-permute-done.10.rest_8_ = bf16[64,32,256]{2,1,0:T(8,128)(2,1)S(1)} collective-permute-done((bf16[64,32,256]{2,1,0:T(8,128)(2,1)S(1)}, bf16[64,32,256]{2,1,0:T(8,128)(2,1)S(1)}, u32[]{:S(2)}, u32[]{:S(2)}) %collective-permute-start.10) | collective-permute-done | bytes 1048608 | tf_op jit(solution)/shard_map/ppermute | solution.py:50
  92.7 6.8 %pack_lists.7 = (bf16[72,32,256]{2,1,0:T(8,128)(2,1)}, bf16[72,32,256]{2,1,0:T(8,128)(2,1)S(1)}, bf16[68,32,256]{2,1,0:T(8,128)(2,1)}, bf16[60,32,256]{2,1,0:T(8,128)(2,1)}) custom-call(s32[16,128]{1,0:T(8,128)S(1)} %get-tuple-element.125.table_ref, bf16[256,32,256]{2,1,0:T(8,128)(2,1)} %bitcast.496, bf16[256,32,256]{2,1,0:T(8,128)(2,1)} %collective-permute-done.1.other_ref, ...), custom_call_target="tpu_custom_call" | custom-call | bytes 4096 | tf_op jit(solution)/shard_map/pack_lists/pallas_call | solution.py:274
  99.6 2.6 %collective-permute-start.14 = (bf16[72,32,256]{2,1,0:T(8,128)(2,1)}, bf16[72,32,256]{2,1,0:T(8,128)(2,1)S(1)}, u32[]{:S(2)}, u32[]{:S(2)}) collective-permute-start(bf16[72,32,256]{2,1,0:T(8,128)(2,1)} %get-tuple-element.131), channel_id=1, source_target_pairs={{0,32},{8,40},{16,48},{24,56},{32,0},{40,8},{48,16},{56,24},{64,96... | collective-permute-start | bytes 3538952 | tf_op jit(solution)/shard_map/ppermute | solution.py:50
  102.2 0.7 collective-permute-start.15
  102.9 0.9 collective-permute-start.16
  103.9 8.1 %running_rows.7 = bf16[16,16,128]{2,1,0:T(8,128)(2,1)S(1)} custom-call(s32[1]{0:T(128)} %bitcast.180.half_ref, s32[768]{0:T(1024)S(1)} %reshape_squeeze.4.pages_ref, s32[128]{0:T(128)S(1)} %reshape_squeeze.5.lens_ref, bf16[80,16,128]{2,1,0:T(8,128)(2,1)S(1)} %bitcast.506, bf16[80,2,256]{2,1,0:T(2,128)(2,1)S(1)} %bitcast.515, bf16[224,2,64,256]{3,2,1,0:T(8,128)(2,1)} %bitcast.501), custom_call_target="tpu_custom_call" | custom-call | bytes 4096 | tf_op jit(solution)/shard_map/running_rows/pallas_call | solution.py:369
  112.0 12.6 %collective-permute-done.17.rest_15_ = bf16[60,32,256]{2,1,0:T(8,128)(2,1)S(1)} collective-permute-done((bf16[60,32,256]{2,1,0:T(8,128)(2,1)}, bf16[60,32,256]{2,1,0:T(8,128)(2,1)S(1)}, u32[]{:S(2)}, u32[]{:S(2)}) %collective-permute-start.17) | collective-permute-done | bytes 983072 | tf_op jit(solution)/shard_map/ppermute | solution.py:50
  124.7 1.8 %collective-permute-done.16.rest_14_ = bf16[68,32,256]{2,1,0:T(8,128)(2,1)S(1)} collective-permute-done((bf16[68,32,256]{2,1,0:T(8,128)(2,1)}, bf16[68,32,256]{2,1,0:T(8,128)(2,1)S(1)}, u32[]{:S(2)}, u32[]{:S(2)}) %collective-permute-start.16) | collective-permute-done | bytes 1114144 | tf_op jit(solution)/shard_map/ppermute | solution.py:49
  126.5 0.5 collective-permute-done.15.rest_13_
  127.1 13.0 %land_rows.1 = (bf16[16,16,128]{2,1,0:T(8,128)(2,1)S(1)}, bf16[16,2,16,32,256]{4,3,2,1,0:T(8,128)(2,1)}) custom-call(s32[40,128]{1,0:T(8,128)S(1)} %get-tuple-element.137.land_ref, bf16[80,16,128]{2,1,0:T(8,128)(2,1)S(1)} %bitcast.507, bf16[80,2,256]{2,1,0:T(2,128)(2,1)S(1)} %bitcast.516, bf16[256,32,256]{2,1,0:T(8,128)(2,1)} %bitcast.497, ...), custom_call_target="tpu_custom_call" | custom-call | bytes 4096 | tf_op jit(solution)/shard_map/land_rows/pallas_call | solution.py:450
  140.1 0.6 copy.95
  140.8 0.7 copy-done.6
  141.5 0.8 while.11
  142.3 1.5 %constant_dynamic-update-slice_fusion = bf16[80,2048]{1,0:T(8,128)(2,1)} fusion(bf16[80,2048]{1,0:T(8,128)(2,1)} %copy-done.6, bf16[16,2048]{1,0:T(8,128)(2,1)} %get-tuple-element.144), kind=kLoop, calls=%fused_computation.734 | loop fusion | bytes 131072 | tf_op jit(solution)/shard_map/concatenate | solution.py:580
  (27 shorter events, 0.1 us)
Async XLA Ops:
  0.6 21.8 %copy-start.7 = (s32[1,2,64,6]{2,1,3,0:T(2,128)S(1)}, s32[1,2,64,6]{2,1,3,0:T(2,128)}, u32[]{:S(2)}) copy-start(s32[1,2,64,6]{2,1,3,0:T(2,128)} %param.15) | copy-start | bytes 9220
  0.6 23.5 %copy-start.8 = (s32[1,2,64]{2,1,0:T(2,128)S(1)}, s32[1,2,64]{2,1,0:T(2,128)}, u32[]{:S(2)}) copy-start(s32[1,2,64]{2,1,0:T(2,128)} %param.16) | copy-start | bytes 1540
  0.7 10.2 %collective-permute-start.1 = (bf16[256,32,256]{2,1,0:T(8,128)(2,1)}, bf16[256,32,256]{2,1,0:T(8,128)(2,1)}, u32[]{:S(2)}, u32[]{:S(2)}) collective-permute-start(bf16[256,32,256]{2,1,0:T(8,128)(2,1)} %bitcast.492), channel_id=1, source_target_pairs={{0,8},{8,0},{16,24},{24,16},{32,40},{40,32},{48,56},{56,48},{64,72... | collective-permute-start | bytes 12582920 | tf_op jit(solution)/shard_map/ppermute | solution.py:50
  0.8 0.7 copy-start
  1.5 20.1 %copy-start.4 = (bf16[1,1,80,2048]{3,2,1,0:T(8,128)(2,1)S(1)}, bf16[1,1,80,2048]{3,2,1,0:T(8,128)(2,1)}, u32[]{:S(2)}) copy-start(bf16[1,1,80,2048]{3,2,1,0:T(8,128)(2,1)} %param.17) | copy-start | bytes 983044
  16.7 20.0 %collective-permute-start.4 = (bf16[48,32,256]{2,1,0:T(8,128)(2,1)S(1)}, bf16[48,32,256]{2,1,0:T(8,128)(2,1)S(1)}, u32[]{:S(2)}, u32[]{:S(2)}) collective-permute-start(bf16[48,32,256]{2,1,0:T(8,128)(2,1)S(1)} %get-tuple-element.97), channel_id=1, source_target_pairs={{0,96},{8,104},{16,112},{24,120},{32,64},{40,72},{48,80},{56,88},{... | collective-permute-start | bytes 2359304 | tf_op jit(solution)/shard_map/ppermute | solution.py:50
  17.2 17.9 %collective-permute-start.2 = (bf16[40,32,256]{2,1,0:T(8,128)(2,1)}, bf16[40,32,256]{2,1,0:T(8,128)(2,1)S(1)}, u32[]{:S(2)}, u32[]{:S(2)}) collective-permute-start(bf16[40,32,256]{2,1,0:T(8,128)(2,1)} %get-tuple-element.95), channel_id=1, source_target_pairs={{0,16},{8,24},{16,0},{24,8},{32,48},{40,56},{48,32},{56,40},{64,80... | collective-permute-start | bytes 1966088 | tf_op jit(solution)/shard_map/ppermute | solution.py:50
  18.7 16.8 %collective-permute-start.3 = (bf16[40,32,256]{2,1,0:T(8,128)(2,1)}, bf16[40,32,256]{2,1,0:T(8,128)(2,1)S(1)}, u32[]{:S(2)}, u32[]{:S(2)}) collective-permute-start(bf16[40,32,256]{2,1,0:T(8,128)(2,1)} %get-tuple-element.96), channel_id=1, source_target_pairs={{0,32},{8,40},{16,48},{24,56},{32,0},{40,8},{48,16},{56,24},{64,96... | collective-permute-start | bytes 1966088 | tf_op jit(solution)/shard_map/ppermute | solution.py:50
  19.8 15.4 %collective-permute-start.5 = (bf16[36,32,256]{2,1,0:T(8,128)(2,1)}, bf16[36,32,256]{2,1,0:T(8,128)(2,1)S(1)}, u32[]{:S(2)}, u32[]{:S(2)}) collective-permute-start(bf16[36,32,256]{2,1,0:T(8,128)(2,1)} %get-tuple-element.98), channel_id=1, source_target_pairs={{0,1},{1,0},{2,3},{3,2},{4,5},{5,4},{6,7},{7,6},{8,9},{9,8},{10,11... | collective-permute-start | bytes 1769480 | tf_op jit(solution)/shard_map/ppermute | solution.py:49
  32.7 14.7 %copy-start.1 = (bf16[10,8,16,128]{3,2,1,0:T(8,128)(2,1)S(1)}, bf16[10,8,16,128]{3,2,1,0:T(8,128)(2,1)}, u32[]{:S(2)}) copy-start(bf16[10,8,16,128]{3,2,1,0:T(8,128)(2,1)} %copy.52) | copy-start | bytes 983044
  32.7 14.7 %copy-start.2 = (bf16[1,1,80,2,256]{4,3,2,1,0:T(2,128)(2,1)S(1)}, bf16[1,1,80,2,256]{4,3,2,1,0:T(2,128)(2,1)}, u32[]{:S(2)}) copy-start(bf16[1,1,80,2,256]{4,3,2,1,0:T(2,128)(2,1)} %param.18) | copy-start | bytes 245764
  41.4 22.9 %collective-permute-start.6 = (bf16[48,32,256]{2,1,0:T(8,128)(2,1)S(1)}, bf16[48,32,256]{2,1,0:T(8,128)(2,1)S(1)}, u32[]{:S(2)}, u32[]{:S(2)}) collective-permute-start(bf16[48,32,256]{2,1,0:T(8,128)(2,1)S(1)} %get-tuple-element.107), channel_id=1, source_target_pairs={{0,1},{1,0},{2,3},{3,2},{4,5},{5,4},{6,7},{7,6},{8,9},{9,8},{10,11... | collective-permute-start | bytes 2359304 | tf_op jit(solution)/shard_map/ppermute | solution.py:49
  43.4 20.9 %collective-permute-start.8 = (bf16[48,32,256]{2,1,0:T(8,128)(2,1)S(1)}, bf16[48,32,256]{2,1,0:T(8,128)(2,1)S(1)}, u32[]{:S(2)}, u32[]{:S(2)}) collective-permute-start(bf16[48,32,256]{2,1,0:T(8,128)(2,1)S(1)} %get-tuple-element.109), channel_id=1, source_target_pairs={{0,32},{8,40},{16,48},{24,56},{32,0},{40,8},{48,16},{56,24},{64,96... | collective-permute-start | bytes 2359304 | tf_op jit(solution)/shard_map/ppermute | solution.py:50
  45.9 18.6 %collective-permute-start.9 = (bf16[48,32,256]{2,1,0:T(8,128)(2,1)S(1)}, bf16[48,32,256]{2,1,0:T(8,128)(2,1)S(1)}, u32[]{:S(2)}, u32[]{:S(2)}) collective-permute-start(bf16[48,32,256]{2,1,0:T(8,128)(2,1)S(1)} %get-tuple-element.110), channel_id=1, source_target_pairs={{0,16},{8,24},{16,0},{24,8},{32,48},{40,56},{48,32},{56,40},{64,80... | collective-permute-start | bytes 2359304 | tf_op jit(solution)/shard_map/ppermute | solution.py:50
  47.4 16.9 %collective-permute-start.7 = (bf16[44,32,256]{2,1,0:T(8,128)(2,1)S(1)}, bf16[44,32,256]{2,1,0:T(8,128)(2,1)S(1)}, u32[]{:S(2)}, u32[]{:S(2)}) collective-permute-start(bf16[44,32,256]{2,1,0:T(8,128)(2,1)S(1)} %get-tuple-element.108), channel_id=1, source_target_pairs={{0,96},{8,104},{16,112},{24,120},{32,64},{40,72},{48,80},{56,88},{... | collective-permute-start | bytes 2162696 | tf_op jit(solution)/shard_map/ppermute | solution.py:50
  69.4 23.4 %collective-permute-start.10 = (bf16[64,32,256]{2,1,0:T(8,128)(2,1)S(1)}, bf16[64,32,256]{2,1,0:T(8,128)(2,1)S(1)}, u32[]{:S(2)}, u32[]{:S(2)}) collective-permute-start(bf16[64,32,256]{2,1,0:T(8,128)(2,1)S(1)} %get-tuple-element.119), channel_id=1, source_target_pairs={{0,96},{8,104},{16,112},{24,120},{32,64},{40,72},{48,80},{56,88},{... | collective-permute-start | bytes 3145736 | tf_op jit(solution)/shard_map/ppermute | solution.py:50
  69.6 19.3 %collective-permute-start.11 = (bf16[52,32,256]{2,1,0:T(8,128)(2,1)S(1)}, bf16[52,32,256]{2,1,0:T(8,128)(2,1)S(1)}, u32[]{:S(2)}, u32[]{:S(2)}) collective-permute-start(bf16[52,32,256]{2,1,0:T(8,128)(2,1)S(1)} %get-tuple-element.120), channel_id=1, source_target_pairs={{0,1},{1,0},{2,3},{3,2},{4,5},{5,4},{6,7},{7,6},{8,9},{9,8},{10,11... | collective-permute-start | bytes 2555912 | tf_op jit(solution)/shard_map/ppermute | solution.py:49
  70.1 19.0 %collective-permute-start.13 = (bf16[52,32,256]{2,1,0:T(8,128)(2,1)S(1)}, bf16[52,32,256]{2,1,0:T(8,128)(2,1)S(1)}, u32[]{:S(2)}, u32[]{:S(2)}) collective-permute-start(bf16[52,32,256]{2,1,0:T(8,128)(2,1)S(1)} %get-tuple-element.122), channel_id=1, source_target_pairs={{0,32},{8,40},{16,48},{24,56},{32,0},{40,8},{48,16},{56,24},{64,96... | collective-permute-start | bytes 2555912 | tf_op jit(solution)/shard_map/ppermute | solution.py:50
  71.8 17.1 %collective-permute-start.12 = (bf16[48,32,256]{2,1,0:T(8,128)(2,1)S(1)}, bf16[48,32,256]{2,1,0:T(8,128)(2,1)S(1)}, u32[]{:S(2)}, u32[]{:S(2)}) collective-permute-start(bf16[48,32,256]{2,1,0:T(8,128)(2,1)S(1)} %get-tuple-element.121), channel_id=1, source_target_pairs={{0,16},{8,24},{16,0},{24,8},{32,48},{40,56},{48,32},{56,40},{64,80... | collective-permute-start | bytes 2359304 | tf_op jit(solution)/shard_map/ppermute | solution.py:50
  99.6 26.9 %collective-permute-start.14 = (bf16[72,32,256]{2,1,0:T(8,128)(2,1)}, bf16[72,32,256]{2,1,0:T(8,128)(2,1)S(1)}, u32[]{:S(2)}, u32[]{:S(2)}) collective-permute-start(bf16[72,32,256]{2,1,0:T(8,128)(2,1)} %get-tuple-element.131), channel_id=1, source_target_pairs={{0,32},{8,40},{16,48},{24,56},{32,0},{40,8},{48,16},{56,24},{64,96... | collective-permute-start | bytes 3538952 | tf_op jit(solution)/shard_map/ppermute | solution.py:50
  102.2 24.9 %collective-permute-start.15 = (bf16[72,32,256]{2,1,0:T(8,128)(2,1)S(1)}, bf16[72,32,256]{2,1,0:T(8,128)(2,1)S(1)}, u32[]{:S(2)}, u32[]{:S(2)}) collective-permute-start(bf16[72,32,256]{2,1,0:T(8,128)(2,1)S(1)} %get-tuple-element.132), channel_id=1, source_target_pairs={{0,16},{8,24},{16,0},{24,8},{32,48},{40,56},{48,32},{56,40},{64,80... | collective-permute-start | bytes 3538952 | tf_op jit(solution)/shard_map/ppermute | solution.py:50
  102.9 23.6 %collective-permute-start.16 = (bf16[68,32,256]{2,1,0:T(8,128)(2,1)}, bf16[68,32,256]{2,1,0:T(8,128)(2,1)S(1)}, u32[]{:S(2)}, u32[]{:S(2)}) collective-permute-start(bf16[68,32,256]{2,1,0:T(8,128)(2,1)} %get-tuple-element.133), channel_id=1, source_target_pairs={{0,1},{1,0},{2,3},{3,2},{4,5},{5,4},{6,7},{7,6},{8,9},{9,8},{10,11... | collective-permute-start | bytes 3342344 | tf_op jit(solution)/shard_map/ppermute | solution.py:49
  103.9 20.8 %collective-permute-start.17 = (bf16[60,32,256]{2,1,0:T(8,128)(2,1)}, bf16[60,32,256]{2,1,0:T(8,128)(2,1)S(1)}, u32[]{:S(2)}, u32[]{:S(2)}) collective-permute-start(bf16[60,32,256]{2,1,0:T(8,128)(2,1)} %get-tuple-element.134), channel_id=1, source_target_pairs={{0,96},{8,104},{16,112},{24,120},{32,64},{40,72},{48,80},{56,88},{... | collective-permute-start | bytes 2949128 | tf_op jit(solution)/shard_map/ppermute | solution.py:50
  112.0 28.8 %copy-start.3 = (s32[256]{0:T(256)S(1)}, s32[256]{0:T(256)}, u32[]{:S(2)}) copy-start(s32[256]{0:T(256)} %param.11) | copy-start | bytes 3076
  112.0 28.8 %copy-start.5 = (s32[256]{0:T(256)S(1)}, s32[256]{0:T(256)}, u32[]{:S(2)}) copy-start(s32[256]{0:T(256)} %param.12) | copy-start | bytes 3076
  140.8 0.7 copy-start.6
where the time goes:
time: 144 us
  Pallas kernels  77.2 us (54%)
  waiting for transfers between devices  39.8 us (28%)
  starting transfers between devices  18.3 us (13%)
  local copies, waits for them, and re-layouts  6.72 us (5%)
    ppermute x13, waiting for transfers between devices, hop(): lax.ppermute(value, 'grp', [(g, flipped(g, axis)) for g in range(lax.axis...  35.6 us
    pallas_call x4, Pallas kernels, running_rows(): pl.pallas_call(functools.partial(running_kernel, first), out_shape=jax.Sh...  32.6 us
    pallas_call x4, Pallas kernels, pack_lists(): pl.pallas_call(functools.partial(pack_kernel, phase), out_shape=tuple((ch...  22.3 us
    pallas_call x1, Pallas kernels, land_rows(): pl.pallas_call(functools.partial(land_kernel, first), out_shape=(jax.Shap...  13 us
    ppermute x13, starting transfers between devices, hop(): lax.ppermute(value, 'grp', [(g, flipped(g, axis)) for g in range(lax.axis...  12.9 us
    pallas_call x1, Pallas kernels, plan(): pl.pallas_call(plan_kernel, out_shape=(jax.ShapeDtypeStruct((16, 128), jn...  9.28 us
    ppermute x4, starting transfers between devices, hop(): lax.ppermute(value, 'tp', [(t, t ^ 1) for t in range(lax.axis_size('tp'))])  5.41 us
    ppermute x4, waiting for transfers between devices, hop(): lax.ppermute(value, 'tp', [(t, t ^ 1) for t in range(lax.axis_size('tp'))])  4.25 us
  transfers between devices with their start and end apart: 17, of which 11 were waited for; matrix products, arithmetic and copies ran while one was open for 2% of the time, Pallas kernels for 29%

commit v1 on v0

v1 whole, which is shorter than its diff:
```python
import functools
import math

import jax
import jax.numpy as jnp
import numpy as np
from jax import lax
from jax.experimental import pallas as pl
from jax.experimental.pallas import tpu as pltpu
from jax.sharding import PartitionSpec as P

CHUNK = 32
PROMPT_CHUNKS = 16
OWN_CHUNKS = 256
HOME = 512
X, YA, YB, Z, CORE = 1, 2, 4, 8, 16
ORDERS = ((X, Z, YB, YA), (YA, YB, Z, X), (YB, YA, X, Z), (Z, X, YA, YB))
DEAL = (2, 0, 1, 3, 2, 0, 1, 2, 3, 0, 1, 2, 0, 1, 3, 2)
SHARES = tuple(sum(1 << k for k, part in enumerate(DEAL) if part == q) for q in range(4))
ROOM = ((40, 40, 48, 36), (48, 44, 48, 48), (64, 52, 48, 52), (72, 72, 68, 60))
MIB = 1024 * 1024
SMALL = 4096


KEPT = (52, 52, 64, 40)


def region(phase, part):
    return KEPT[part] + sum(rooms[part] for rooms in ROOM[:phase])


def begin_of(part):
    return sum(region(4, q) for q in range(part))


def flipped(group, mask):
    x, core, y = (group >> 1) & 1, group & 1, group >> 2
    if mask & X:
        x ^= 1
    if mask & YA:
        y ^= 1
    if mask & YB:
        y = 3 - y
    if mask & CORE:
        core ^= 1
    return (y << 2) | (x << 1) | core


def hop(value, axis):
    if axis == Z:
        return lax.ppermute(value, "tp", [(t, t ^ 1) for t in range(lax.axis_size("tp"))])
    return lax.ppermute(value, "grp", [(g, flipped(g, axis)) for g in range(lax.axis_size("grp"))])


def node_of(group, parity):
    y = group >> 2
    return (
        ((group >> 1) & 1)
        | (((y ^ (y >> 1)) & 1) << 1)
        | (((y >> 1) & 1) << 2)
        | (parity << 3)
        | ((group & 1) << 4)
    )


def bits_set(word):
    word = word - ((word >> 1) & 0x5555)
    word = (word & 0x3333) + ((word >> 2) & 0x3333)
    word = (word + (word >> 4)) & 0x0F0F
    return (word + (word >> 8)) & 0x1F


def turned(share, by):
    return ((share | (share << 16)) >> by) & 0xFFFF


def below(k):
    return (1 << k) - 1


def exact(values):
    return values.astype(jnp.float32).astype(jnp.bfloat16)


def dot(left, right):
    return jnp.dot(left, right, preferred_element_type=jnp.float32)


def standing(row):
    size = row.shape[1]
    down = lax.broadcasted_iota(jnp.int32, (size, size), 0)
    along = lax.broadcasted_iota(jnp.int32, (size, size), 1)
    return jnp.sum(jnp.where(down == along, row, 0), axis=1, keepdims=True)


def ends_of(targets, prompt, parity):
    start = node_of(prompt >> 4, parity)
    end = node_of(targets >> 1, targets & 1)
    start = (start & 15) | (end & CORE)
    return start, start ^ end


def earlier_rows(size):
    down = lax.broadcasted_iota(jnp.int32, (size, size), 0)
    along = lax.broadcasted_iota(jnp.int32, (size, size), 1)
    return exact(jnp.where(along < down, 1, 0))


SENT, RECEIVED, SLOTS, HELD = 0, 16, 32, 36


def first_plan_kernel(where_ref, targets_ref, lens_ref, const_ref, table_ref):
    me, group = where_ref[0], where_ref[2]
    local = lax.broadcasted_iota(jnp.int32, (32, 1), 0)
    prompt = 16 * (group & ~1) + local
    match = lax.broadcasted_iota(jnp.int32, (32, targets_ref.shape[1]), 1) == prompt
    targets = jnp.sum(jnp.where(match, targets_ref[...], 0), axis=1, keepdims=True)
    lens = jnp.sum(jnp.where(match, lens_ref[...], 0), axis=1, keepdims=True)
    start, ways = ends_of(targets, prompt, (me >> 3) & 1)
    bit, share = const_ref[1:2, :], const_ref[3:4, :]
    lane = lax.broadcasted_iota(jnp.int32, (1, 64), 1)
    word = turned(share, (prompt * 5) & 15) & below((lens + (CHUNK - 1)) >> 5)
    goes = (lane < 4) & ((ways & bit) != 0) | (lane >= HELD) & (lane < HELD + 4)
    goes = goes & (start == me)
    place = dot(earlier_rows(32), exact(jnp.where(goes, bits_set(word), 0))).astype(jnp.int32)
    place = jnp.where(goes, place, -256)

    def each_chunk(values):
        wide = jnp.broadcast_to(values[:, None, :], (32, PROMPT_CHUNKS, values.shape[1]))
        return wide.reshape(32 * PROMPT_CHUNKS, values.shape[1])

    unit = lax.broadcasted_iota(jnp.int32, (HOME, 1), 0)
    k = unit & 15
    home = jnp.where(((unit >> 8) & 1) == (group & 1), 0, OWN_CHUNKS) + (unit & (OWN_CHUNKS - 1))
    words = each_chunk(word)
    spot = jnp.where(((words >> k) & 1) != 0, each_chunk(place) + bits_set(words & below(k)), -1)
    slot = lax.broadcasted_iota(jnp.int32, (1, 128), 1)
    rows = []
    for c in (0, 1, 2, 3, HELD, HELD + 1, HELD + 2, HELD + 3):
        rows.append(jnp.sum(jnp.where(spot[:, c : c + 1] == slot, home, 0), axis=0, keepdims=True))
    table_ref[...] = jnp.concatenate(rows, axis=0)


LENGTH, OVER = 32, 33


def plan_kernel(where_ref, targets_ref, lens_ref, const_ref, slots_ref, land_ref):
    me, mine = where_ref[0], where_ref[1]
    row_t = jnp.concatenate([targets_ref[...], targets_ref[...]], axis=1)
    items = row_t.shape[1]
    prompts = items // 2
    col_t, col_l = standing(targets_ref[...]), standing(lens_ref[...])
    col_t, col_l = (jnp.concatenate([c, c], axis=0) for c in (col_t, col_l))
    item = lax.broadcasted_iota(jnp.int32, (items, 1), 0)
    prompt, parity = item & (prompts - 1), item >> 8
    start, ways = ends_of(col_t, prompt, parity)
    turn = (prompt * 5) & 15
    routed, bit, sender, share, room = (const_ref[k : k + 1, :] for k in range(5))
    lane = lax.broadcasted_iota(jnp.int32, (1, 64), 1)
    keeps = (lane >= HELD) & (lane < HELD + 4)
    weight = bits_set(turned(share, turn) & below((col_l + (CHUNK - 1)) >> 5))
    crosses = ((ways & bit) != 0) & (lane < SLOTS) | keeps
    listed = crosses & ((start ^ (ways & routed)) == (me ^ sender))
    landing = (col_t == mine) & (lane == SLOTS + parity)
    amount = jnp.where(listed, weight, jnp.where(landing, 1, 0))
    place = dot(earlier_rows(items), exact(amount)).astype(jnp.int32)

    everyone = exact(jnp.where(crosses, weight, 0))
    row_item = lax.broadcasted_iota(jnp.int32, (1, items), 1)
    row_start, row_ways = ends_of(row_t, row_item & (prompts - 1), row_item >> 8)
    nodes = lax.broadcasted_iota(jnp.int32, (32, 1), 0)
    need = jnp.zeros((1, 64), jnp.float32)
    for done in sorted({sum(order[:p]) for order in ORDERS for p in range(4)}):
        present = exact(jnp.where(nodes == (row_start ^ (row_ways & done)), 1, 0))
        held = jnp.max(dot(present, everyone), axis=0, keepdims=True)
        need = jnp.where(routed == done, held, need)
    over = (need.astype(jnp.int32) > room) & ((lane < RECEIVED) | keeps)
    over = jnp.max(jnp.where(over, 1, 0), axis=1, keepdims=True)

    bases = [[place[:, HELD + q : HELD + q + 1] for q in range(4)]]
    for p in range(4):
        came = []
        for q in range(4):
            c = RECEIVED + 4 * p + q
            moved = (ways & ORDERS[q][p]) != 0
            came.append(jnp.where(moved, region(p, q) + place[:, c : c + 1], bases[p][q]))
        bases.append(came)

    slot = lax.broadcasted_iota(jnp.int32, (1, 128), 1)

    def sources(p, q):
        c = 4 * p + q
        first = jnp.where(listed[:, c : c + 1], place[:, c : c + 1], 1 << 20)
        offset = slot - first
        inside = (offset >= 0) & (offset < weight[:, c : c + 1])
        found = jnp.where(inside, offset + bases[p][q], 0)
        return jnp.minimum(jnp.sum(found, axis=0, keepdims=True), region(p, q) - 1)

    slots_ref[...] = jnp.concatenate(
        [jnp.zeros((4, 128), jnp.int32)] + [sources(p, q) for p in range(1, 4) for q in range(4)], axis=0
    )

    rank = jnp.where(parity == 0, place[:, SLOTS : SLOTS + 1], place[:, SLOTS + 1 : SLOTS + 2])
    rank = jnp.where(col_t == mine, rank, -1)
    lands = [rank[:prompts] == slot, rank[prompts:] == slot]

    def landed(value, j):
        return jnp.sum(jnp.where(lands[j], value[j * prompts : (j + 1) * prompts], 0), axis=0, keepdims=True)

    length = landed(col_l, 0)
    live = (length + (CHUNK - 1)) >> 5
    by = landed(turn, 0)
    parts = [turned(jnp.full_like(by, SHARES[q]), by) for q in range(4)]
    rows = []
    for j in range(2):
        held = [landed(bases[4][q], j) for q in range(4)]
        for k in range(PROMPT_CHUNKS):
            source = jnp.zeros_like(by)
            for q in range(4):
                spot = jnp.minimum(held[q] + bits_set(parts[q] & ((1 << k) - 1)), region(4, q) - 1)
                source += ((parts[q] >> k) & 1) * (begin_of(q) + spot)
            rows.append(jnp.where(k < live, source, begin_of(4)))
    rows += [length, jnp.broadcast_to(over, (1, 128)), jnp.zeros((6, 128), jnp.int32)]
    land_ref[...] = jnp.concatenate(rows, axis=0)


def plan_const():
    const = np.zeros((8, 64), np.int32)
    for p in range(4):
        for q, order in enumerate(ORDERS):
            for first, sender in ((SENT, 0), (RECEIVED, order[p])):
                const[:5, first + 4 * p + q] = (sum(order[:p]), order[p], sender, SHARES[q], ROOM[p][q])
    for q in range(4):
        const[3:5, HELD + q] = (SHARES[q], KEPT[q])
    return jnp.asarray(const)


def plan_call(kernel, name, rows, *operands):
    vmem = pl.BlockSpec(memory_space=pltpu.VMEM)
    return pl.pallas_call(
        kernel,
        out_shape=tuple(jax.ShapeDtypeStruct((r, 128), jnp.int32) for r in rows),
        in_specs=[pl.BlockSpec(memory_space=pltpu.SMEM), vmem, vmem, vmem],
        out_specs=(vmem,) * len(rows),
        compiler_params=pltpu.CompilerParams(vmem_limit_bytes=24 * MIB),
        cost_estimate=cost(SMALL),
        name=name,
    )(*operands)


def plan_operands(targets, prompt_lens, group, member):
    where = jnp.stack([node_of(group, member % 2), 2 * group + member % 2, group]).astype(jnp.int32)
    return where, targets.reshape(1, -1), prompt_lens.reshape(1, -1), plan_const()


def fetch(pairs, sems):
    copies = [
        pltpu.make_async_copy(source, target, sems.at[k]) for k, (source, target) in enumerate(pairs)
    ]
    for copy in copies:
        copy.start()
    return copies


def gather_chunks(table_ref, row, out_ref, pick):
    batch = 4

    def body(s, carry):
        first = s * batch
        held = [pick(table_ref[row, first + b]) for b in range(batch)]
        for b in range(batch):
            out_ref[first + b] = held[b]
        return carry

    lax.fori_loop(0, out_ref.shape[0] // batch, body, 0, unroll=2)


SMEM = pl.BlockSpec(memory_space=pltpu.SMEM)
ANY = pl.BlockSpec(memory_space=pl.ANY)
VMEM = pl.BlockSpec(memory_space=pltpu.VMEM)


def chunks_of(count):
    return jax.ShapeDtypeStruct((count, CHUNK, 256), jnp.bfloat16)


def cost(bytes_accessed, flops=0):
    return pl.CostEstimate(flops=flops, bytes_accessed=bytes_accessed, transcendentals=0)


def home_kernel(rows, table_ref, kv_ref, other_ref, *rest):
    outs, space, sems = rest[:4], rest[4], rest[5]
    pairs = [(ref, space.at[pl.ds(OWN_CHUNKS * k, OWN_CHUNKS)]) for k, ref in enumerate((kv_ref, other_ref))]
    for copy in fetch(pairs, sems):
        copy.wait()
    for q in range(4):
        gather_chunks(table_ref, rows + q, outs[q], lambda i: space[i])


def home_lists(rows, rooms, table, kv, other):
    return pl.pallas_call(
        functools.partial(home_kernel, rows),
        out_shape=tuple(chunks_of(room) for room in rooms),
        in_specs=[SMEM, ANY, ANY],
        out_specs=(VMEM,) * 4,
        scratch_shapes=[
            pltpu.VMEM((HOME, CHUNK, 256), jnp.bfloat16),
            pltpu.SemaphoreType.DMA((2,)),
        ],
        compiler_params=pltpu.CompilerParams(vmem_limit_bytes=24 * MIB),
        cost_estimate=cost(SMALL),
        name="home_lists",
    )(table, kv, other)


def part_pairs(part, boxes, space, begin=0):
    pairs = []
    for k, box in enumerate(boxes):
        at = begin + (region(k - 1, part) if k else 0)
        pairs.append((box, space.at[pl.ds(at, box.shape[0])]))
    return pairs


def next_kernel(phase, part, table_ref, *rest):
    boxes, out_ref, space, sems = rest[: phase + 1], rest[phase + 1], rest[phase + 2], rest[phase + 3]
    for copy in fetch(part_pairs(part, boxes, space), sems):
        copy.wait()
    gather_chunks(table_ref, 4 * phase + part, out_ref, lambda i: space[i])


def next_list(phase, part, table, boxes):
    return pl.pallas_call(
        functools.partial(next_kernel, phase, part),
        out_shape=chunks_of(ROOM[phase][part]),
        in_specs=[SMEM] + [ANY] * len(boxes),
        out_specs=VMEM,
        scratch_shapes=[
            pltpu.VMEM((region(phase, part), CHUNK, 256), jnp.bfloat16),
            pltpu.SemaphoreType.DMA((len(boxes),)),
        ],
        compiler_params=pltpu.CompilerParams(vmem_limit_bytes=16 * MIB),
        cost_estimate=cost(SMALL),
        name="next_list",
    )(table, *boxes)


def attend_row(query, first, second, own, length):
    scaling = 1.0 / math.sqrt(query.shape[1])
    upper = lax.broadcasted_iota(jnp.int32, query.shape, 0) < 8
    zero = jnp.zeros_like(query)
    wide = jnp.concatenate([jnp.where(upper, query, zero), jnp.where(upper, zero, query)], axis=1)
    keys = jnp.concatenate([first[:, :128], second[:, :128]], axis=1)
    values = jnp.concatenate([first[:, 128:], second[:, 128:]], axis=1)
    scores = (
        lax.dot_general(wide, keys, (((1,), (1,)), ((), ())), preferred_element_type=jnp.float32)
        * scaling
    )
    own = own.astype(jnp.float32)
    own_key = jnp.where(upper, own[0:1, :128], own[1:2, :128])
    own_value = jnp.where(upper, own[0:1, 128:], own[1:2, 128:])
    own_score = jnp.sum(query.astype(jnp.float32) * own_key, axis=1, keepdims=True) * scaling
    live = lax.broadcasted_iota(jnp.int32, scores.shape, 1) < length
    scores = jnp.where(live, scores, -jnp.inf)
    row_max = jnp.maximum(jnp.max(scores, axis=1, keepdims=True), own_score)
    weights = jnp.where(live, jnp.exp(scores - row_max), 0.0)
    own_weight = jnp.exp(own_score - row_max)
    denominator = jnp.sum(weights, axis=1, keepdims=True) + own_weight
    both = jnp.dot(weights.astype(jnp.bfloat16), values, preferred_element_type=jnp.float32)
    mixture = jnp.where(upper, both[:, :128], both[:, 128:])
    mixture += own_weight.astype(jnp.bfloat16).astype(jnp.float32) * own_value
    return (mixture / denominator).astype(jnp.bfloat16)


TOGETHER = 4
DEPTH = 4 * TOGETHER


def running_kernel(first, half_ref, pages_ref, lens_ref, query_ref, own_ref, pool_ref, out_ref, held, sems):
    rows = out_ref.shape[0]
    all_rows = lens_ref.shape[0] // 2
    max_pages = held.shape[1]
    start = half_ref[0] * all_rows + first

    def each_page(row, action):
        slot = row % DEPTH
        for c in range(max_pages):
            page = pages_ref[(start + row) * max_pages + c]
            action(pltpu.make_async_copy(pool_ref.at[page], held.at[slot, c], sems.at[slot, c]))

    def begin(group):
        for r in range(TOGETHER):
            each_page(group * TOGETHER + r, lambda copy: copy.start())

    ahead = DEPTH // TOGETHER - 1
    for group in range(ahead):
        begin(group)

    def body(group, carry):
        @pl.when(group + ahead < rows // TOGETHER)
        def _():
            begin(group + ahead)

        for r in range(TOGETHER):
            each_page(group * TOGETHER + r, lambda copy: copy.wait())
        results = []
        for r in range(TOGETHER):
            row = group * TOGETHER + r
            slot = row % DEPTH
            blocks = [held[slot, :, j].reshape(max_pages * 64, 256) for j in range(2)]
            results.append(
                attend_row(query_ref[first + row], *blocks, own_ref[first + row], lens_ref[start + row])
            )
        for r in range(TOGETHER):
            out_ref[group * TOGETHER + r] = results[r]
        return carry

    lax.fori_loop(0, rows // TOGETHER, body, 0)


def running_rows(first, count, half, pages, lens, queries, own, pool):
    max_pages = pages.shape[-1]
    return pl.pallas_call(
        functools.partial(running_kernel, first),
        out_shape=jax.ShapeDtypeStruct((count, 16, 128), jnp.bfloat16),
        in_specs=[SMEM, SMEM, SMEM, VMEM, VMEM, pl.BlockSpec(memory_space=pltpu.HBM)],
        out_specs=VMEM,
        scratch_shapes=[
            pltpu.VMEM((DEPTH, max_pages) + pool.shape[1:], jnp.bfloat16),
            pltpu.SemaphoreType.DMA((DEPTH, max_pages)),
        ],
        compiler_params=pltpu.CompilerParams(vmem_limit_bytes=48 * MIB),
        cost_estimate=cost(SMALL),
        name="running_rows",
    )(half, pages.reshape(-1), lens.reshape(-1), queries, own, pool)


RING = 4


def land_kernel(given, land_ref, query_ref, own_ref, *rest):
    contexts, rest = rest[:given], rest[given:]
    boxes, (out_ref, landed_ref, block, sems, space, box_sems) = rest[:20], rest[20:]
    slots = landed_ref.shape[0]
    first = out_ref.shape[0] - slots
    pairs = []
    for q in range(4):
        pairs += part_pairs(q, boxes[5 * q : 5 * q + 5], space, begin_of(q))
    copies = fetch(pairs, box_sems)
    done = 0
    for context in contexts:
        out_ref[done : done + context.shape[0]] = context[...]
        done += context.shape[0]
    space[begin_of(4)] = jnp.zeros((CHUNK, 256), jnp.bfloat16)
    for copy in copies:
        copy.wait()

    def write(slot):
        turn = slot % RING
        return pltpu.make_async_copy(block.at[turn], landed_ref.at[slot], sems.at[turn])

    def assemble(slot):
        turn = slot % RING
        length = land_ref[LENGTH, slot]
        for j in range(2):
            for k in range(0, PROMPT_CHUNKS, 4):
                held = [space[land_ref[PROMPT_CHUNKS * j + k + b, slot]] for b in range(4)]
                for b in range(4):
                    block[turn, j, k + b] = held[b]
        last = jnp.maximum(length - 1, 0) // CHUNK
        row = last * CHUNK + lax.broadcasted_iota(jnp.int32, (CHUNK, 256), 0)
        zero = jnp.zeros((CHUNK, 256), jnp.bfloat16)
        for j in range(2):
            block[turn, j, last] = jnp.where(row < length, block[turn, j, last], zero)

    def body(pair, carry):
        both = (2 * pair, 2 * pair + 1)

        @pl.when(2 * pair >= RING)
        def _():
            for slot in both:
                write(slot).wait()

        for slot in both:
            assemble(slot)
        for slot in both:
            write(slot).start()
        results = []
        for slot in both:
            blocks = [block[slot % RING, j].reshape(PROMPT_CHUNKS * CHUNK, 256) for j in range(2)]
            results.append(
                attend_row(query_ref[first + slot], *blocks, own_ref[first + slot], land_ref[LENGTH, slot])
            )
        for slot, result in zip(both, results):
            out_ref[first + slot] = result
        return carry

    lax.fori_loop(0, slots // 2, body, 0)
    for slot in range(slots - RING, slots):
        write(slot).wait()


def land_rows(slots, land, queries, own, contexts, boxes):
    return pl.pallas_call(
        functools.partial(land_kernel, len(contexts)),
        out_shape=(
            jax.ShapeDtypeStruct(queries.shape, jnp.bfloat16),
            jax.ShapeDtypeStruct((slots, 2, PROMPT_CHUNKS, CHUNK, 256), jnp.bfloat16),
        ),
        in_specs=[SMEM, VMEM, VMEM] + [VMEM] * len(contexts) + [ANY] * 20,
        out_specs=(VMEM, ANY),
        scratch_shapes=[
            pltpu.VMEM((RING, 2, PROMPT_CHUNKS, CHUNK, 256), jnp.bfloat16),
            pltpu.SemaphoreType.DMA((RING,)),
            pltpu.VMEM((begin_of(4) + 1, CHUNK, 256), jnp.bfloat16),
            pltpu.SemaphoreType.DMA((20,)),
        ],
        compiler_params=pltpu.CompilerParams(vmem_limit_bytes=32 * MIB),
        cost_estimate=cost(SMALL),
        name="land_rows",
    )(land, queries, own, *contexts, *boxes)


def routed(operands, kv, other, half, pages, lens, queries, own, pool):
    running = pages.shape[1]
    rows = queries.shape[0]
    (table,) = plan_call(first_plan_kernel, "first_plan", (8,), *operands)
    lists = home_lists(0, ROOM[0], table, kv, other)
    sent = [hop(value, order[0]) for value, order in zip(lists, ORDERS)]
    (where, table), _ = lax.optimization_barrier(((operands[0], table), lists))
    kept = home_lists(4, KEPT, table, kv, other)
    table, land = plan_call(plan_kernel, "plan", (16, 40), where, *operands[1:])
    boxes = [[k] for k in kept]
    contexts = []
    count = running // 2
    for phase in range(1, 4):
        turns = sorted(range(4), key=lambda q: region(phase, q) - KEPT[q])
        lists = [None] * 4
        for q in turns:
            boxes[q] = boxes[q] + [sent[q]]
            lists[q] = next_list(phase, q, table, boxes[q])
            table, _ = lax.optimization_barrier((table, lists[q]))
        if phase > 1:
            ready, _ = lax.optimization_barrier((half, lists))
            context = running_rows(len(contexts) * count, count, ready, pages, lens, queries, own, pool)
            contexts.append(context)
            table, land, _ = lax.optimization_barrier((table, land, context))
        sent = [hop(value, order[phase]) for value, order in zip(lists, ORDERS)]
    boxes = [box for q in range(4) for box in boxes[q] + [sent[q]]]
    context, landed = land_rows(rows - running, land, queries, own, contexts, boxes)
    return context, landed, land[OVER, 0]


def earlier_matches(labels, block_len, kind_count):
    onehot = (labels[:, None] == jnp.arange(kind_count, dtype=jnp.int32)[None, :]).astype(jnp.int32)
    blocks = onehot.reshape(labels.shape[0] // block_len, block_len, kind_count)
    before = jnp.cumsum(blocks, axis=1) - blocks
    return jnp.sum(before * blocks, axis=2).reshape(labels.shape[0])


def lookup(matches):
    prompt_ids = jnp.arange(matches.shape[1], dtype=jnp.int32)
    row_index = jnp.sum(jnp.where(matches, prompt_ids[None, :], 0), axis=1)
    return (row_index, jnp.any(matches, axis=1))


def pick_rows(table_rows, row_index, is_valid):
    picked = jnp.take(table_rows, row_index, axis=0)
    mask_shape = (is_valid.shape[0],) + (1,) * (picked.ndim - 1)
    return jnp.where(is_valid.reshape(mask_shape), picked, jnp.zeros_like(picked))


def any_fill(targets, prompt_lens, kv, queries, own):
    prompt_kv = kv.reshape(16, 1, 512, 256)
    groups = lax.axis_size("grp")
    group_id = lax.axis_index("grp")
    half_id = lax.axis_index("tp") % 2
    block_len = prompt_kv.shape[0]
    prompt_count = targets.shape[0]
    span_len = prompt_kv.shape[2]
    capacity = max(2, block_len // groups)
    source = jnp.arange(prompt_count, dtype=jnp.int32) // block_len
    arrival = earlier_matches(targets, prompt_count, 2 * groups)
    slot_ids = jnp.arange(block_len, dtype=jnp.int32)
    land_match = (targets[None, :] == 2 * group_id + half_id) & (
        arrival[None, :] == slot_ids[:, None]
    )
    land_len = jnp.sum(jnp.where(land_match, prompt_lens[None, :], 0), axis=1)
    land_live = jnp.arange(span_len, dtype=jnp.int32)[None, :] < land_len[:, None]
    land_index, land_valid = lookup(land_match)
    outgoing = source == group_id
    dest_ids = jnp.arange(groups, dtype=jnp.int32)
    cap_ids = jnp.arange(capacity, dtype=jnp.int32)
    partner = hop(prompt_kv, Z)
    pair_kv = jnp.where(
        half_id == 0,
        jnp.concatenate([prompt_kv, partner], axis=1),
        jnp.concatenate([partner, prompt_kv], axis=1),
    )
    within = earlier_matches(targets, block_len, 2 * groups)
    send_match = (
        outgoing[None, None, :]
        & (targets[None, None, :] == (2 * dest_ids + half_id)[:, None, None])
        & (within[None, None, :] == cap_ids[None, :, None])
    )
    send_index, send_valid = lookup(send_match.reshape(groups * capacity, prompt_count))
    send_index = jnp.where(send_valid, send_index - group_id * block_len, 0)
    outbox = pick_rows(pair_kv, send_index, send_valid)
    outbox = outbox.reshape((groups, capacity) + outbox.shape[1:])
    inbound = lax.all_to_all(outbox, "grp", split_axis=0, concat_axis=0, tiled=True)
    inbound = inbound.reshape((groups * capacity,) + inbound.shape[2:])
    entry_ids = source * capacity + within
    landed = pick_rows(inbound, jnp.take(entry_ids, land_index), land_valid)
    landed = jnp.where(land_live[:, None, :, None], landed, jnp.zeros_like(landed))
    handed = jnp.stack(
        [
            attend_row(queries[s], landed[s, 0], landed[s, 1], own[s], land_len[s])
            for s in range(block_len)
        ]
    )
    return handed, landed.reshape(block_len, 2, PROMPT_CHUNKS, CHUNK, 256)


def local(targets, prompt_lens, prompt_kv, cache_pool, block_table, cache_lens, queries, new_kv):
    group = lax.axis_index("grp")
    member = lax.axis_index("tp")
    kv = prompt_kv.reshape(OWN_CHUNKS, CHUNK, 256)
    other = hop(kv, CORE)
    operands = plan_operands(targets, prompt_lens, group, member)
    half = (member % 2).astype(jnp.int32).reshape(1)
    rows = queries.shape[2]
    running = block_table.shape[2]
    by_head = queries.reshape(rows, 16, 128)
    own = new_kv[0, 0]
    context, landed, over = routed(
        operands, kv, other, half, block_table[0], cache_lens[0], by_head, own, cache_pool[0, 0]
    )

    def again(carry):
        handed, landed = any_fill(targets, prompt_lens, kv, by_head[running:], own[running:])
        return carry[0].at[running:].set(handed), landed, jnp.zeros((), jnp.int32)

    context, landed, _ = lax.while_loop(lambda carry: carry[2] > 0, again, (context, landed, over))
    return (
        context.reshape(1, 1, rows, queries.shape[3]),
        landed.reshape(1, 1, 16, 2, 512, 256),
    )


def solution(mesh):
    placed = (
        P(),
        P(),
        P("grp", "tp", None, None),
        P("grp", "tp", None, None, None, None),
        P("grp", None, None, None),
        P("grp", None, None),
        P("grp", "tp", None, None),
        P("grp", "tp", None, None, None),
    )
    return jax.shard_map(
        local,
        mesh=mesh,
        in_specs=placed,
        out_specs=(P("grp", "tp", None, None), P("grp", "tp", None, None, None, None)),
        check_vma=False,
    )
```

time: 144 us -> 138 us (0.958); the launches traced: 144 us -> 136 us
  waiting for transfers between devices: 39.8 us -> 27.7 us
  Pallas kernels: 77.2 us -> 80.9 us
    ppermute x13, waiting for transfers between devices: 35.6 us -> 23.2 us  [hop(): lax.ppermute(value, 'grp', [(g, flipped(g, axis)) for g in range(lax.axis...]
    pallas_call x6 -> x17, Pallas kernels: 44.6 us -> 53.6 us  [the longest x12 25.1 us: next_list(): pl.pallas_call(functools.partial(next_kernel, phase, part), out_shape=chu...]
    pallas_call x4 -> x2, Pallas kernels: 32.6 us -> 27.3 us  [running_rows(): pl.pallas_call(functools.partial(running_kernel, first), out_shape=jax.Sh...]
    reshape x0 -> x1, local copies, waits for them, and re-layouts: none -> 1.84 us  [local(): context.reshape(1, 1, rows, queries.shape[3])]
    concatenate x1 -> x0, local copies, waits for them, and re-layouts: 1.48 us -> none  [local(): jnp.concatenate([decoded, handed], axis=0)]
    unnamed x25 -> x58, local copies, waits for them, and re-layouts: 3.65 us -> 3 us
  transfers between devices with their start and end apart: 17 -> 17, of which waited for: 11 -> 6; matrix products, arithmetic and copies ran while one was open for 2% -> 3% of each run, Pallas kernels for 29% -> 47%
where the time goes in v1:
time: 138 us; the launch traced here: 136 us
  Pallas kernels  80.9 us (59%)
  waiting for transfers between devices  27.7 us (20%)
  starting transfers between devices  18.3 us (13%)
  local copies, waits for them, and re-layouts  7.11 us (5%)
    pallas_call x2, Pallas kernels, running_rows(): pl.pallas_call(functools.partial(running_kernel, first), out_shape=jax.Sh...  27.3 us
    pallas_call x12, Pallas kernels, next_list(): pl.pallas_call(functools.partial(next_kernel, phase, part), out_shape=chu...  25.1 us
    ppermute x13, waiting for transfers between devices, hop(): lax.ppermute(value, 'grp', [(g, flipped(g, axis)) for g in range(lax.axis...  23.2 us
    ppermute x13, starting transfers between devices, hop(): lax.ppermute(value, 'grp', [(g, flipped(g, axis)) for g in range(lax.axis...  12.5 us
    pallas_call x1, Pallas kernels, land_rows(): pl.pallas_call(functools.partial(land_kernel, len(contexts)), out_shape=(...  11.8 us
    pallas_call x2, Pallas kernels, plan_call(): pl.pallas_call(kernel, out_shape=tuple((jax.ShapeDtypeStruct((r, 128), jn...  8.45 us
    pallas_call x2, Pallas kernels, home_lists(): pl.pallas_call(functools.partial(home_kernel, rows), out_shape=tuple((chu...  8.21 us
    ppermute x4, starting transfers between devices, hop(): lax.ppermute(value, 'tp', [(t, t ^ 1) for t in range(lax.axis_size('tp'))])  5.84 us
  transfers between devices with their start and end apart: 17, of which 6 were waited for; matrix products, arithmetic and copies ran while one was open for 3% of the time, Pallas kernels for 47%

profile of v1, /device:TPU:16, one launch (start us, length us, event | category | flops | bytes accessed | tf_op | source)
XLA Modules:
  0.0 135.9 jit_solution(1487309456060253835)
XLA Ops:
  0.7 0.1 collective-permute-start.1
  0.9 0.7 copy-done.18
  1.6 1.8 %first_plan.1.table_ref = s32[8,128]{1,0:T(8,128)S(1)} custom-call(s32[3]{0:T(128)S(1)} %pad_add_fusion.where_ref, s32[1,256]{1,0:T(1,128)} %bitcast.422, s32[1,256]{1,0:T(1,128)} %bitcast.426, s32[8,64]{1,0:T(8,128)S(1)} %copy-done.18), custom_call_target="tpu_custom_call" | custom-call | bytes 4096 | tf_op jit(solution)/shard_map/first_plan/pallas_call | solution.py:240
  3.4 4.9 %collective-permute-done.1.other_ref = bf16[256,32,256]{2,1,0:T(8,128)(2,1)} collective-permute-done((bf16[256,32,256]{2,1,0:T(8,128)(2,1)}, bf16[256,32,256]{2,1,0:T(8,128)(2,1)}, u32[]{:S(2)}, u32[]{:S(2)}) %collective-permute-start.1) | collective-permute-done | bytes 4194336 | tf_op jit(solution)/shard_map/ppermute | solution.py:52
  8.2 4.5 %home_lists.2 = (bf16[40,32,256]{2,1,0:T(8,128)(2,1)S(1)}, bf16[40,32,256]{2,1,0:T(8,128)(2,1)S(1)}, bf16[48,32,256]{2,1,0:T(8,128)(2,1)S(1)}, bf16[36,32,256]{2,1,0:T(8,128)(2,1)S(1)}) custom-call(s32[8,128]{1,0:T(8,128)S(1)} %first_plan.1.table_ref, bf16[256,32,256]{2,1,0:T(8,128)(2,1)} %bitcast.407, bf16[256,32,256]{2,1,0:T(8,128)(2,1)} %collective-permute-done.1.other_ref), custom_call_target="tpu_custom_call" | custom-call | bytes 4096 | tf_op jit(solution)/shard_map/home_lists/pallas_call | solution.py:301
  12.8 1.6 %collective-permute-start.3 = (bf16[40,32,256]{2,1,0:T(8,128)(2,1)S(1)}, bf16[40,32,256]{2,1,0:T(8,128)(2,1)S(1)}, u32[]{:S(2)}, u32[]{:S(2)}) collective-permute-start(bf16[40,32,256]{2,1,0:T(8,128)(2,1)S(1)} %get-tuple-element.85), channel_id=1, source_target_pairs={{0,16},{8,24},{16,0},{24,8},{32,48},{40,56},{48,32},{56,40},{64,80... | collective-permute-start | bytes 1966088 | tf_op jit(solution)/shard_map/ppermute | solution.py:52
  14.3 1.3 collective-permute-start.4
  15.6 1.9 %collective-permute-start.2 = (bf16[36,32,256]{2,1,0:T(8,128)(2,1)S(1)}, bf16[36,32,256]{2,1,0:T(8,128)(2,1)S(1)}, u32[]{:S(2)}, u32[]{:S(2)}) collective-permute-start(bf16[36,32,256]{2,1,0:T(8,128)(2,1)S(1)} %get-tuple-element.88), channel_id=1, source_target_pairs={{0,1},{1,0},{2,3},{3,2},{4,5},{5,4},{6,7},{7,6},{8,9},{9,8},{10,11... | collective-permute-start | bytes 1769480 | tf_op jit(solution)/shard_map/ppermute | solution.py:51
  17.6 6.6 %plan.1 = (s32[16,128]{1,0:T(8,128)S(1)}, s32[40,128]{1,0:T(8,128)S(1)}) custom-call(s32[3]{0:T(128)S(1)} %pad_add_fusion.where_ref, s32[1,256]{1,0:T(1,128)S(1)} %bitcast.423, s32[1,256]{1,0:T(1,128)S(1)} %bitcast.427, s32[8,64]{1,0:T(8,128)S(1)} %copy-done.19), custom_call_target="tpu_custom_call" | custom-call | bytes 4096 | tf_op jit(solution)/shard_map/plan/pallas_call | solution.py:240
  24.2 3.7 %home_lists.3 = (bf16[52,32,256]{2,1,0:T(8,128)(2,1)S(1)}, bf16[52,32,256]{2,1,0:T(8,128)(2,1)S(1)}, bf16[64,32,256]{2,1,0:T(8,128)(2,1)S(1)}, bf16[40,32,256]{2,1,0:T(8,128)(2,1)S(1)}) custom-call(s32[8,128]{1,0:T(8,128)S(1)} %first_plan.1.table_ref, bf16[256,32,256]{2,1,0:T(8,128)(2,1)S(1)} %bitcast.408, bf16[256,32,256]{2,1,0:T(8,128)(2,1)} %collective-permute-done.1.other_ref), custom_call_target="tpu_custom_call" | custom-call | bytes 4096 | tf_op jit(solution)/shard_map/home_lists/pallas_call | solution.py:301
  27.9 2.7 %collective-permute-done.2.rest_1_.rest_18_ = bf16[36,32,256]{2,1,0:T(8,128)(2,1)S(1)} collective-permute-done((bf16[36,32,256]{2,1,0:T(8,128)(2,1)S(1)}, bf16[36,32,256]{2,1,0:T(8,128)(2,1)S(1)}, u32[]{:S(2)}, u32[]{:S(2)}) %collective-permute-start.2) | collective-permute-done | bytes 589856 | tf_op jit(solution)/shard_map/ppermute | solution.py:51
  30.6 1.2 next_list.12
  31.8 0.6 collective-permute-start.7
  32.4 1.2 next_list.13
  33.6 1.8 %collective-permute-start.8 = (bf16[48,32,256]{2,1,0:T(8,128)(2,1)S(1)}, bf16[48,32,256]{2,1,0:T(8,128)(2,1)S(1)}, u32[]{:S(2)}, u32[]{:S(2)}) collective-permute-start(bf16[48,32,256]{2,1,0:T(8,128)(2,1)S(1)} %next_list.13), channel_id=1, source_target_pairs={{0,1},{1,0},{2,3},{3,2},{4,5},{5,4},{6,7},{7,6},{8,9},{9,8},{10,11... | collective-permute-start | bytes 2359304 | tf_op jit(solution)/shard_map/ppermute | solution.py:51
  35.4 1.2 next_list.14
  36.7 1.0 next_list.15
  37.7 1.9 %collective-permute-start.9 = (bf16[48,32,256]{2,1,0:T(8,128)(2,1)S(1)}, bf16[48,32,256]{2,1,0:T(8,128)(2,1)S(1)}, u32[]{:S(2)}, u32[]{:S(2)}) collective-permute-start(bf16[48,32,256]{2,1,0:T(8,128)(2,1)S(1)} %next_list.15), channel_id=1, source_target_pairs={{0,32},{8,40},{16,48},{24,56},{32,0},{40,8},{48,16},{56,24},{64,96... | collective-permute-start | bytes 2359304 | tf_op jit(solution)/shard_map/ppermute | solution.py:52
  39.5 13.3 %collective-permute-done.6.rest_2_.rest_9_ = bf16[44,32,256]{2,1,0:T(8,128)(2,1)S(1)} collective-permute-done((bf16[44,32,256]{2,1,0:T(8,128)(2,1)S(1)}, bf16[44,32,256]{2,1,0:T(8,128)(2,1)S(1)}, u32[]{:S(2)}, u32[]{:S(2)}) %collective-permute-start.6) | collective-permute-done | bytes 720928 | tf_op jit(solution)/shard_map/ppermute | solution.py:52
  52.8 2.4 %next_list.16 = bf16[52,32,256]{2,1,0:T(8,128)(2,1)} custom-call(s32[16,128]{1,0:T(8,128)S(1)} %get-tuple-element.110.table_ref, bf16[52,32,256]{2,1,0:T(8,128)(2,1)S(1)} %get-tuple-element.96.rest_0_.rest_7_, bf16[40,32,256]{2,1,0:T(8,128)(2,1)S(1)} %collective-permute-done.4.rest_1_.rest_8_, bf16[44,32,256]{2,1,0:T(8,128)(2,1)S(1)} %collective-permute-done.6.rest_2_.rest_9_), custom_call_target="tpu_custom_call" | custom-call | bytes 4096 | tf_op jit(solution)/shard_map/next_list/pallas_call | solution.py:332
  55.2 2.2 %next_list.17 = bf16[52,32,256]{2,1,0:T(8,128)(2,1)} custom-call(s32[16,128]{1,0:T(8,128)S(1)} %get-tuple-element.110.table_ref, bf16[40,32,256]{2,1,0:T(8,128)(2,1)S(1)} %get-tuple-element.92.rest_0_.rest_17_, bf16[36,32,256]{2,1,0:T(8,128)(2,1)S(1)} %collective-permute-done.2.rest_1_.rest_18_, bf16[48,32,256]{2,1,0:T(8,128)(2,1)S(1)} %collective-permute-done.7.rest_2_.rest_19_), custom_call_target="tpu_custom_call" | custom-call | bytes 4096 | tf_op jit(solution)/shard_map/next_list/pallas_call | solution.py:332
  57.4 2.3 %next_list.18 = bf16[64,32,256]{2,1,0:T(8,128)(2,1)} custom-call(s32[16,128]{1,0:T(8,128)S(1)} %get-tuple-element.110.table_ref, bf16[52,32,256]{2,1,0:T(8,128)(2,1)S(1)} %get-tuple-element.94.rest_0_.rest_2_, bf16[40,32,256]{2,1,0:T(8,128)(2,1)S(1)} %collective-permute-done.3.rest_1_.rest_3_, bf16[48,32,256]{2,1,0:T(8,128)(2,1)S(1)} %collective-permute-done.8.rest_2_.rest_4_), custom_call_target="tpu_custom_call" | custom-call | bytes 4096 | tf_op jit(solution)/shard_map/next_list/pallas_call | solution.py:332
  59.7 0.4 collective-permute-start.13
  60.1 0.5 collective-permute-start.10
  60.6 2.7 %collective-permute-start.11 = (bf16[52,32,256]{2,1,0:T(8,128)(2,1)}, bf16[52,32,256]{2,1,0:T(8,128)(2,1)}, u32[]{:S(2)}, u32[]{:S(2)}) collective-permute-start(bf16[52,32,256]{2,1,0:T(8,128)(2,1)} %next_list.17), channel_id=1, source_target_pairs={{0,32},{8,40},{16,48},{24,56},{32,0},{40,8},{48,16},{56,24},{64,96... | collective-permute-start | bytes 2555912 | tf_op jit(solution)/shard_map/ppermute | solution.py:52
  63.3 2.0 %next_list.19 = bf16[48,32,256]{2,1,0:T(8,128)(2,1)} custom-call(s32[16,128]{1,0:T(8,128)S(1)} %get-tuple-element.110.table_ref, bf16[64,32,256]{2,1,0:T(8,128)(2,1)S(1)} %get-tuple-element.98.rest_0_.rest_12_, bf16[48,32,256]{2,1,0:T(8,128)(2,1)S(1)} %collective-permute-done.5.rest_1_.rest_13_, bf16[48,32,256]{2,1,0:T(8,128)(2,1)S(1)} %collective-permute-done.9.rest_2_.rest_14_), custom_call_target="tpu_custom_call" | custom-call | bytes 4096 | tf_op jit(solution)/shard_map/next_list/pallas_call | solution.py:332
  65.3 1.8 %collective-permute-start.12 = (bf16[48,32,256]{2,1,0:T(8,128)(2,1)}, bf16[48,32,256]{2,1,0:T(8,128)(2,1)}, u32[]{:S(2)}, u32[]{:S(2)}) collective-permute-start(bf16[48,32,256]{2,1,0:T(8,128)(2,1)} %next_list.19), channel_id=1, source_target_pairs={{0,16},{8,24},{16,0},{24,8},{32,48},{40,56},{48,32},{56,40},{64,80... | collective-permute-start | bytes 2359304 | tf_op jit(solution)/shard_map/ppermute | solution.py:52
  67.1 0.8 copy.36
  67.9 1.4 %copy.35 = s32[1,2,64,6]{3,2,1,0:T(8,128)} copy(s32[1,2,64,6]{2,1,3,0:T(2,128)} %param.17) | data formatting | bytes 6144 | tf_op args[4]
  69.3 1.0 reshape_squeeze.8.pages_ref
  70.3 0.8 reshape_squeeze.9.lens_ref
  71.1 14.1 %running_rows.2.rest_0_ = bf16[32,16,128]{2,1,0:T(8,128)(2,1)S(1)} custom-call(s32[1]{0:T(128)} %bitcast.196.half_ref, s32[768]{0:T(1024)S(1)} %reshape_squeeze.8.pages_ref, s32[128]{0:T(128)S(1)} %reshape_squeeze.9.lens_ref, bf16[80,16,128]{2,1,0:T(8,128)(2,1)} %bitcast.411, bf16[80,2,256]{2,1,0:T(2,128)(2,1)} %bitcast.418, bf16[224,2,64,256]{3,2,1,0:T(8,128)(2,1)} %bitcast.409), custom_call_target="tpu_custom_call" | custom-call | bytes 4096 | tf_op jit(solution)/shard_map/running_rows/pallas_call | solution.py:422
  85.3 2.7 %next_list.20 = bf16[72,32,256]{2,1,0:T(8,128)(2,1)S(1)} custom-call(s32[16,128]{1,0:T(8,128)S(1)} %get-tuple-element.110.table_ref, bf16[52,32,256]{2,1,0:T(8,128)(2,1)S(1)} %get-tuple-element.96.rest_0_.rest_7_, bf16[40,32,256]{2,1,0:T(8,128)(2,1)S(1)} %copy-done.3, bf16[44,32,256]{2,1,0:T(8,128)(2,1)S(1)} %copy-done.15, ...), custom_call_target="tpu_custom_call" | custom-call | bytes 4096 | tf_op jit(solution)/shard_map/next_list/pallas_call | solution.py:332
  88.0 0.3 collective-permute-start.15
  88.3 3.4 %next_list.21 = bf16[60,32,256]{2,1,0:T(8,128)(2,1)} custom-call(s32[16,128]{1,0:T(8,128)S(1)} %get-tuple-element.110.table_ref, bf16[40,32,256]{2,1,0:T(8,128)(2,1)S(1)} %copy-done.5, bf16[36,32,256]{2,1,0:T(8,128)(2,1)S(1)} %copy-done.7, bf16[48,32,256]{2,1,0:T(8,128)(2,1)S(1)} %copy-done.9, bf16[52,32,256]{2,1,0:T(8,128)(2,1)} %collective-permute-done.11.rest_3_.rest_20_), custom_call_target="tpu_custom_call" | custom-call | bytes 4096 | tf_op jit(solution)/shard_map/next_list/pallas_call | solution.py:332
  91.7 3.2 %next_list.22 = bf16[68,32,256]{2,1,0:T(8,128)(2,1)} custom-call(s32[16,128]{1,0:T(8,128)S(1)} %get-tuple-element.110.table_ref, bf16[64,32,256]{2,1,0:T(8,128)(2,1)S(1)} %get-tuple-element.98.rest_0_.rest_12_, bf16[48,32,256]{2,1,0:T(8,128)(2,1)S(1)} %collective-permute-done.5.rest_1_.rest_13_, bf16[48,32,256]{2,1,0:T(8,128)(2,1)S(1)} %copy-done.13, ...), custom_call_target="tpu_custom_call" | custom-call | bytes 4096 | tf_op jit(solution)/shard_map/next_list/pallas_call | solution.py:332
  94.9 2.5 %next_list.23 = bf16[72,32,256]{2,1,0:T(8,128)(2,1)S(1)} custom-call(s32[16,128]{1,0:T(8,128)S(1)} %get-tuple-element.110.table_ref, bf16[52,32,256]{2,1,0:T(8,128)(2,1)S(1)} %get-tuple-element.94.rest_0_.rest_2_, bf16[40,32,256]{2,1,0:T(8,128)(2,1)S(1)} %copy-done.1, bf16[48,32,256]{2,1,0:T(8,128)(2,1)S(1)} %copy-done.11, ...), custom_call_target="tpu_custom_call" | custom-call | bytes 4096 | tf_op jit(solution)/shard_map/next_list/pallas_call | solution.py:332
  97.5 0.3 collective-permute-start.14
  97.8 1.6 %collective-permute-start.16 = (bf16[68,32,256]{2,1,0:T(8,128)(2,1)}, bf16[68,32,256]{2,1,0:T(8,128)(2,1)S(1)}, u32[]{:S(2)}, u32[]{:S(2)}) collective-permute-start(bf16[68,32,256]{2,1,0:T(8,128)(2,1)} %next_list.22), channel_id=1, source_target_pairs={{0,1},{1,0},{2,3},{3,2},{4,5},{5,4},{6,7},{7,6},{8,9},{9,8},{10,11... | collective-permute-start | bytes 3342344 | tf_op jit(solution)/shard_map/ppermute | solution.py:51
  99.4 1.5 %collective-permute-start.17 = (bf16[60,32,256]{2,1,0:T(8,128)(2,1)}, bf16[60,32,256]{2,1,0:T(8,128)(2,1)S(1)}, u32[]{:S(2)}, u32[]{:S(2)}) collective-permute-start(bf16[60,32,256]{2,1,0:T(8,128)(2,1)} %next_list.21), channel_id=1, source_target_pairs={{0,96},{8,104},{16,112},{24,120},{32,64},{40,72},{48,80},{56,88},{... | collective-permute-start | bytes 2949128 | tf_op jit(solution)/shard_map/ppermute | solution.py:52
  100.9 13.2 %running_rows.3.rest_1_ = bf16[32,16,128]{2,1,0:T(8,128)(2,1)S(1)} custom-call(s32[1]{0:T(128)} %bitcast.196.half_ref, s32[768]{0:T(1024)S(1)} %reshape_squeeze.8.pages_ref, s32[128]{0:T(128)S(1)} %reshape_squeeze.9.lens_ref, bf16[80,16,128]{2,1,0:T(8,128)(2,1)S(1)} %bitcast.413, bf16[80,2,256]{2,1,0:T(2,128)(2,1)S(1)} %bitcast.420, ...), custom_call_target="tpu_custom_call" | custom-call | bytes 4096 | tf_op jit(solution)/shard_map/running_rows/pallas_call | solution.py:422
  114.1 0.5 slice.785
  114.6 4.0 %collective-permute-done.17.rest_21_ = bf16[60,32,256]{2,1,0:T(8,128)(2,1)S(1)} collective-permute-done((bf16[60,32,256]{2,1,0:T(8,128)(2,1)}, bf16[60,32,256]{2,1,0:T(8,128)(2,1)S(1)}, u32[]{:S(2)}, u32[]{:S(2)}) %collective-permute-start.17) | collective-permute-done | bytes 983072 | tf_op jit(solution)/shard_map/ppermute | solution.py:52
  118.6 1.8 %collective-permute-done.16.rest_16_ = bf16[68,32,256]{2,1,0:T(8,128)(2,1)S(1)} collective-permute-done((bf16[68,32,256]{2,1,0:T(8,128)(2,1)}, bf16[68,32,256]{2,1,0:T(8,128)(2,1)S(1)}, u32[]{:S(2)}, u32[]{:S(2)}) %collective-permute-start.16) | collective-permute-done | bytes 1114144 | tf_op jit(solution)/shard_map/ppermute | solution.py:51
  120.5 1.1 collective-permute-done.14.rest_6_
  121.5 11.8 %land_rows.1 = (bf16[80,16,128]{2,1,0:T(8,128)(2,1)}, bf16[16,2,16,32,256]{4,3,2,1,0:T(8,128)(2,1)}) custom-call(s32[40,128]{1,0:T(8,128)S(1)} %copy-done.17, bf16[80,16,128]{2,1,0:T(8,128)(2,1)S(1)} %bitcast.414, bf16[80,2,256]{2,1,0:T(2,128)(2,1)S(1)} %bitcast.421, bf16[32,16,128]{2,1,0:T(8,128)(2,1)S(1)} %running_rows.2.rest_0_, ...), custom_call_target="tpu_custom_call" | custom-call | bytes 4096 | tf_op jit(solution)/shard_map/land_rows/pallas_call | solution.py:503
  133.4 0.6 while.12
  134.0 1.8 %reshape.874 = bf16[1,1,80,2048]{3,2,1,0:T(8,128)(2,1)} reshape(bf16[80,16,128]{2,1,0:T(8,128)(2,1)} %get-tuple-element.115) | data formatting | bytes 655360 | tf_op jit(solution)/shard_map/reshape | solution.py:644
  (69 shorter events, 0.3 us)
Async XLA Ops:
  0.6 16.9 %copy-start.19 = (s32[8,64]{1,0:T(8,128)S(1)}, s32[8,64]{1,0:T(8,128)}, u32[]{:S(2)}) copy-start(s32[8,64]{1,0:T(8,128)} %constant.173.clone.const_ref) | copy-start | bytes 6148
  0.6 16.9 %copy-start.23 = (s32[256]{0:T(256)S(1)}, s32[256]{0:T(256)}, u32[]{:S(2)}) copy-start(s32[256]{0:T(256)} %param.13) | copy-start | bytes 3076
  0.7 16.9 %copy-start.26 = (s32[256]{0:T(256)S(1)}, s32[256]{0:T(256)}, u32[]{:S(2)}) copy-start(s32[256]{0:T(256)} %param.14) | copy-start | bytes 3076
  0.7 7.6 %collective-permute-start.1 = (bf16[256,32,256]{2,1,0:T(8,128)(2,1)}, bf16[256,32,256]{2,1,0:T(8,128)(2,1)}, u32[]{:S(2)}, u32[]{:S(2)}) collective-permute-start(bf16[256,32,256]{2,1,0:T(8,128)(2,1)} %bitcast.406), channel_id=1, source_target_pairs={{0,8},{8,0},{16,24},{24,16},{32,40},{40,32},{48,56},{56,48},{64,72... | collective-permute-start | bytes 12582920 | tf_op jit(solution)/shard_map/ppermute | solution.py:52
  0.9 0.7 copy-start.18
  1.5 22.6 %copy-start.20 = (bf16[16,1,512,256]{3,2,1,0:T(8,128)(2,1)S(1)}, bf16[16,1,512,256]{3,2,1,0:T(8,128)(2,1)}, u32[]{:S(2)}) copy-start(bf16[16,1,512,256]{3,2,1,0:T(8,128)(2,1)} %param.15) | copy-start | bytes 12582916
  12.8 19.6 %collective-permute-start.3 = (bf16[40,32,256]{2,1,0:T(8,128)(2,1)S(1)}, bf16[40,32,256]{2,1,0:T(8,128)(2,1)S(1)}, u32[]{:S(2)}, u32[]{:S(2)}) collective-permute-start(bf16[40,32,256]{2,1,0:T(8,128)(2,1)S(1)} %get-tuple-element.85), channel_id=1, source_target_pairs={{0,16},{8,24},{16,0},{24,8},{32,48},{40,56},{48,32},{56,40},{64,80... | collective-permute-start | bytes 1966088 | tf_op jit(solution)/shard_map/ppermute | solution.py:52
  14.3 21.1 %collective-permute-start.4 = (bf16[40,32,256]{2,1,0:T(8,128)(2,1)S(1)}, bf16[40,32,256]{2,1,0:T(8,128)(2,1)S(1)}, u32[]{:S(2)}, u32[]{:S(2)}) collective-permute-start(bf16[40,32,256]{2,1,0:T(8,128)(2,1)S(1)} %get-tuple-element.86), channel_id=1, source_target_pairs={{0,32},{8,40},{16,48},{24,56},{32,0},{40,8},{48,16},{56,24},{64,96... | collective-permute-start | bytes 1966088 | tf_op jit(solution)/shard_map/ppermute | solution.py:52
  15.6 15.0 %collective-permute-start.2 = (bf16[36,32,256]{2,1,0:T(8,128)(2,1)S(1)}, bf16[36,32,256]{2,1,0:T(8,128)(2,1)S(1)}, u32[]{:S(2)}, u32[]{:S(2)}) collective-permute-start(bf16[36,32,256]{2,1,0:T(8,128)(2,1)S(1)} %get-tuple-element.88), channel_id=1, source_target_pairs={{0,1},{1,0},{2,3},{3,2},{4,5},{5,4},{6,7},{7,6},{8,9},{9,8},{10,11... | collective-permute-start | bytes 1769480 | tf_op jit(solution)/shard_map/ppermute | solution.py:51
  17.5 19.1 %collective-permute-start.5 = (bf16[48,32,256]{2,1,0:T(8,128)(2,1)S(1)}, bf16[48,32,256]{2,1,0:T(8,128)(2,1)S(1)}, u32[]{:S(2)}, u32[]{:S(2)}) collective-permute-start(bf16[48,32,256]{2,1,0:T(8,128)(2,1)S(1)} %get-tuple-element.87), channel_id=1, source_target_pairs={{0,96},{8,104},{16,112},{24,120},{32,64},{40,72},{48,80},{56,88},{... | collective-permute-start | bytes 2359304 | tf_op jit(solution)/shard_map/ppermute | solution.py:52
  24.2 13.5 %copy-start.16 = (s32[40,128]{1,0:T(8,128)}, s32[40,128]{1,0:T(8,128)S(1)}, u32[]{:S(2)}) copy-start(s32[40,128]{1,0:T(8,128)S(1)} %get-tuple-element.112.land_ref) | copy-start | bytes 61444
  27.9 31.8 %copy-start.4 = (bf16[40,32,256]{2,1,0:T(8,128)(2,1)}, bf16[40,32,256]{2,1,0:T(8,128)(2,1)S(1)}, u32[]{:S(2)}) copy-start(bf16[40,32,256]{2,1,0:T(8,128)(2,1)S(1)} %get-tuple-element.92.rest_0_.rest_17_) | copy-start | bytes 1966084
  30.6 29.1 %copy-start.6 = (bf16[36,32,256]{2,1,0:T(8,128)(2,1)}, bf16[36,32,256]{2,1,0:T(8,128)(2,1)S(1)}, u32[]{:S(2)}) copy-start(bf16[36,32,256]{2,1,0:T(8,128)(2,1)S(1)} %collective-permute-done.2.rest_1_.rest_18_) | copy-start | bytes 1769476
  31.8 23.4 %collective-permute-start.7 = (bf16[48,32,256]{2,1,0:T(8,128)(2,1)S(1)}, bf16[48,32,256]{2,1,0:T(8,128)(2,1)S(1)}, u32[]{:S(2)}, u32[]{:S(2)}) collective-permute-start(bf16[48,32,256]{2,1,0:T(8,128)(2,1)S(1)} %next_list.12), channel_id=1, source_target_pairs={{0,16},{8,24},{16,0},{24,8},{32,48},{40,56},{48,32},{56,40},{64,80... | collective-permute-start | bytes 2359304 | tf_op jit(solution)/shard_map/ppermute | solution.py:52
  32.4 32.9 %copy-start = (bf16[40,32,256]{2,1,0:T(8,128)(2,1)}, bf16[40,32,256]{2,1,0:T(8,128)(2,1)S(1)}, u32[]{:S(2)}) copy-start(bf16[40,32,256]{2,1,0:T(8,128)(2,1)S(1)} %collective-permute-done.3.rest_1_.rest_3_) | copy-start | bytes 1966084
  33.6 23.8 %collective-permute-start.8 = (bf16[48,32,256]{2,1,0:T(8,128)(2,1)S(1)}, bf16[48,32,256]{2,1,0:T(8,128)(2,1)S(1)}, u32[]{:S(2)}, u32[]{:S(2)}) collective-permute-start(bf16[48,32,256]{2,1,0:T(8,128)(2,1)S(1)} %next_list.13), channel_id=1, source_target_pairs={{0,1},{1,0},{2,3},{3,2},{4,5},{5,4},{6,7},{7,6},{8,9},{9,8},{10,11... | collective-permute-start | bytes 2359304 | tf_op jit(solution)/shard_map/ppermute | solution.py:51
  35.4 29.9 %copy-start.2 = (bf16[40,32,256]{2,1,0:T(8,128)(2,1)}, bf16[40,32,256]{2,1,0:T(8,128)(2,1)S(1)}, u32[]{:S(2)}) copy-start(bf16[40,32,256]{2,1,0:T(8,128)(2,1)S(1)} %collective-permute-done.4.rest_1_.rest_8_) | copy-start | bytes 1966084
  35.4 31.7 %copy-start.25 = (bf16[1,1,80,2048]{3,2,1,0:T(8,128)(2,1)S(1)}, bf16[1,1,80,2048]{3,2,1,0:T(8,128)(2,1)}, u32[]{:S(2)}) copy-start(bf16[1,1,80,2048]{3,2,1,0:T(8,128)(2,1)} %param.19) | copy-start | bytes 983044
  36.6 16.2 %collective-permute-start.6 = (bf16[44,32,256]{2,1,0:T(8,128)(2,1)S(1)}, bf16[44,32,256]{2,1,0:T(8,128)(2,1)S(1)}, u32[]{:S(2)}, u32[]{:S(2)}) collective-permute-start(bf16[44,32,256]{2,1,0:T(8,128)(2,1)S(1)} %next_list.14), channel_id=1, source_target_pairs={{0,96},{8,104},{16,112},{24,120},{32,64},{40,72},{48,80},{56,88},{... | collective-permute-start | bytes 2162696 | tf_op jit(solution)/shard_map/ppermute | solution.py:52
  37.7 25.7 %collective-permute-start.9 = (bf16[48,32,256]{2,1,0:T(8,128)(2,1)S(1)}, bf16[48,32,256]{2,1,0:T(8,128)(2,1)S(1)}, u32[]{:S(2)}, u32[]{:S(2)}) collective-permute-start(bf16[48,32,256]{2,1,0:T(8,128)(2,1)S(1)} %next_list.15), channel_id=1, source_target_pairs={{0,32},{8,40},{16,48},{24,56},{32,0},{40,8},{48,16},{56,24},{64,96... | collective-permute-start | bytes 2359304 | tf_op jit(solution)/shard_map/ppermute | solution.py:52
  52.8 14.3 %copy-start.14 = (bf16[44,32,256]{2,1,0:T(8,128)(2,1)}, bf16[44,32,256]{2,1,0:T(8,128)(2,1)S(1)}, u32[]{:S(2)}) copy-start(bf16[44,32,256]{2,1,0:T(8,128)(2,1)S(1)} %collective-permute-done.6.rest_2_.rest_9_) | copy-start | bytes 2162692
  55.2 11.9 %copy-start.8 = (bf16[48,32,256]{2,1,0:T(8,128)(2,1)}, bf16[48,32,256]{2,1,0:T(8,128)(2,1)S(1)}, u32[]{:S(2)}) copy-start(bf16[48,32,256]{2,1,0:T(8,128)(2,1)S(1)} %collective-permute-done.7.rest_2_.rest_19_) | copy-start | bytes 2359300
  57.4 2.7 %copy-start.10 = (bf16[48,32,256]{2,1,0:T(8,128)(2,1)}, bf16[48,32,256]{2,1,0:T(8,128)(2,1)S(1)}, u32[]{:S(2)}) copy-start(bf16[48,32,256]{2,1,0:T(8,128)(2,1)S(1)} %collective-permute-done.8.rest_2_.rest_4_) | copy-start | bytes 2359300
  59.7 35.1 %collective-permute-start.13 = (bf16[64,32,256]{2,1,0:T(8,128)(2,1)}, bf16[64,32,256]{2,1,0:T(8,128)(2,1)}, u32[]{:S(2)}, u32[]{:S(2)}) collective-permute-start(bf16[64,32,256]{2,1,0:T(8,128)(2,1)} %next_list.18), channel_id=1, source_target_pairs={{0,96},{8,104},{16,112},{24,120},{32,64},{40,72},{48,80},{56,88},{... | collective-permute-start | bytes 3145736 | tf_op jit(solution)/shard_map/ppermute | solution.py:52
  60.1 25.1 %collective-permute-start.10 = (bf16[52,32,256]{2,1,0:T(8,128)(2,1)}, bf16[52,32,256]{2,1,0:T(8,128)(2,1)}, u32[]{:S(2)}, u32[]{:S(2)}) collective-permute-start(bf16[52,32,256]{2,1,0:T(8,128)(2,1)} %next_list.16), channel_id=1, source_target_pairs={{0,1},{1,0},{2,3},{3,2},{4,5},{5,4},{6,7},{7,6},{8,9},{9,8},{10,11... | collective-permute-start | bytes 2555912 | tf_op jit(solution)/shard_map/ppermute | solution.py:51
  60.6 27.7 %collective-permute-start.11 = (bf16[52,32,256]{2,1,0:T(8,128)(2,1)}, bf16[52,32,256]{2,1,0:T(8,128)(2,1)}, u32[]{:S(2)}, u32[]{:S(2)}) collective-permute-start(bf16[52,32,256]{2,1,0:T(8,128)(2,1)} %next_list.17), channel_id=1, source_target_pairs={{0,32},{8,40},{16,48},{24,56},{32,0},{40,8},{48,16},{56,24},{64,96... | collective-permute-start | bytes 2555912 | tf_op jit(solution)/shard_map/ppermute | solution.py:52
  63.3 3.8 %copy-start.12 = (bf16[48,32,256]{2,1,0:T(8,128)(2,1)}, bf16[48,32,256]{2,1,0:T(8,128)(2,1)S(1)}, u32[]{:S(2)}) copy-start(bf16[48,32,256]{2,1,0:T(8,128)(2,1)S(1)} %collective-permute-done.9.rest_2_.rest_14_) | copy-start | bytes 2359300
  65.3 26.3 %collective-permute-start.12 = (bf16[48,32,256]{2,1,0:T(8,128)(2,1)}, bf16[48,32,256]{2,1,0:T(8,128)(2,1)}, u32[]{:S(2)}, u32[]{:S(2)}) collective-permute-start(bf16[48,32,256]{2,1,0:T(8,128)(2,1)} %next_list.19), channel_id=1, source_target_pairs={{0,16},{8,24},{16,0},{24,8},{32,48},{40,56},{48,32},{56,40},{64,80... | collective-permute-start | bytes 2359304 | tf_op jit(solution)/shard_map/ppermute | solution.py:52
  71.0 14.2 %copy-start.3 = (bf16[40,32,256]{2,1,0:T(8,128)(2,1)S(1)}, bf16[40,32,256]{2,1,0:T(8,128)(2,1)}, u32[]{:S(2)}) copy-start(bf16[40,32,256]{2,1,0:T(8,128)(2,1)} %copy-done.2) | copy-start | bytes 1966084
  71.0 14.2 %copy-start.15 = (bf16[44,32,256]{2,1,0:T(8,128)(2,1)S(1)}, bf16[44,32,256]{2,1,0:T(8,128)(2,1)}, u32[]{:S(2)}) copy-start(bf16[44,32,256]{2,1,0:T(8,128)(2,1)} %copy-done.14) | copy-start | bytes 2162692
  71.0 17.2 %copy-start.5 = (bf16[40,32,256]{2,1,0:T(8,128)(2,1)S(1)}, bf16[40,32,256]{2,1,0:T(8,128)(2,1)}, u32[]{:S(2)}) copy-start(bf16[40,32,256]{2,1,0:T(8,128)(2,1)} %copy-done.4) | copy-start | bytes 1966084
  71.0 17.2 %copy-start.7 = (bf16[36,32,256]{2,1,0:T(8,128)(2,1)S(1)}, bf16[36,32,256]{2,1,0:T(8,128)(2,1)}, u32[]{:S(2)}) copy-start(bf16[36,32,256]{2,1,0:T(8,128)(2,1)} %copy-done.6) | copy-start | bytes 1769476
  71.0 17.2 %copy-start.9 = (bf16[48,32,256]{2,1,0:T(8,128)(2,1)S(1)}, bf16[48,32,256]{2,1,0:T(8,128)(2,1)}, u32[]{:S(2)}) copy-start(bf16[48,32,256]{2,1,0:T(8,128)(2,1)} %copy-done.8) | copy-start | bytes 2359300
  71.1 20.6 %copy-start.13 = (bf16[48,32,256]{2,1,0:T(8,128)(2,1)S(1)}, bf16[48,32,256]{2,1,0:T(8,128)(2,1)}, u32[]{:S(2)}) copy-start(bf16[48,32,256]{2,1,0:T(8,128)(2,1)} %copy-done.12) | copy-start | bytes 2359300
  85.2 9.7 %copy-start.1 = (bf16[40,32,256]{2,1,0:T(8,128)(2,1)S(1)}, bf16[40,32,256]{2,1,0:T(8,128)(2,1)}, u32[]{:S(2)}) copy-start(bf16[40,32,256]{2,1,0:T(8,128)(2,1)} %copy-done) | copy-start | bytes 1966084
  85.2 9.7 %copy-start.11 = (bf16[48,32,256]{2,1,0:T(8,128)(2,1)S(1)}, bf16[48,32,256]{2,1,0:T(8,128)(2,1)}, u32[]{:S(2)}) copy-start(bf16[48,32,256]{2,1,0:T(8,128)(2,1)} %copy-done.10) | copy-start | bytes 2359300
  85.2 15.7 %copy-start.21 = (bf16[10,8,16,128]{3,2,1,0:T(8,128)(2,1)S(1)}, bf16[10,8,16,128]{3,2,1,0:T(8,128)(2,1)}, u32[]{:S(2)}) copy-start(bf16[10,8,16,128]{3,2,1,0:T(8,128)(2,1)} %copy.36) | copy-start | bytes 983044
  85.2 15.7 %copy-start.22 = (bf16[1,1,80,2,256]{4,3,2,1,0:T(2,128)(2,1)S(1)}, bf16[1,1,80,2,256]{4,3,2,1,0:T(2,128)(2,1)}, u32[]{:S(2)}) copy-start(bf16[1,1,80,2,256]{4,3,2,1,0:T(2,128)(2,1)} %param.20) | copy-start | bytes 245764
  88.0 30.7 %collective-permute-start.15 = (bf16[72,32,256]{2,1,0:T(8,128)(2,1)S(1)}, bf16[72,32,256]{2,1,0:T(8,128)(2,1)S(1)}, u32[]{:S(2)}, u32[]{:S(2)}) collective-permute-start(bf16[72,32,256]{2,1,0:T(8,128)(2,1)S(1)} %next_list.20), channel_id=1, source_target_pairs={{0,16},{8,24},{16,0},{24,8},{32,48},{40,56},{48,32},{56,40},{64,80... | collective-permute-start | bytes 3538952 | tf_op jit(solution)/shard_map/ppermute | solution.py:52
  97.4 16.6 %copy-start.17 = (s32[40,128]{1,0:T(8,128)S(1)}, s32[40,128]{1,0:T(8,128)}, u32[]{:S(2)}) copy-start(s32[40,128]{1,0:T(8,128)} %copy-done.16) | copy-start | bytes 61444
  97.5 24.1 %collective-permute-start.14 = (bf16[72,32,256]{2,1,0:T(8,128)(2,1)S(1)}, bf16[72,32,256]{2,1,0:T(8,128)(2,1)S(1)}, u32[]{:S(2)}, u32[]{:S(2)}) collective-permute-start(bf16[72,32,256]{2,1,0:T(8,128)(2,1)S(1)} %next_list.23), channel_id=1, source_target_pairs={{0,32},{8,40},{16,48},{24,56},{32,0},{40,8},{48,16},{56,24},{64,96... | collective-permute-start | bytes 3538952 | tf_op jit(solution)/shard_map/ppermute | solution.py:52
  97.8 22.7 %collective-permute-start.16 = (bf16[68,32,256]{2,1,0:T(8,128)(2,1)}, bf16[68,32,256]{2,1,0:T(8,128)(2,1)S(1)}, u32[]{:S(2)}, u32[]{:S(2)}) collective-permute-start(bf16[68,32,256]{2,1,0:T(8,128)(2,1)} %next_list.22), channel_id=1, source_target_pairs={{0,1},{1,0},{2,3},{3,2},{4,5},{5,4},{6,7},{7,6},{8,9},{9,8},{10,11... | collective-permute-start | bytes 3342344 | tf_op jit(solution)/shard_map/ppermute | solution.py:51
  99.4 19.2 %collective-permute-start.17 = (bf16[60,32,256]{2,1,0:T(8,128)(2,1)}, bf16[60,32,256]{2,1,0:T(8,128)(2,1)S(1)}, u32[]{:S(2)}, u32[]{:S(2)}) collective-permute-start(bf16[60,32,256]{2,1,0:T(8,128)(2,1)} %next_list.21), channel_id=1, source_target_pairs={{0,96},{8,104},{16,112},{24,120},{32,64},{40,72},{48,80},{56,88},{... | collective-permute-start | bytes 2949128 | tf_op jit(solution)/shard_map/ppermute | solution.py:52
  114.6 18.7 %copy-start.24 = (s32[256]{0:T(256)S(1)}, s32[256]{0:T(256)}, u32[]{:S(2)}) copy-start(s32[256]{0:T(256)} %param.13) | copy-start | bytes 3076
  114.6 18.7 %copy-start.27 = (s32[256]{0:T(256)S(1)}, s32[256]{0:T(256)}, u32[]{:S(2)}) copy-start(s32[256]{0:T(256)} %param.14) | copy-start | bytes 3076

commit v2 on v1

--- a/solution.py
+++ b/solution.py
@@ -29,8 +29,11 @@
     return KEPT[part] + sum(rooms[part] for rooms in ROOM[:phase])
 
 
-def begin_of(part):
-    return sum(region(4, q) for q in range(part))
+def begin_of(part, phase):
+    return sum(region(phase, q) for q in range(part))
+
+
+LATE_BEGIN = tuple(sum(ROOM[3][:q]) for q in range(5))
 
 
 def flipped(group, mask):
@@ -141,7 +144,7 @@
     table_ref[...] = jnp.concatenate(rows, axis=0)
 
 
-LENGTH, OVER = 32, 33
+LATE, LENGTH, OVER = 32, 64, 65
 
 
 def plan_kernel(where_ref, targets_ref, lens_ref, const_ref, slots_ref, land_ref):
@@ -169,11 +172,13 @@
     row_item = lax.broadcasted_iota(jnp.int32, (1, items), 1)
     row_start, row_ways = ends_of(row_t, row_item & (prompts - 1), row_item >> 8)
     nodes = lax.broadcasted_iota(jnp.int32, (32, 1), 0)
+    ways_done = sorted({sum(order[:p]) for order in ORDERS for p in range(4)})
+    present = [jnp.where(nodes == (row_start ^ (row_ways & done)), 1, 0) for done in ways_done]
+    held = dot(exact(jnp.concatenate(present, axis=0)), everyone)
     need = jnp.zeros((1, 64), jnp.float32)
-    for done in sorted({sum(order[:p]) for order in ORDERS for p in range(4)}):
-        present = exact(jnp.where(nodes == (row_start ^ (row_ways & done)), 1, 0))
-        held = jnp.max(dot(present, everyone), axis=0, keepdims=True)
-        need = jnp.where(routed == done, held, need)
+    for k, done in enumerate(ways_done):
+        most = jnp.max(held[32 * k : 32 * k + 32], axis=0, keepdims=True)
+        need = jnp.where(routed == done, most, need)
     over = (need.astype(jnp.int32) > room) & ((lane < RECEIVED) | keeps)
     over = jnp.max(jnp.where(over, 1, 0), axis=1, keepdims=True)
 
@@ -210,18 +215,27 @@
     length = landed(col_l, 0)
     live = (length + (CHUNK - 1)) >> 5
     by = landed(turn, 0)
-    parts = [turned(jnp.full_like(by, SHARES[q]), by) for q in range(4)]
-    rows = []
+    k = lax.broadcasted_iota(jnp.int32, (PROMPT_CHUNKS, 1), 0)
+    early, late = [], []
     for j in range(2):
-        held = [landed(bases[4][q], j) for q in range(4)]
-        for k in range(PROMPT_CHUNKS):
-            source = jnp.zeros_like(by)
-            for q in range(4):
-                spot = jnp.minimum(held[q] + bits_set(parts[q] & ((1 << k) - 1)), region(4, q) - 1)
-                source += ((parts[q] >> k) & 1) * (begin_of(q) + spot)
-            rows.append(jnp.where(k < live, source, begin_of(4)))
-    rows += [length, jnp.broadcast_to(over, (1, 128)), jnp.zeros((6, 128), jnp.int32)]
-    land_ref[...] = jnp.concatenate(rows, axis=0)
+        here = jnp.zeros((PROMPT_CHUNKS, 128), jnp.int32)
+        last = jnp.zeros((PROMPT_CHUNKS, 128), jnp.int32)
+        for q in range(4):
+            c = RECEIVED + 12 + q
+            moves = landed(jnp.where((ways & ORDERS[q][3]) != 0, 1, 0), j)
+            held = landed(bases[3][q], j)
+            comes = landed(place[:, c : c + 1], j)
+            part = turned(jnp.full_like(by, SHARES[q]), by)
+            rest = bits_set(part & below(k))
+            dealt = (part >> k) & 1
+            spot = begin_of(q, 3) + jnp.minimum(held + rest, region(3, q) - 1)
+            here += dealt * jnp.where(moves != 0, begin_of(4, 3), spot)
+            spot = LATE_BEGIN[q] + jnp.minimum(comes + rest, ROOM[3][q] - 1)
+            last += dealt * jnp.where(moves != 0, spot, -1)
+        early.append(jnp.where(k < live, here, begin_of(4, 3)))
+        late.append(jnp.where(k < live, last, -1))
+    rows = [length, jnp.broadcast_to(over, (1, 128)), jnp.zeros((6, 128), jnp.int32)]
+    land_ref[...] = jnp.concatenate(early + late + rows, axis=0)
 
 
 def plan_const():
@@ -288,25 +302,21 @@
     return pl.CostEstimate(flops=flops, bytes_accessed=bytes_accessed, transcendentals=0)
 
 
-def home_kernel(rows, table_ref, kv_ref, other_ref, *rest):
-    outs, space, sems = rest[:4], rest[4], rest[5]
-    pairs = [(ref, space.at[pl.ds(OWN_CHUNKS * k, OWN_CHUNKS)]) for k, ref in enumerate((kv_ref, other_ref))]
-    for copy in fetch(pairs, sems):
-        copy.wait()
+def home_kernel(rows, table_ref, kv_ref, other_ref, *outs):
+    def pick(i):
+        row = i & (OWN_CHUNKS - 1)
+        return jnp.where(i < OWN_CHUNKS, kv_ref[row], other_ref[row])
+
     for q in range(4):
-        gather_chunks(table_ref, rows + q, outs[q], lambda i: space[i])
+        gather_chunks(table_ref, rows + q, outs[q], pick)
 
 
 def home_lists(rows, rooms, table, kv, other):
     return pl.pallas_call(
         functools.partial(home_kernel, rows),
         out_shape=tuple(chunks_of(room) for room in rooms),
-        in_specs=[SMEM, ANY, ANY],
+        in_specs=[SMEM, VMEM, VMEM],
         out_specs=(VMEM,) * 4,
-        scratch_shapes=[
-            pltpu.VMEM((HOME, CHUNK, 256), jnp.bfloat16),
-            pltpu.SemaphoreType.DMA((2,)),
-        ],
         compiler_params=pltpu.CompilerParams(vmem_limit_bytes=24 * MIB),
         cost_estimate=cost(SMALL),
         name="home_lists",
@@ -321,27 +331,35 @@
     return pairs
 
 
-def next_kernel(phase, part, table_ref, *rest):
-    boxes, out_ref, space, sems = rest[: phase + 1], rest[phase + 1], rest[phase + 2], rest[phase + 3]
-    for copy in fetch(part_pairs(part, boxes, space), sems):
-        copy.wait()
-    gather_chunks(table_ref, 4 * phase + part, out_ref, lambda i: space[i])
-
-
-def next_list(phase, part, table, boxes):
+def next_kernel(phase, table_ref, *rest):
+    each = phase + 1
+    boxes, outs, space, sems = rest[: 4 * each], rest[4 * each : 4 * each + 4], rest[4 * each + 4], rest[4 * each + 5]
+    copies = []
+    for q in range(4):
+        pairs = part_pairs(q, boxes[each * q : each * q + each], space, begin_of(q, phase))
+        copies.append(fetch(pairs, sems.at[q]))
+    for q in range(4):
+        for copy in copies[q]:
+            copy.wait()
+        begin = begin_of(q, phase)
+        gather_chunks(table_ref, 4 * phase + q, outs[q], lambda i: space[begin + i])
+
+
+def next_lists(phase, table, boxes):
+    flat = [box for part in boxes for box in part]
     return pl.pallas_call(
-        functools.partial(next_kernel, phase, part),
-        out_shape=chunks_of(ROOM[phase][part]),
-        in_specs=[SMEM] + [ANY] * len(boxes),
-        out_specs=VMEM,
+        functools.partial(next_kernel, phase),
+        out_shape=tuple(chunks_of(room) for room in ROOM[phase]),
+        in_specs=[SMEM] + [ANY] * len(flat),
+        out_specs=(VMEM,) * 4,
         scratch_shapes=[
-            pltpu.VMEM((region(phase, part), CHUNK, 256), jnp.bfloat16),
-            pltpu.SemaphoreType.DMA((len(boxes),)),
+            pltpu.VMEM((begin_of(4, phase), CHUNK, 256), jnp.bfloat16),
+            pltpu.SemaphoreType.DMA((4, phase + 1)),
         ],
-        compiler_params=pltpu.CompilerParams(vmem_limit_bytes=16 * MIB),
+        compiler_params=pltpu.CompilerParams(vmem_limit_bytes=28 * MIB),
         cost_estimate=cost(SMALL),
-        name="next_list",
-    )(table, *boxes)
+        name="next_lists",
+    )(table, *flat)
 
 
 def attend_row(query, first, second, own, length):
@@ -368,14 +386,21 @@
     both = jnp.dot(weights.astype(jnp.bfloat16), values, preferred_element_type=jnp.float32)
     mixture = jnp.where(upper, both[:, :128], both[:, 128:])
     mixture += own_weight.astype(jnp.bfloat16).astype(jnp.float32) * own_value
-    return (mixture / denominator).astype(jnp.bfloat16)
+    return mixture / denominator
+
+
+def lay_rows(result, out_ref, first, rows):
+    for row in range(0, rows, 16):
+        for head in range(16):
+            values = result[pl.ds(16 * row + head, 16, stride=16)]
+            out_ref[first + row : first + row + 16, 128 * head : 128 * head + 128] = values.astype(jnp.bfloat16)
 
 
 TOGETHER = 4
 DEPTH = 4 * TOGETHER
 
 
-def running_kernel(first, half_ref, pages_ref, lens_ref, query_ref, own_ref, pool_ref, out_ref, held, sems):
+def running_kernel(first, half_ref, pages_ref, lens_ref, query_ref, own_ref, pool_ref, out_ref, held, result, sems):
     rows = out_ref.shape[0]
     all_rows = lens_ref.shape[0] // 2
     max_pages = held.shape[1]
@@ -411,21 +436,23 @@
                 attend_row(query_ref[first + row], *blocks, own_ref[first + row], lens_ref[start + row])
             )
         for r in range(TOGETHER):
-            out_ref[group * TOGETHER + r] = results[r]
+            result[pl.ds((group * TOGETHER + r) * 16, 16)] = results[r]
         return carry
 
     lax.fori_loop(0, rows // TOGETHER, body, 0)
+    lay_rows(result, out_ref, 0, rows)
 
 
 def running_rows(first, count, half, pages, lens, queries, own, pool):
     max_pages = pages.shape[-1]
     return pl.pallas_call(
         functools.partial(running_kernel, first),
-        out_shape=jax.ShapeDtypeStruct((count, 16, 128), jnp.bfloat16),
+        out_shape=jax.ShapeDtypeStruct((count, 2048), jnp.bfloat16),
         in_specs=[SMEM, SMEM, SMEM, VMEM, VMEM, pl.BlockSpec(memory_space=pltpu.HBM)],
         out_specs=VMEM,
         scratch_shapes=[
             pltpu.VMEM((DEPTH, max_pages) + pool.shape[1:], jnp.bfloat16),
+            pltpu.VMEM((count * 16, 128), jnp.float32),
             pltpu.SemaphoreType.DMA((DEPTH, max_pages)),
         ],
         compiler_params=pltpu.CompilerParams(vmem_limit_bytes=48 * MIB),
@@ -437,34 +464,94 @@
 RING = 4
 
 
-def land_kernel(given, land_ref, query_ref, own_ref, *rest):
+def early_kernel(land_ref, *rest):
+    boxes, (landed_ref, block, sems, space, box_sems) = rest[:16], rest[16:]
+    slots = landed_ref.shape[0]
+    pairs = []
+    for q in range(4):
+        pairs += part_pairs(q, boxes[4 * q : 4 * q + 4], space, begin_of(q, 3))
+    copies = fetch(pairs, box_sems)
+    space[begin_of(4, 3)] = jnp.zeros((CHUNK, 256), jnp.bfloat16)
+    for copy in copies:
+        copy.wait()
+
+    def write(slot):
+        turn = slot % RING
+        return pltpu.make_async_copy(block.at[turn], landed_ref.at[slot], sems.at[turn])
+
+    def body(slot, carry):
+        @pl.when(slot >= RING)
+        def _():
+            write(slot).wait()
+
+        for j in range(2):
+            for k in range(0, PROMPT_CHUNKS, 4):
+                held = [space[land_ref[PROMPT_CHUNKS * j + k + b, slot]] for b in range(4)]
+                for b in range(4):
+                    block[slot % RING, j, k + b] = held[b]
+        write(slot).start()
+        return carry
+
+    lax.fori_loop(0, slots, body, 0)
+    for slot in range(slots - RING, slots):
+        write(slot).wait()
+
+
+def early_rows(slots, land, boxes):
+    return pl.pallas_call(
+        early_kernel,
+        out_shape=jax.ShapeDtypeStruct((slots, 2, PROMPT_CHUNKS, CHUNK, 256), jnp.bfloat16),
+        in_specs=[SMEM] + [ANY] * 16,
+        out_specs=ANY,
+        scratch_shapes=[
+            pltpu.VMEM((RING, 2, PROMPT_CHUNKS, CHUNK, 256), jnp.bfloat16),
+            pltpu.SemaphoreType.DMA((RING,)),
+            pltpu.VMEM((begin_of(4, 3) + 1, CHUNK, 256), jnp.bfloat16),
+            pltpu.SemaphoreType.DMA((16,)),
+        ],
+        compiler_params=pltpu.CompilerParams(vmem_limit_bytes=28 * MIB),
+        cost_estimate=cost(SMALL),
+        name="early_rows",
+    )(land, *boxes)
+
+
+LAND_RING = 8
+
+
+def land_kernel(given, land_ref, query_ref, own_ref, early_ref, *rest):
     contexts, rest = rest[:given], rest[given:]
-    boxes, (out_ref, landed_ref, block, sems, space, box_sems) = rest[:20], rest[20:]
+    boxes, (out_ref, landed_ref, block, result, in_sems, sems, space, box_sems) = rest[:4], rest[4:]
     slots = landed_ref.shape[0]
     first = out_ref.shape[0] - slots
-    pairs = []
-    for q in range(4):
-        pairs += part_pairs(q, boxes[5 * q : 5 * q + 5], space, begin_of(q))
-    copies = fetch(pairs, box_sems)
+
+    def read(slot):
+        turn = slot % LAND_RING
+        return pltpu.make_async_copy(early_ref.at[slot], block.at[turn], in_sems.at[turn])
+
+    def write(slot):
+        turn = slot % LAND_RING
+        return pltpu.make_async_copy(block.at[turn], landed_ref.at[slot], sems.at[turn])
+
+    copies = fetch([(box, space.at[pl.ds(LATE_BEGIN[q], box.shape[0])]) for q, box in enumerate(boxes)], box_sems)
+    for slot in range(4):
+        read(slot).start()
     done = 0
     for context in contexts:
         out_ref[done : done + context.shape[0]] = context[...]
         done += context.shape[0]
-    space[begin_of(4)] = jnp.zeros((CHUNK, 256), jnp.bfloat16)
     for copy in copies:
         copy.wait()
 
-    def write(slot):
-        turn = slot % RING
-        return pltpu.make_async_copy(block.at[turn], landed_ref.at[slot], sems.at[turn])
-
-    def assemble(slot):
-        turn = slot % RING
+    def complete(slot):
+        turn = slot % LAND_RING
         length = land_ref[LENGTH, slot]
         for j in range(2):
-            for k in range(0, PROMPT_CHUNKS, 4):
-                held = [space[land_ref[PROMPT_CHUNKS * j + k + b, slot]] for b in range(4)]
-                for b in range(4):
+            for k in range(0, PROMPT_CHUNKS, 2):
+                held = []
+                for b in range(2):
+                    source = land_ref[LATE + PROMPT_CHUNKS * j + k + b, slot]
+                    held.append(jnp.where(source >= 0, space[jnp.maximum(source, 0)], block[turn, j, k + b]))
+                for b in range(2):
                     block[turn, j, k + b] = held[b]
         last = jnp.maximum(length - 1, 0) // CHUNK
         row = last * CHUNK + lax.broadcasted_iota(jnp.int32, (CHUNK, 256), 0)
@@ -475,49 +562,59 @@
     def body(pair, carry):
         both = (2 * pair, 2 * pair + 1)
 
-        @pl.when(2 * pair >= RING)
+        @pl.when(2 * pair + 4 < slots)
         def _():
             for slot in both:
-                write(slot).wait()
+
+                @pl.when(slot + 4 >= LAND_RING)
+                def _():
+                    write(slot + 4).wait()
+
+                read(slot + 4).start()
 
         for slot in both:
-            assemble(slot)
+            read(slot).wait()
+        for slot in both:
+            complete(slot)
         for slot in both:
             write(slot).start()
         results = []
         for slot in both:
-            blocks = [block[slot % RING, j].reshape(PROMPT_CHUNKS * CHUNK, 256) for j in range(2)]
+            blocks = [block[slot % LAND_RING, j].reshape(PROMPT_CHUNKS * CHUNK, 256) for j in range(2)]
             results.append(
                 attend_row(query_ref[first + slot], *blocks, own_ref[first + slot], land_ref[LENGTH, slot])
             )
-        for slot, result in zip(both, results):
-            out_ref[first + slot] = result
+        for slot, value in zip(both, results):
+            result[pl.ds(16 * slot, 16)] = value
         return carry
 
     lax.fori_loop(0, slots // 2, body, 0)
-    for slot in range(slots - RING, slots):
+    lay_rows(result, out_ref, first, slots)
+    for slot in range(slots - LAND_RING, slots):
         write(slot).wait()
 
 
-def land_rows(slots, land, queries, own, contexts, boxes):
+def land_rows(land, queries, own, early, contexts, boxes):
     return pl.pallas_call(
         functools.partial(land_kernel, len(contexts)),
         out_shape=(
-            jax.ShapeDtypeStruct(queries.shape, jnp.bfloat16),
-            jax.ShapeDtypeStruct((slots, 2, PROMPT_CHUNKS, CHUNK, 256), jnp.bfloat16),
+            jax.ShapeDtypeStruct((queries.shape[0], 2048), jnp.bfloat16),
+            jax.ShapeDtypeStruct(early.shape, jnp.bfloat16),
         ),
-        in_specs=[SMEM, VMEM, VMEM] + [VMEM] * len(contexts) + [ANY] * 20,
+        in_specs=[SMEM, VMEM, VMEM, ANY] + [VMEM] * len(contexts) + [ANY] * 4,
         out_specs=(VMEM, ANY),
         scratch_shapes=[
-            pltpu.VMEM((RING, 2, PROMPT_CHUNKS, CHUNK, 256), jnp.bfloat16),
-            pltpu.SemaphoreType.DMA((RING,)),
-            pltpu.VMEM((begin_of(4) + 1, CHUNK, 256), jnp.bfloat16),
-            pltpu.SemaphoreType.DMA((20,)),
+            pltpu.VMEM((LAND_RING,) + early.shape[1:], jnp.bfloat16),
+            pltpu.VMEM((16 * early.shape[0], 128), jnp.float32),
+            pltpu.SemaphoreType.DMA((LAND_RING,)),
+            pltpu.SemaphoreType.DMA((LAND_RING,)),
+            pltpu.VMEM((LATE_BEGIN[4], CHUNK, 256), jnp.bfloat16),
+            pltpu.SemaphoreType.DMA((4,)),
         ],
-        compiler_params=pltpu.CompilerParams(vmem_limit_bytes=32 * MIB),
+        compiler_params=pltpu.CompilerParams(vmem_limit_bytes=24 * MIB),
         cost_estimate=cost(SMALL),
         name="land_rows",
-    )(land, queries, own, *contexts, *boxes)
+    )(land, queries, own, early, *contexts, *boxes)
 
 
 def routed(operands, kv, other, half, pages, lens, queries, own, pool):
@@ -528,25 +625,24 @@
     sent = [hop(value, order[0]) for value, order in zip(lists, ORDERS)]
     (where, table), _ = lax.optimization_barrier(((operands[0], table), lists))
     kept = home_lists(4, KEPT, table, kv, other)
-    table, land = plan_call(plan_kernel, "plan", (16, 40), where, *operands[1:])
+    table, land = plan_call(plan_kernel, "plan", (16, 72), where, *operands[1:])
     boxes = [[k] for k in kept]
     contexts = []
-    count = running // 2
-    for phase in range(1, 4):
-        turns = sorted(range(4), key=lambda q: region(phase, q) - KEPT[q])
-        lists = [None] * 4
-        for q in turns:
-            boxes[q] = boxes[q] + [sent[q]]
-            lists[q] = next_list(phase, q, table, boxes[q])
-            table, _ = lax.optimization_barrier((table, lists[q]))
-        if phase > 1:
-            ready, _ = lax.optimization_barrier((half, lists))
-            context = running_rows(len(contexts) * count, count, ready, pages, lens, queries, own, pool)
-            contexts.append(context)
-            table, land, _ = lax.optimization_barrier((table, land, context))
+    done = 0
+    for phase, count in ((1, running // 4), (2, running // 2), (3, running // 4)):
+        boxes = [part + [box] for part, box in zip(boxes, sent)]
+        lists = next_lists(phase, table, boxes)
         sent = [hop(value, order[phase]) for value, order in zip(lists, ORDERS)]
-    boxes = [box for q in range(4) for box in boxes[q] + [sent[q]]]
-    context, landed = land_rows(rows - running, land, queries, own, contexts, boxes)
+        ready, _ = lax.optimization_barrier((half, lists))
+        contexts.append(running_rows(done, count, ready, pages, lens, queries, own, pool))
+        done += count
+        if phase == 3:
+            land, _ = lax.optimization_barrier((land, lists))
+            early = early_rows(rows - running, land, [box for part in boxes for box in part])
+            sent, _, early = lax.optimization_barrier((sent, contexts, early))
+        else:
+            table, _ = lax.optimization_barrier((table, contexts))
+    context, landed = land_rows(land, queries, own, early, contexts, sent)
     return context, landed, land[OVER, 0]
 
 
@@ -637,6 +733,7 @@
 
     def again(carry):
         handed, landed = any_fill(targets, prompt_lens, kv, by_head[running:], own[running:])
+        handed = handed.astype(jnp.bfloat16).reshape(rows - running, -1)
         return carry[0].at[running:].set(handed), landed, jnp.zeros((), jnp.int32)
 
     context, landed, _ = lax.while_loop(lambda carry: carry[2] > 0, again, (context, landed, over))

time: 138 us -> 131 us (0.949); the launches traced: 136 us -> 131 us
  Pallas kernels: 80.9 us -> 75.5 us
    pallas_call x12 -> x4, Pallas kernels: 25.1 us -> 18.5 us  [the longest x3 12.9 us: next_lists(): pl.pallas_call(functools.partial(next_kernel, phase), out_shape=tuple((ch...]
    pallas_call x2 -> x3, Pallas kernels: 27.3 us -> 31.2 us  [running_rows(): pl.pallas_call(functools.partial(running_kernel, first), out_shape=jax.Sh...]
    reshape x1 -> x0, local copies, waits for them, and re-layouts: 1.84 us -> none  [local(): context.reshape(1, 1, rows, queries.shape[3])]
    pallas_call x1, Pallas kernels: 11.8 us -> 10.2 us  [land_rows(): pl.pallas_call(functools.partial(land_kernel, len(contexts)), out_shape=(...]
    unnamed x58 -> x48, local copies, waits for them, and re-layouts: 3 us -> 4.45 us
  transfers between devices with their start and end apart: 17 -> 17, of which waited for: 6 -> 12; matrix products, arithmetic and copies ran while one was open for 3% -> 3% of each run, Pallas kernels for 47% -> 37%
where the time goes in v2:
time: 131 us
  Pallas kernels  75.5 us (58%)
  waiting for transfers between devices  28.9 us (22%)
  starting transfers between devices  17.8 us (14%)
  local copies, waits for them, and re-layouts  6.69 us (5%)
    pallas_call x3, Pallas kernels, running_rows(): pl.pallas_call(functools.partial(running_kernel, first), out_shape=jax.Sh...  31.2 us
    ppermute x13, waiting for transfers between devices, hop(): lax.ppermute(value, 'grp', [(g, flipped(g, axis)) for g in range(lax.axis...  24.2 us
    pallas_call x3, Pallas kernels, next_lists(): pl.pallas_call(functools.partial(next_kernel, phase), out_shape=tuple((ch...  12.9 us
    ppermute x13, starting transfers between devices, hop(): lax.ppermute(value, 'grp', [(g, flipped(g, axis)) for g in range(lax.axis...  12.9 us
    pallas_call x1, Pallas kernels, land_rows(): pl.pallas_call(functools.partial(land_kernel, len(contexts)), out_shape=(...  10.2 us
    pallas_call x2, Pallas kernels, plan_call(): pl.pallas_call(kernel, out_shape=tuple((jax.ShapeDtypeStruct((r, 128), jn...  8.36 us
    pallas_call x2, Pallas kernels, home_lists(): pl.pallas_call(functools.partial(home_kernel, rows), out_shape=tuple((chu...  7.27 us
    pallas_call x1, Pallas kernels, early_rows(): pl.pallas_call(early_kernel, out_shape=jax.ShapeDtypeStruct((slots, 2, PR...  5.57 us
  transfers between devices with their start and end apart: 17, of which 12 were waited for; matrix products, arithmetic and copies ran while one was open for 3% of the time, Pallas kernels for 37%

profile of v2, /device:TPU:16, one launch (start us, length us, event | category | flops | bytes accessed | tf_op | source)
XLA Modules:
  0.0 130.7 jit_solution(11936215991518340104)
XLA Ops:
  0.9 0.7 copy-done.10
  1.6 1.8 %first_plan.1.table_ref = s32[8,128]{1,0:T(8,128)S(1)} custom-call(s32[3]{0:T(128)S(1)} %pad_add_fusion.where_ref, s32[1,256]{1,0:T(1,128)} %bitcast.504, s32[1,256]{1,0:T(1,128)} %bitcast.508, s32[8,64]{1,0:T(8,128)S(1)} %copy-done.10), custom_call_target="tpu_custom_call" | custom-call | bytes 4096 | tf_op jit(solution)/shard_map/first_plan/pallas_call | solution.py:254
  3.4 4.9 %collective-permute-done.1.other_ref = bf16[256,32,256]{2,1,0:T(8,128)(2,1)} collective-permute-done((bf16[256,32,256]{2,1,0:T(8,128)(2,1)}, bf16[256,32,256]{2,1,0:T(8,128)(2,1)}, u32[]{:S(2)}, u32[]{:S(2)}) %collective-permute-start.1) | collective-permute-done | bytes 4194336 | tf_op jit(solution)/shard_map/ppermute | solution.py:55
  8.2 4.2 %home_lists.2 = (bf16[40,32,256]{2,1,0:T(8,128)(2,1)S(1)}, bf16[40,32,256]{2,1,0:T(8,128)(2,1)S(1)}, bf16[48,32,256]{2,1,0:T(8,128)(2,1)S(1)}, bf16[36,32,256]{2,1,0:T(8,128)(2,1)S(1)}) custom-call(s32[8,128]{1,0:T(8,128)S(1)} %first_plan.1.table_ref, bf16[256,32,256]{2,1,0:T(8,128)(2,1)} %bitcast.470, bf16[256,32,256]{2,1,0:T(8,128)(2,1)} %collective-permute-done.1.other_ref), custom_call_target="tpu_custom_call" | custom-call | bytes 4096 | tf_op jit(solution)/shard_map/home_lists/pallas_call | solution.py:315
  12.4 0.5 collective-permute-start.4
  13.0 1.5 %collective-permute-start.2 = (bf16[40,32,256]{2,1,0:T(8,128)(2,1)S(1)}, bf16[40,32,256]{2,1,0:T(8,128)(2,1)S(1)}, u32[]{:S(2)}, u32[]{:S(2)}) collective-permute-start(bf16[40,32,256]{2,1,0:T(8,128)(2,1)S(1)} %get-tuple-element.92), channel_id=1, source_target_pairs={{0,16},{8,24},{16,0},{24,8},{32,48},{40,56},{48,32},{56,40},{64,80... | collective-permute-start | bytes 1966088 | tf_op jit(solution)/shard_map/ppermute | solution.py:55
  14.5 1.1 collective-permute-start.3
  15.5 1.9 %collective-permute-start.5 = (bf16[36,32,256]{2,1,0:T(8,128)(2,1)S(1)}, bf16[36,32,256]{2,1,0:T(8,128)(2,1)S(1)}, u32[]{:S(2)}, u32[]{:S(2)}) collective-permute-start(bf16[36,32,256]{2,1,0:T(8,128)(2,1)S(1)} %get-tuple-element.95), channel_id=1, source_target_pairs={{0,1},{1,0},{2,3},{3,2},{4,5},{5,4},{6,7},{7,6},{8,9},{9,8},{10,11... | collective-permute-start | bytes 1769480 | tf_op jit(solution)/shard_map/ppermute | solution.py:54
  17.4 6.5 %plan.1 = (s32[16,128]{1,0:T(8,128)S(1)}, s32[72,128]{1,0:T(8,128)S(1)}) custom-call(s32[3]{0:T(128)S(1)} %pad_add_fusion.where_ref, s32[1,256]{1,0:T(1,128)S(1)} %bitcast.505, s32[1,256]{1,0:T(1,128)S(1)} %bitcast.509, s32[8,64]{1,0:T(8,128)S(1)} %copy-done.11), custom_call_target="tpu_custom_call" | custom-call | bytes 4096 | tf_op jit(solution)/shard_map/plan/pallas_call | solution.py:254
  24.0 0.6 copy-done.8
  24.6 3.1 %home_lists.3 = (bf16[52,32,256]{2,1,0:T(8,128)(2,1)S(1)}, bf16[52,32,256]{2,1,0:T(8,128)(2,1)S(1)}, bf16[64,32,256]{2,1,0:T(8,128)(2,1)S(1)}, bf16[40,32,256]{2,1,0:T(8,128)(2,1)S(1)}) custom-call(s32[8,128]{1,0:T(8,128)S(1)} %first_plan.1.table_ref, bf16[256,32,256]{2,1,0:T(8,128)(2,1)S(1)} %bitcast.471, bf16[256,32,256]{2,1,0:T(8,128)(2,1)} %collective-permute-done.1.other_ref), custom_call_target="tpu_custom_call" | custom-call | bytes 4096 | tf_op jit(solution)/shard_map/home_lists/pallas_call | solution.py:315
  27.7 2.6 %collective-permute-done.5.rest_7_.rest_10_.rest_13_ = bf16[36,32,256]{2,1,0:T(8,128)(2,1)S(1)} collective-permute-done((bf16[36,32,256]{2,1,0:T(8,128)(2,1)S(1)}, bf16[36,32,256]{2,1,0:T(8,128)(2,1)S(1)}, u32[]{:S(2)}, u32[]{:S(2)}) %collective-permute-start.5) | collective-permute-done | bytes 589856 | tf_op jit(solution)/shard_map/ppermute | solution.py:54
  30.4 0.3 collective-permute-done.3.rest_3_.rest_4_.rest_5_
  30.7 1.4 %collective-permute-done.4.rest_5_.rest_7_.rest_9_ = bf16[48,32,256]{2,1,0:T(8,128)(2,1)S(1)} collective-permute-done((bf16[48,32,256]{2,1,0:T(8,128)(2,1)S(1)}, bf16[48,32,256]{2,1,0:T(8,128)(2,1)S(1)}, u32[]{:S(2)}, u32[]{:S(2)}) %collective-permute-start.4) | collective-permute-done | bytes 786464 | tf_op jit(solution)/shard_map/ppermute | solution.py:55
  32.1 4.1 %next_lists.3 = (bf16[48,32,256]{2,1,0:T(8,128)(2,1)}, bf16[44,32,256]{2,1,0:T(8,128)(2,1)}, bf16[48,32,256]{2,1,0:T(8,128)(2,1)}, bf16[48,32,256]{2,1,0:T(8,128)(2,1)}) custom-call(s32[16,128]{1,0:T(8,128)S(1)} %get-tuple-element.115.table_ref, bf16[52,32,256]{2,1,0:T(8,128)(2,1)S(1)} %get-tuple-element.100.rest_0_, ...), custom_call_target="tpu_custom_call" | custom-call | bytes 4096 | tf_op jit(solution)/shard_map/next_lists/pallas_call | solution.py:350
  36.2 0.8 copy-done
  37.1 1.9 %collective-permute-start.6 = (bf16[48,32,256]{2,1,0:T(8,128)(2,1)}, bf16[48,32,256]{2,1,0:T(8,128)(2,1)}, u32[]{:S(2)}, u32[]{:S(2)}) collective-permute-start(bf16[48,32,256]{2,1,0:T(8,128)(2,1)} %get-tuple-element.104), channel_id=1, source_target_pairs={{0,1},{1,0},{2,3},{3,2},{4,5},{5,4},{6,7},{7,6},{8,9},{9,8},{10,11... | collective-permute-start | bytes 2359304 | tf_op jit(solution)/shard_map/ppermute | solution.py:54
  39.0 2.5 %collective-permute-start.8 = (bf16[48,32,256]{2,1,0:T(8,128)(2,1)}, bf16[48,32,256]{2,1,0:T(8,128)(2,1)}, u32[]{:S(2)}, u32[]{:S(2)}) collective-permute-start(bf16[48,32,256]{2,1,0:T(8,128)(2,1)} %get-tuple-element.106), channel_id=1, source_target_pairs={{0,32},{8,40},{16,48},{24,56},{32,0},{40,8},{48,16},{56,24},{64,96... | collective-permute-start | bytes 2359304 | tf_op jit(solution)/shard_map/ppermute | solution.py:55
  41.5 1.5 %collective-permute-start.9 = (bf16[48,32,256]{2,1,0:T(8,128)(2,1)}, bf16[48,32,256]{2,1,0:T(8,128)(2,1)}, u32[]{:S(2)}, u32[]{:S(2)}) collective-permute-start(bf16[48,32,256]{2,1,0:T(8,128)(2,1)} %get-tuple-element.107), channel_id=1, source_target_pairs={{0,16},{8,24},{16,0},{24,8},{32,48},{40,56},{48,32},{56,40},{64,80... | collective-permute-start | bytes 2359304 | tf_op jit(solution)/shard_map/ppermute | solution.py:55
  43.0 0.8 copy.52
  43.8 0.7 copy.35
  44.5 1.0 reshape_squeeze.4.pages_ref
  45.5 0.8 reshape_squeeze.5.lens_ref
  46.2 8.7 %running_rows.3.rest_0_ = bf16[16,2048]{1,0:T(8,128)(2,1)S(1)} custom-call(s32[1]{0:T(128)} %bitcast.180.half_ref, s32[768]{0:T(1024)S(1)} %reshape_squeeze.4.pages_ref, s32[128]{0:T(128)S(1)} %reshape_squeeze.5.lens_ref, bf16[80,16,128]{2,1,0:T(8,128)(2,1)} %bitcast.475, bf16[80,2,256]{2,1,0:T(2,128)(2,1)} %bitcast.483, bf16[224,2,64,256]{3,2,1,0:T(8,128)(2,1)} %bitcast.472), custom_call_target="tpu_custom_call" | custom-call | bytes 4096 | tf_op jit(solution)/shard_map/running_rows/pallas_call | solution.py:448
  55.0 4.8 %collective-permute-done.7.rest_5_.rest_6_ = bf16[44,32,256]{2,1,0:T(8,128)(2,1)} collective-permute-done((bf16[44,32,256]{2,1,0:T(8,128)(2,1)}, bf16[44,32,256]{2,1,0:T(8,128)(2,1)}, u32[]{:S(2)}, u32[]{:S(2)}) %collective-permute-start.7) | collective-permute-done | bytes 720928 | tf_op jit(solution)/shard_map/ppermute | solution.py:55
  59.8 0.2 collective-permute-done.9.rest_11_.rest_14_
  60.0 3.3 %next_lists.4 = (bf16[64,32,256]{2,1,0:T(8,128)(2,1)S(1)}, bf16[52,32,256]{2,1,0:T(8,128)(2,1)S(1)}, bf16[48,32,256]{2,1,0:T(8,128)(2,1)S(1)}, bf16[52,32,256]{2,1,0:T(8,128)(2,1)S(1)}) custom-call(s32[16,128]{1,0:T(8,128)S(1)} %get-tuple-element.115.table_ref, bf16[52,32,256]{2,1,0:T(8,128)(2,1)S(1)} %get-tuple-element.100.rest_0_, ...), custom_call_target="tpu_custom_call" | custom-call | bytes 4096 | tf_op jit(solution)/shard_map/next_lists/pallas_call | solution.py:350
  63.4 0.2 collective-permute-start.10
  63.6 0.4 collective-permute-start.11
  63.9 1.7 %collective-permute-start.13 = (bf16[52,32,256]{2,1,0:T(8,128)(2,1)S(1)}, bf16[52,32,256]{2,1,0:T(8,128)(2,1)S(1)}, u32[]{:S(2)}, u32[]{:S(2)}) collective-permute-start(bf16[52,32,256]{2,1,0:T(8,128)(2,1)S(1)} %get-tuple-element.113), channel_id=1, source_target_pairs={{0,32},{8,40},{16,48},{24,56},{32,0},{40,8},{48,16},{56,24},{64,96... | collective-permute-start | bytes 2555912 | tf_op jit(solution)/shard_map/ppermute | solution.py:55
  65.6 0.5 collective-permute-start.12
  66.1 14.0 %running_rows.4.rest_1_ = bf16[32,2048]{1,0:T(8,128)(2,1)S(1)} custom-call(s32[1]{0:T(128)} %bitcast.180.half_ref, s32[768]{0:T(1024)S(1)} %reshape_squeeze.4.pages_ref, s32[128]{0:T(128)S(1)} %reshape_squeeze.5.lens_ref, bf16[80,16,128]{2,1,0:T(8,128)(2,1)} %bitcast.476, bf16[80,2,256]{2,1,0:T(2,128)(2,1)S(1)} %bitcast.486, bf16[224,2,64,256]{3,2,1,0:T(8,128)(2,1)} %bitcast.473), custom_call_target="tpu_custom_call" | custom-call | bytes 4096 | tf_op jit(solution)/shard_map/running_rows/pallas_call | solution.py:448
  80.1 2.2 %collective-permute-done.12.rest_11_ = bf16[48,32,256]{2,1,0:T(8,128)(2,1)S(1)} collective-permute-done((bf16[48,32,256]{2,1,0:T(8,128)(2,1)S(1)}, bf16[48,32,256]{2,1,0:T(8,128)(2,1)S(1)}, u32[]{:S(2)}, u32[]{:S(2)}) %collective-permute-start.12) | collective-permute-done | bytes 786464 | tf_op jit(solution)/shard_map/ppermute | solution.py:55
  82.3 0.2 collective-permute-done.13.rest_15_
  82.6 3.8 %collective-permute-done.10.rest_3_ = bf16[64,32,256]{2,1,0:T(8,128)(2,1)S(1)} collective-permute-done((bf16[64,32,256]{2,1,0:T(8,128)(2,1)S(1)}, bf16[64,32,256]{2,1,0:T(8,128)(2,1)S(1)}, u32[]{:S(2)}, u32[]{:S(2)}) %collective-permute-start.10) | collective-permute-done | bytes 1048608 | tf_op jit(solution)/shard_map/ppermute | solution.py:55
  86.3 5.5 %next_lists.5 = (bf16[72,32,256]{2,1,0:T(8,128)(2,1)}, bf16[72,32,256]{2,1,0:T(8,128)(2,1)S(1)}, bf16[68,32,256]{2,1,0:T(8,128)(2,1)}, bf16[60,32,256]{2,1,0:T(8,128)(2,1)}) custom-call(s32[16,128]{1,0:T(8,128)S(1)} %get-tuple-element.115.table_ref, bf16[52,32,256]{2,1,0:T(8,128)(2,1)S(1)} %get-tuple-element.100.rest_0_, bf16[40,32,256]{2,1,0:T(8,128)(2,1)S(1)} %copy-done.1, ...), custom_call_target="tpu_custom_call" | custom-call | bytes 4096 | tf_op jit(solution)/shard_map/next_lists/pallas_call | solution.py:350
  91.8 2.6 %collective-permute-start.14 = (bf16[72,32,256]{2,1,0:T(8,128)(2,1)}, bf16[72,32,256]{2,1,0:T(8,128)(2,1)S(1)}, u32[]{:S(2)}, u32[]{:S(2)}) collective-permute-start(bf16[72,32,256]{2,1,0:T(8,128)(2,1)} %get-tuple-element.116), channel_id=1, source_target_pairs={{0,32},{8,40},{16,48},{24,56},{32,0},{40,8},{48,16},{56,24},{64,96... | collective-permute-start | bytes 3538952 | tf_op jit(solution)/shard_map/ppermute | solution.py:55
  94.4 0.7 collective-permute-start.15
  95.2 0.7 collective-permute-start.16
  95.9 8.5 %running_rows.5.rest_2_ = bf16[16,2048]{1,0:T(8,128)(2,1)S(1)} custom-call(s32[1]{0:T(128)} %bitcast.180.half_ref, s32[768]{0:T(1024)S(1)} %reshape_squeeze.4.pages_ref, s32[128]{0:T(128)S(1)} %reshape_squeeze.5.lens_ref, bf16[80,16,128]{2,1,0:T(8,128)(2,1)} %bitcast.477, bf16[80,2,256]{2,1,0:T(2,128)(2,1)} %bitcast.484, bf16[224,2,64,256]{3,2,1,0:T(8,128)(2,1)} %bitcast.474), custom_call_target="tpu_custom_call" | custom-call | bytes 4096 | tf_op jit(solution)/shard_map/running_rows/pallas_call | solution.py:448
  104.4 0.5 slice.780
  104.9 5.6 %early_rows.1.early_ref = bf16[16,2,16,32,256]{4,3,2,1,0:T(8,128)(2,1)S(1)} custom-call(s32[72,128]{1,0:T(8,128)S(1)} %copy-done.9, bf16[52,32,256]{2,1,0:T(8,128)(2,1)S(1)} %get-tuple-element.100.rest_0_, bf16[40,32,256]{2,1,0:T(8,128)(2,1)S(1)} %copy-done.1, bf16[48,32,256]{2,1,0:T(8,128)(2,1)} %collective-permute-done.6.rest_2_, ...), custom_call_target="tpu_custom_call" | custom-call | bytes 4096 | tf_op jit(solution)/shard_map/early_rows/pallas_call | solution.py:501
  110.5 5.8 %collective-permute-done.17.rest_6_ = bf16[60,32,256]{2,1,0:T(8,128)(2,1)S(1)} collective-permute-done((bf16[60,32,256]{2,1,0:T(8,128)(2,1)}, bf16[60,32,256]{2,1,0:T(8,128)(2,1)S(1)}, u32[]{:S(2)}, u32[]{:S(2)}) %collective-permute-start.17) | collective-permute-done | bytes 983072 | tf_op jit(solution)/shard_map/ppermute | solution.py:55
  116.3 2.1 %collective-permute-done.16.rest_5_ = bf16[68,32,256]{2,1,0:T(8,128)(2,1)S(1)} collective-permute-done((bf16[68,32,256]{2,1,0:T(8,128)(2,1)}, bf16[68,32,256]{2,1,0:T(8,128)(2,1)S(1)}, u32[]{:S(2)}, u32[]{:S(2)}) %collective-permute-start.16) | collective-permute-done | bytes 1114144 | tf_op jit(solution)/shard_map/ppermute | solution.py:54
  118.4 0.6 collective-permute-done.15.rest_4_
  118.9 10.2 %land_rows.1 = (bf16[80,2048]{1,0:T(8,128)(2,1)S(1)}, bf16[16,2,16,32,256]{4,3,2,1,0:T(8,128)(2,1)}) custom-call(s32[72,128]{1,0:T(8,128)S(1)} %copy-done.9, bf16[80,16,128]{2,1,0:T(8,128)(2,1)S(1)} %bitcast.479, bf16[80,2,256]{2,1,0:T(2,128)(2,1)S(1)} %bitcast.487, bf16[16,2,16,32,256]{4,3,2,1,0:T(8,128)(2,1)S(1)} %early_rows.1.early_ref, ...), custom_call_target="tpu_custom_call" | custom-call | bytes 4096 | tf_op jit(solution)/shard_map/land_rows/pallas_call | solution.py:598
  129.1 0.8 while.12
  129.9 0.7 copy-done.22
  (51 shorter events, 0.3 us)
Async XLA Ops:
  0.6 16.8 %copy-start.11 = (s32[8,64]{1,0:T(8,128)S(1)}, s32[8,64]{1,0:T(8,128)}, u32[]{:S(2)}) copy-start(s32[8,64]{1,0:T(8,128)} %constant.173.clone.const_ref) | copy-start | bytes 6148
  0.6 16.8 %copy-start.16 = (s32[256]{0:T(256)S(1)}, s32[256]{0:T(256)}, u32[]{:S(2)}) copy-start(s32[256]{0:T(256)} %param.13) | copy-start | bytes 3076
  0.7 16.8 %copy-start.19 = (s32[256]{0:T(256)S(1)}, s32[256]{0:T(256)}, u32[]{:S(2)}) copy-start(s32[256]{0:T(256)} %param.14) | copy-start | bytes 3076
  0.7 7.6 %collective-permute-start.1 = (bf16[256,32,256]{2,1,0:T(8,128)(2,1)}, bf16[256,32,256]{2,1,0:T(8,128)(2,1)}, u32[]{:S(2)}, u32[]{:S(2)}) collective-permute-start(bf16[256,32,256]{2,1,0:T(8,128)(2,1)} %bitcast.469), channel_id=1, source_target_pairs={{0,8},{8,0},{16,24},{24,16},{32,40},{40,32},{48,56},{56,48},{64,72... | collective-permute-start | bytes 12582920 | tf_op jit(solution)/shard_map/ppermute | solution.py:55
  0.9 0.7 copy-start.10
  1.5 23.0 %copy-start.12 = (bf16[16,1,512,256]{3,2,1,0:T(8,128)(2,1)S(1)}, bf16[16,1,512,256]{3,2,1,0:T(8,128)(2,1)}, u32[]{:S(2)}) copy-start(bf16[16,1,512,256]{3,2,1,0:T(8,128)(2,1)} %param.15) | copy-start | bytes 12582916
  12.4 30.6 %copy-start.18 = (bf16[1,1,80,2048]{3,2,1,0:T(8,128)(2,1)S(1)}, bf16[1,1,80,2048]{3,2,1,0:T(8,128)(2,1)}, u32[]{:S(2)}) copy-start(bf16[1,1,80,2048]{3,2,1,0:T(8,128)(2,1)} %param.19) | copy-start | bytes 983044
  12.4 31.3 %copy-start.21 = (s32[1,2,64,6]{2,1,3,0:T(2,128)S(1)}, s32[1,2,64,6]{2,1,3,0:T(2,128)}, u32[]{:S(2)}) copy-start(s32[1,2,64,6]{2,1,3,0:T(2,128)} %param.17) | copy-start | bytes 9220
  12.4 19.7 %collective-permute-start.4 = (bf16[48,32,256]{2,1,0:T(8,128)(2,1)S(1)}, bf16[48,32,256]{2,1,0:T(8,128)(2,1)S(1)}, u32[]{:S(2)}, u32[]{:S(2)}) collective-permute-start(bf16[48,32,256]{2,1,0:T(8,128)(2,1)S(1)} %get-tuple-element.94), channel_id=1, source_target_pairs={{0,96},{8,104},{16,112},{24,120},{32,64},{40,72},{48,80},{56,88},{... | collective-permute-start | bytes 2359304 | tf_op jit(solution)/shard_map/ppermute | solution.py:55
  13.0 17.4 %collective-permute-start.2 = (bf16[40,32,256]{2,1,0:T(8,128)(2,1)S(1)}, bf16[40,32,256]{2,1,0:T(8,128)(2,1)S(1)}, u32[]{:S(2)}, u32[]{:S(2)}) collective-permute-start(bf16[40,32,256]{2,1,0:T(8,128)(2,1)S(1)} %get-tuple-element.92), channel_id=1, source_target_pairs={{0,16},{8,24},{16,0},{24,8},{32,48},{40,56},{48,32},{56,40},{64,80... | collective-permute-start | bytes 1966088 | tf_op jit(solution)/shard_map/ppermute | solution.py:55
  14.5 16.2 %collective-permute-start.3 = (bf16[40,32,256]{2,1,0:T(8,128)(2,1)S(1)}, bf16[40,32,256]{2,1,0:T(8,128)(2,1)S(1)}, u32[]{:S(2)}, u32[]{:S(2)}) collective-permute-start(bf16[40,32,256]{2,1,0:T(8,128)(2,1)S(1)} %get-tuple-element.93), channel_id=1, source_target_pairs={{0,32},{8,40},{16,48},{24,56},{32,0},{40,8},{48,16},{56,24},{64,96... | collective-permute-start | bytes 1966088 | tf_op jit(solution)/shard_map/ppermute | solution.py:55
  15.5 14.9 %collective-permute-start.5 = (bf16[36,32,256]{2,1,0:T(8,128)(2,1)S(1)}, bf16[36,32,256]{2,1,0:T(8,128)(2,1)S(1)}, u32[]{:S(2)}, u32[]{:S(2)}) collective-permute-start(bf16[36,32,256]{2,1,0:T(8,128)(2,1)S(1)} %get-tuple-element.95), channel_id=1, source_target_pairs={{0,1},{1,0},{2,3},{3,2},{4,5},{5,4},{6,7},{7,6},{8,9},{9,8},{10,11... | collective-permute-start | bytes 1769480 | tf_op jit(solution)/shard_map/ppermute | solution.py:54
  24.0 0.6 copy-start.8
  27.7 9.4 %copy-start.4 = (bf16[40,32,256]{2,1,0:T(8,128)(2,1)}, bf16[40,32,256]{2,1,0:T(8,128)(2,1)S(1)}, u32[]{:S(2)}) copy-start(bf16[40,32,256]{2,1,0:T(8,128)(2,1)S(1)} %get-tuple-element.103.rest_6_.rest_9_.rest_12_) | copy-start | bytes 1966084
  30.4 8.6 %copy-start.6 = (bf16[36,32,256]{2,1,0:T(8,128)(2,1)}, bf16[36,32,256]{2,1,0:T(8,128)(2,1)S(1)}, u32[]{:S(2)}) copy-start(bf16[36,32,256]{2,1,0:T(8,128)(2,1)S(1)} %collective-permute-done.5.rest_7_.rest_10_.rest_13_) | copy-start | bytes 1769476
  30.7 5.5 %copy-start.2 = (bf16[40,32,256]{2,1,0:T(8,128)(2,1)}, bf16[40,32,256]{2,1,0:T(8,128)(2,1)S(1)}, u32[]{:S(2)}) copy-start(bf16[40,32,256]{2,1,0:T(8,128)(2,1)S(1)} %collective-permute-done.3.rest_3_.rest_4_.rest_5_) | copy-start | bytes 1966084
  36.2 0.8 copy-start
  37.1 22.7 %collective-permute-start.6 = (bf16[48,32,256]{2,1,0:T(8,128)(2,1)}, bf16[48,32,256]{2,1,0:T(8,128)(2,1)}, u32[]{:S(2)}, u32[]{:S(2)}) collective-permute-start(bf16[48,32,256]{2,1,0:T(8,128)(2,1)} %get-tuple-element.104), channel_id=1, source_target_pairs={{0,1},{1,0},{2,3},{3,2},{4,5},{5,4},{6,7},{7,6},{8,9},{9,8},{10,11... | collective-permute-start | bytes 2359304 | tf_op jit(solution)/shard_map/ppermute | solution.py:54
  39.0 20.8 %collective-permute-start.8 = (bf16[48,32,256]{2,1,0:T(8,128)(2,1)}, bf16[48,32,256]{2,1,0:T(8,128)(2,1)}, u32[]{:S(2)}, u32[]{:S(2)}) collective-permute-start(bf16[48,32,256]{2,1,0:T(8,128)(2,1)} %get-tuple-element.106), channel_id=1, source_target_pairs={{0,32},{8,40},{16,48},{24,56},{32,0},{40,8},{48,16},{56,24},{64,96... | collective-permute-start | bytes 2359304 | tf_op jit(solution)/shard_map/ppermute | solution.py:55
  41.5 18.5 %collective-permute-start.9 = (bf16[48,32,256]{2,1,0:T(8,128)(2,1)}, bf16[48,32,256]{2,1,0:T(8,128)(2,1)}, u32[]{:S(2)}, u32[]{:S(2)}) collective-permute-start(bf16[48,32,256]{2,1,0:T(8,128)(2,1)} %get-tuple-element.107), channel_id=1, source_target_pairs={{0,16},{8,24},{16,0},{24,8},{32,48},{40,56},{48,32},{56,40},{64,80... | collective-permute-start | bytes 2359304 | tf_op jit(solution)/shard_map/ppermute | solution.py:55
  43.0 16.8 %collective-permute-start.7 = (bf16[44,32,256]{2,1,0:T(8,128)(2,1)}, bf16[44,32,256]{2,1,0:T(8,128)(2,1)}, u32[]{:S(2)}, u32[]{:S(2)}) collective-permute-start(bf16[44,32,256]{2,1,0:T(8,128)(2,1)} %get-tuple-element.105), channel_id=1, source_target_pairs={{0,96},{8,104},{16,112},{24,120},{32,64},{40,72},{48,80},{56,88},{... | collective-permute-start | bytes 2162696 | tf_op jit(solution)/shard_map/ppermute | solution.py:55
  46.2 13.8 %copy-start.1 = (bf16[40,32,256]{2,1,0:T(8,128)(2,1)S(1)}, bf16[40,32,256]{2,1,0:T(8,128)(2,1)}, u32[]{:S(2)}) copy-start(bf16[40,32,256]{2,1,0:T(8,128)(2,1)} %copy-done) | copy-start | bytes 1966084
  46.2 13.8 %copy-start.3 = (bf16[40,32,256]{2,1,0:T(8,128)(2,1)S(1)}, bf16[40,32,256]{2,1,0:T(8,128)(2,1)}, u32[]{:S(2)}) copy-start(bf16[40,32,256]{2,1,0:T(8,128)(2,1)} %copy-done.2) | copy-start | bytes 1966084
  46.2 13.8 %copy-start.5 = (bf16[40,32,256]{2,1,0:T(8,128)(2,1)S(1)}, bf16[40,32,256]{2,1,0:T(8,128)(2,1)}, u32[]{:S(2)}) copy-start(bf16[40,32,256]{2,1,0:T(8,128)(2,1)} %copy-done.4) | copy-start | bytes 1966084
  46.2 13.8 %copy-start.7 = (bf16[36,32,256]{2,1,0:T(8,128)(2,1)S(1)}, bf16[36,32,256]{2,1,0:T(8,128)(2,1)}, u32[]{:S(2)}) copy-start(bf16[36,32,256]{2,1,0:T(8,128)(2,1)} %copy-done.6) | copy-start | bytes 1769476
  46.2 19.9 %copy-start.14 = (bf16[1,1,80,2,256]{4,3,2,1,0:T(2,128)(2,1)S(1)}, bf16[1,1,80,2,256]{4,3,2,1,0:T(2,128)(2,1)}, u32[]{:S(2)}) copy-start(bf16[1,1,80,2,256]{4,3,2,1,0:T(2,128)(2,1)} %param.20) | copy-start | bytes 245764
  63.4 23.0 %collective-permute-start.10 = (bf16[64,32,256]{2,1,0:T(8,128)(2,1)S(1)}, bf16[64,32,256]{2,1,0:T(8,128)(2,1)S(1)}, u32[]{:S(2)}, u32[]{:S(2)}) collective-permute-start(bf16[64,32,256]{2,1,0:T(8,128)(2,1)S(1)} %get-tuple-element.110), channel_id=1, source_target_pairs={{0,96},{8,104},{16,112},{24,120},{32,64},{40,72},{48,80},{56,88},{... | collective-permute-start | bytes 3145736 | tf_op jit(solution)/shard_map/ppermute | solution.py:55
  63.6 18.8 %collective-permute-start.11 = (bf16[52,32,256]{2,1,0:T(8,128)(2,1)S(1)}, bf16[52,32,256]{2,1,0:T(8,128)(2,1)S(1)}, u32[]{:S(2)}, u32[]{:S(2)}) collective-permute-start(bf16[52,32,256]{2,1,0:T(8,128)(2,1)S(1)} %get-tuple-element.111), channel_id=1, source_target_pairs={{0,1},{1,0},{2,3},{3,2},{4,5},{5,4},{6,7},{7,6},{8,9},{9,8},{10,11... | collective-permute-start | bytes 2555912 | tf_op jit(solution)/shard_map/ppermute | solution.py:54
  63.9 18.6 %collective-permute-start.13 = (bf16[52,32,256]{2,1,0:T(8,128)(2,1)S(1)}, bf16[52,32,256]{2,1,0:T(8,128)(2,1)S(1)}, u32[]{:S(2)}, u32[]{:S(2)}) collective-permute-start(bf16[52,32,256]{2,1,0:T(8,128)(2,1)S(1)} %get-tuple-element.113), channel_id=1, source_target_pairs={{0,32},{8,40},{16,48},{24,56},{32,0},{40,8},{48,16},{56,24},{64,96... | collective-permute-start | bytes 2555912 | tf_op jit(solution)/shard_map/ppermute | solution.py:55
  65.6 16.7 %collective-permute-start.12 = (bf16[48,32,256]{2,1,0:T(8,128)(2,1)S(1)}, bf16[48,32,256]{2,1,0:T(8,128)(2,1)S(1)}, u32[]{:S(2)}, u32[]{:S(2)}) collective-permute-start(bf16[48,32,256]{2,1,0:T(8,128)(2,1)S(1)} %get-tuple-element.112), channel_id=1, source_target_pairs={{0,16},{8,24},{16,0},{24,8},{32,48},{40,56},{48,32},{56,40},{64,80... | collective-permute-start | bytes 2359304 | tf_op jit(solution)/shard_map/ppermute | solution.py:55
  91.8 12.6 %copy-start.9 = (s32[72,128]{1,0:T(8,128)S(1)}, s32[72,128]{1,0:T(8,128)}, u32[]{:S(2)}) copy-start(s32[72,128]{1,0:T(8,128)} %copy-done.8) | copy-start | bytes 110596
  91.8 26.6 %collective-permute-start.14 = (bf16[72,32,256]{2,1,0:T(8,128)(2,1)}, bf16[72,32,256]{2,1,0:T(8,128)(2,1)S(1)}, u32[]{:S(2)}, u32[]{:S(2)}) collective-permute-start(bf16[72,32,256]{2,1,0:T(8,128)(2,1)} %get-tuple-element.116), channel_id=1, source_target_pairs={{0,32},{8,40},{16,48},{24,56},{32,0},{40,8},{48,16},{56,24},{64,96... | collective-permute-start | bytes 3538952 | tf_op jit(solution)/shard_map/ppermute | solution.py:55
  94.4 24.5 %collective-permute-start.15 = (bf16[72,32,256]{2,1,0:T(8,128)(2,1)S(1)}, bf16[72,32,256]{2,1,0:T(8,128)(2,1)S(1)}, u32[]{:S(2)}, u32[]{:S(2)}) collective-permute-start(bf16[72,32,256]{2,1,0:T(8,128)(2,1)S(1)} %get-tuple-element.117), channel_id=1, source_target_pairs={{0,16},{8,24},{16,0},{24,8},{32,48},{40,56},{48,32},{56,40},{64,80... | collective-permute-start | bytes 3538952 | tf_op jit(solution)/shard_map/ppermute | solution.py:55
  95.2 23.2 %collective-permute-start.16 = (bf16[68,32,256]{2,1,0:T(8,128)(2,1)}, bf16[68,32,256]{2,1,0:T(8,128)(2,1)S(1)}, u32[]{:S(2)}, u32[]{:S(2)}) collective-permute-start(bf16[68,32,256]{2,1,0:T(8,128)(2,1)} %get-tuple-element.118), channel_id=1, source_target_pairs={{0,1},{1,0},{2,3},{3,2},{4,5},{5,4},{6,7},{7,6},{8,9},{9,8},{10,11... | collective-permute-start | bytes 3342344 | tf_op jit(solution)/shard_map/ppermute | solution.py:54
  95.9 20.4 %collective-permute-start.17 = (bf16[60,32,256]{2,1,0:T(8,128)(2,1)}, bf16[60,32,256]{2,1,0:T(8,128)(2,1)S(1)}, u32[]{:S(2)}, u32[]{:S(2)}) collective-permute-start(bf16[60,32,256]{2,1,0:T(8,128)(2,1)} %get-tuple-element.119), channel_id=1, source_target_pairs={{0,96},{8,104},{16,112},{24,120},{32,64},{40,72},{48,80},{56,88},{... | collective-permute-start | bytes 2949128 | tf_op jit(solution)/shard_map/ppermute | solution.py:55
  104.9 14.0 %copy-start.13 = (bf16[10,8,16,128]{3,2,1,0:T(8,128)(2,1)S(1)}, bf16[10,8,16,128]{3,2,1,0:T(8,128)(2,1)}, u32[]{:S(2)}) copy-start(bf16[10,8,16,128]{3,2,1,0:T(8,128)(2,1)} %copy.52) | copy-start | bytes 983044
  104.9 14.0 %copy-start.15 = (bf16[1,1,80,2,256]{4,3,2,1,0:T(2,128)(2,1)S(1)}, bf16[1,1,80,2,256]{4,3,2,1,0:T(2,128)(2,1)}, u32[]{:S(2)}) copy-start(bf16[1,1,80,2,256]{4,3,2,1,0:T(2,128)(2,1)} %param.20) | copy-start | bytes 245764
  110.5 18.6 %copy-start.17 = (s32[256]{0:T(256)S(1)}, s32[256]{0:T(256)}, u32[]{:S(2)}) copy-start(s32[256]{0:T(256)} %param.13) | copy-start | bytes 3076
  110.5 18.6 %copy-start.20 = (s32[256]{0:T(256)S(1)}, s32[256]{0:T(256)}, u32[]{:S(2)}) copy-start(s32[256]{0:T(256)} %param.14) | copy-start | bytes 3076
  129.9 0.7 copy-start.22

commit v3 on v2

--- a/solution.py
+++ b/solution.py
@@ -277,16 +277,19 @@
 
 
 def gather_chunks(table_ref, row, out_ref, pick):
-    batch = 4
-
-    def body(s, carry):
-        first = s * batch
-        held = [pick(table_ref[row, first + b]) for b in range(batch)]
+    def some(first, batch):
+        held = [pick(table_ref[row, first + b], first + b) for b in range(batch)]
         for b in range(batch):
             out_ref[first + b] = held[b]
+
+    def body(s, carry):
+        some(8 * s, 8)
         return carry
 
-    lax.fori_loop(0, out_ref.shape[0] // batch, body, 0, unroll=2)
+    count = out_ref.shape[0]
+    lax.fori_loop(0, count // 8, body, 0)
+    if count % 8:
+        some(count // 8 * 8, count % 8)
 
 
 SMEM = pl.BlockSpec(memory_space=pltpu.SMEM)
@@ -303,7 +306,7 @@
 
 
 def home_kernel(rows, table_ref, kv_ref, other_ref, *outs):
-    def pick(i):
+    def pick(i, s):
         row = i & (OWN_CHUNKS - 1)
         return jnp.where(i < OWN_CHUNKS, kv_ref[row], other_ref[row])
 
@@ -311,16 +314,31 @@
         gather_chunks(table_ref, rows + q, outs[q], pick)
 
 
-def home_lists(rows, rooms, table, kv, other):
+def own_kernel(table_ref, kv_ref, *outs):
+    for q in range(4):
+        gather_chunks(table_ref, q, outs[q], lambda i, s: kv_ref[i & (OWN_CHUNKS - 1)])
+
+
+def other_kernel(table_ref, other_ref, *rest):
+    befores, outs = rest[:4], rest[4:]
+    for q in range(4):
+
+        def pick(i, s):
+            return jnp.where(i < OWN_CHUNKS, befores[q][s], other_ref[i & (OWN_CHUNKS - 1)])
+
+        gather_chunks(table_ref, q, outs[q], pick)
+
+
+def lists_call(kernel, name, rooms, table, *operands):
     return pl.pallas_call(
-        functools.partial(home_kernel, rows),
+        kernel,
         out_shape=tuple(chunks_of(room) for room in rooms),
-        in_specs=[SMEM, VMEM, VMEM],
+        in_specs=[SMEM] + [VMEM] * len(operands),
         out_specs=(VMEM,) * 4,
-        compiler_params=pltpu.CompilerParams(vmem_limit_bytes=24 * MIB),
+        compiler_params=pltpu.CompilerParams(vmem_limit_bytes=28 * MIB),
         cost_estimate=cost(SMALL),
-        name="home_lists",
-    )(table, kv, other)
+        name=name,
+    )(table, *operands)
 
 
 def part_pairs(part, boxes, space, begin=0):
@@ -331,35 +349,45 @@
     return pairs
 
 
-def next_kernel(phase, table_ref, *rest):
-    each = phase + 1
-    boxes, outs, space, sems = rest[: 4 * each], rest[4 * each : 4 * each + 4], rest[4 * each + 4], rest[4 * each + 5]
+def before_kernel(phase, table_ref, *rest):
+    boxes, outs, space, sems = rest[: 4 * phase], rest[4 * phase : 4 * phase + 4], rest[4 * phase + 4], rest[4 * phase + 5]
     copies = []
     for q in range(4):
-        pairs = part_pairs(q, boxes[each * q : each * q + each], space, begin_of(q, phase))
+        pairs = part_pairs(q, boxes[phase * q : phase * q + phase], space, begin_of(q, phase - 1))
         copies.append(fetch(pairs, sems.at[q]))
     for q in range(4):
         for copy in copies[q]:
             copy.wait()
-        begin = begin_of(q, phase)
-        gather_chunks(table_ref, 4 * phase + q, outs[q], lambda i: space[begin + i])
-
-
-def next_lists(phase, table, boxes):
+        begin, end = begin_of(q, phase - 1), region(phase - 1, q) - 1
+        gather_chunks(table_ref, 4 * phase + q, outs[q], lambda i, s: space[begin + jnp.minimum(i, end)])
+
+
+def before_lists(phase, table, boxes):
     flat = [box for part in boxes for box in part]
     return pl.pallas_call(
-        functools.partial(next_kernel, phase),
+        functools.partial(before_kernel, phase),
         out_shape=tuple(chunks_of(room) for room in ROOM[phase]),
         in_specs=[SMEM] + [ANY] * len(flat),
         out_specs=(VMEM,) * 4,
         scratch_shapes=[
-            pltpu.VMEM((begin_of(4, phase), CHUNK, 256), jnp.bfloat16),
-            pltpu.SemaphoreType.DMA((4, phase + 1)),
+            pltpu.VMEM((begin_of(4, phase - 1), CHUNK, 256), jnp.bfloat16),
+            pltpu.SemaphoreType.DMA((4, phase)),
         ],
         compiler_params=pltpu.CompilerParams(vmem_limit_bytes=28 * MIB),
         cost_estimate=cost(SMALL),
-        name="next_lists",
+        name="before_lists",
     )(table, *flat)
+
+
+def after_kernel(phase, table_ref, *rest):
+    befores, boxes, outs = rest[:4], rest[4:8], rest[8:]
+    for q in range(4):
+        begin = region(phase - 1, q)
+
+        def pick(i, s):
+            return jnp.where(i < begin, befores[q][s], boxes[q][jnp.maximum(i - begin, 0)])
+
+        gather_chunks(table_ref, 4 * phase + q, outs[q], pick)
 
 
 def attend_row(query, first, second, own, length):
@@ -444,7 +472,7 @@
 
 
 def running_rows(first, count, half, pages, lens, queries, own, pool):
-    max_pages = pages.shape[-1]
+    max_pages = pages.shape[0] // lens.shape[0]
     return pl.pallas_call(
         functools.partial(running_kernel, first),
         out_shape=jax.ShapeDtypeStruct((count, 2048), jnp.bfloat16),
@@ -455,10 +483,10 @@
             pltpu.VMEM((count * 16, 128), jnp.float32),
             pltpu.SemaphoreType.DMA((DEPTH, max_pages)),
         ],
-        compiler_params=pltpu.CompilerParams(vmem_limit_bytes=48 * MIB),
+        compiler_params=pltpu.CompilerParams(vmem_limit_bytes=40 * MIB),
         cost_estimate=cost(SMALL),
         name="running_rows",
-    )(half, pages.reshape(-1), lens.reshape(-1), queries, own, pool)
+    )(half, pages, lens, queries, own, pool)
 
 
 RING = 4
@@ -485,9 +513,9 @@
             write(slot).wait()
 
         for j in range(2):
-            for k in range(0, PROMPT_CHUNKS, 4):
-                held = [space[land_ref[PROMPT_CHUNKS * j + k + b, slot]] for b in range(4)]
-                for b in range(4):
+            for k in range(0, PROMPT_CHUNKS, 8):
+                held = [space[land_ref[PROMPT_CHUNKS * j + k + b, slot]] for b in range(8)]
+                for b in range(8):
                     block[slot % RING, j, k + b] = held[b]
         write(slot).start()
         return carry
@@ -520,7 +548,8 @@
 
 def land_kernel(given, land_ref, query_ref, own_ref, early_ref, *rest):
     contexts, rest = rest[:given], rest[given:]
-    boxes, (out_ref, landed_ref, block, result, in_sems, sems, space, box_sems) = rest[:4], rest[4:]
+    boxes, rest = rest[:4], rest[4:]
+    out_ref, landed_ref, block, result, handed, in_sems, sems, space, box_sems, out_sems = rest
     slots = landed_ref.shape[0]
     first = out_ref.shape[0] - slots
 
@@ -536,9 +565,11 @@
     for slot in range(4):
         read(slot).start()
     done = 0
+    pairs = []
     for context in contexts:
-        out_ref[done : done + context.shape[0]] = context[...]
+        pairs.append((context, out_ref.at[pl.ds(done, context.shape[0])]))
         done += context.shape[0]
+    decoded = fetch(pairs, out_sems)
     for copy in copies:
         copy.wait()
 
@@ -546,12 +577,12 @@
         turn = slot % LAND_RING
         length = land_ref[LENGTH, slot]
         for j in range(2):
-            for k in range(0, PROMPT_CHUNKS, 2):
+            for k in range(0, PROMPT_CHUNKS, 8):
                 held = []
-                for b in range(2):
+                for b in range(8):
                     source = land_ref[LATE + PROMPT_CHUNKS * j + k + b, slot]
                     held.append(jnp.where(source >= 0, space[jnp.maximum(source, 0)], block[turn, j, k + b]))
-                for b in range(2):
+                for b in range(8):
                     block[turn, j, k + b] = held[b]
         last = jnp.maximum(length - 1, 0) // CHUNK
         row = last * CHUNK + lax.broadcasted_iota(jnp.int32, (CHUNK, 256), 0)
@@ -589,9 +620,13 @@
         return carry
 
     lax.fori_loop(0, slots // 2, body, 0)
-    lay_rows(result, out_ref, first, slots)
+    lay_rows(result, handed, 0, slots)
+    last = pltpu.make_async_copy(handed, out_ref.at[pl.ds(first, slots)], out_sems.at[len(contexts)])
+    last.start()
     for slot in range(slots - LAND_RING, slots):
         write(slot).wait()
+    for copy in decoded + [last]:
+        copy.wait()
 
 
 def land_rows(land, queries, own, early, contexts, boxes):
@@ -602,14 +637,16 @@
             jax.ShapeDtypeStruct(early.shape, jnp.bfloat16),
         ),
         in_specs=[SMEM, VMEM, VMEM, ANY] + [VMEM] * len(contexts) + [ANY] * 4,
-        out_specs=(VMEM, ANY),
+        out_specs=(ANY, ANY),
         scratch_shapes=[
             pltpu.VMEM((LAND_RING,) + early.shape[1:], jnp.bfloat16),
             pltpu.VMEM((16 * early.shape[0], 128), jnp.float32),
+            pltpu.VMEM((early.shape[0], 2048), jnp.bfloat16),
             pltpu.SemaphoreType.DMA((LAND_RING,)),
             pltpu.SemaphoreType.DMA((LAND_RING,)),
             pltpu.VMEM((LATE_BEGIN[4], CHUNK, 256), jnp.bfloat16),
             pltpu.SemaphoreType.DMA((4,)),
+            pltpu.SemaphoreType.DMA((len(contexts) + 1,)),
         ],
         compiler_params=pltpu.CompilerParams(vmem_limit_bytes=24 * MIB),
         cost_estimate=cost(SMALL),
@@ -617,31 +654,38 @@
     )(land, queries, own, early, *contexts, *boxes)
 
 
-def routed(operands, kv, other, half, pages, lens, queries, own, pool):
+def routed(operands, kv, half, pages, lens, queries, own, pool):
     running = pages.shape[1]
     rows = queries.shape[0]
+    pages, lens = pages.reshape(-1), lens.reshape(-1)
+    other = hop(kv, CORE)
     (table,) = plan_call(first_plan_kernel, "first_plan", (8,), *operands)
-    lists = home_lists(0, ROOM[0], table, kv, other)
+    lists = lists_call(own_kernel, "own_lists", ROOM[0], table, kv)
+    queries = queries.reshape(rows, 16, 128)
+    lists, other, queries, pages, lens = lax.optimization_barrier((lists, other, queries, pages, lens))
+    lists = lists_call(other_kernel, "first_lists", ROOM[0], table, other, *lists)
     sent = [hop(value, order[0]) for value, order in zip(lists, ORDERS)]
     (where, table), _ = lax.optimization_barrier(((operands[0], table), lists))
-    kept = home_lists(4, KEPT, table, kv, other)
+    kept = lists_call(functools.partial(home_kernel, 4), "kept_lists", KEPT, table, kv, other)
     table, land = plan_call(plan_kernel, "plan", (16, 72), where, *operands[1:])
     boxes = [[k] for k in kept]
+    befores = before_lists(1, table, boxes)
     contexts = []
     done = 0
     for phase, count in ((1, running // 4), (2, running // 2), (3, running // 4)):
+        table, sent, befores = lax.optimization_barrier((table, sent, befores))
+        lists = lists_call(functools.partial(after_kernel, phase), "after_lists", ROOM[phase], table, *befores, *sent)
         boxes = [part + [box] for part, box in zip(boxes, sent)]
-        lists = next_lists(phase, table, boxes)
         sent = [hop(value, order[phase]) for value, order in zip(lists, ORDERS)]
-        ready, _ = lax.optimization_barrier((half, lists))
+        (ready, table, land), _ = lax.optimization_barrier(((half, table, land), lists))
         contexts.append(running_rows(done, count, ready, pages, lens, queries, own, pool))
         done += count
-        if phase == 3:
-            land, _ = lax.optimization_barrier((land, lists))
+        if phase < 3:
+            befores = before_lists(phase + 1, table, boxes)
+            table, _ = lax.optimization_barrier((table, contexts))
+        else:
             early = early_rows(rows - running, land, [box for part in boxes for box in part])
             sent, _, early = lax.optimization_barrier((sent, contexts, early))
-        else:
-            table, _ = lax.optimization_barrier((table, contexts))
     context, landed = land_rows(land, queries, own, early, contexts, sent)
     return context, landed, land[OVER, 0]
 
@@ -720,25 +764,24 @@
     group = lax.axis_index("grp")
     member = lax.axis_index("tp")
     kv = prompt_kv.reshape(OWN_CHUNKS, CHUNK, 256)
-    other = hop(kv, CORE)
     operands = plan_operands(targets, prompt_lens, group, member)
     half = (member % 2).astype(jnp.int32).reshape(1)
     rows = queries.shape[2]
     running = block_table.shape[2]
-    by_head = queries.reshape(rows, 16, 128)
     own = new_kv[0, 0]
+    queries = queries[0, 0]
     context, landed, over = routed(
-        operands, kv, other, half, block_table[0], cache_lens[0], by_head, own, cache_pool[0, 0]
+        operands, kv, half, block_table[0], cache_lens[0], queries, own, cache_pool[0, 0]
     )
 
     def again(carry):
-        handed, landed = any_fill(targets, prompt_lens, kv, by_head[running:], own[running:])
+        handed, landed = any_fill(targets, prompt_lens, kv, queries[running:].reshape(-1, 16, 128), own[running:])
         handed = handed.astype(jnp.bfloat16).reshape(rows - running, -1)
         return carry[0].at[running:].set(handed), landed, jnp.zeros((), jnp.int32)
 
     context, landed, _ = lax.while_loop(lambda carry: carry[2] > 0, again, (context, landed, over))
     return (
-        context.reshape(1, 1, rows, queries.shape[3]),
+        context.reshape(1, 1, rows, -1),
         landed.reshape(1, 1, 16, 2, 512, 256),
     )
 

time: 131 us -> 126 us (0.962)
  waiting for transfers between devices: 28.9 us -> 23.4 us
  Pallas kernels: 75.5 us -> 77.9 us
  local copies, waits for them, and re-layouts: 6.69 us -> 4.67 us
    ppermute x13, waiting for transfers between devices: 24.2 us -> 19.7 us  [hop(): lax.ppermute(value, 'grp', [(g, flipped(g, axis)) for g in range(lax.axis...]
    pallas_call x5 -> x9, Pallas kernels: 20.2 us -> 23.9 us  [the longest x6 16 us: lists_call(): pl.pallas_call(kernel, out_shape=tuple((chunks_of(room) for room in rooms...]
    pallas_call x3, Pallas kernels: 31.2 us -> 29.8 us  [running_rows(): pl.pallas_call(functools.partial(running_kernel, first), out_shape=jax.Sh...]
    unnamed x48 -> x16, local copies, waits for them, and re-layouts: 4.45 us -> 3.26 us
  transfers between devices with their start and end apart: 17 -> 17, of which waited for: 12 -> 10; matrix products, arithmetic and copies ran while one was open for 3% -> 3% of each run, Pallas kernels for 37% -> 45%
where the time goes in v3:
time: 126 us
  Pallas kernels  77.9 us (62%)
  waiting for transfers between devices  23.4 us (19%)
  starting transfers between devices  17.9 us (14%)
  local copies, waits for them, and re-layouts  4.67 us (4%)
    pallas_call x3, Pallas kernels, running_rows(): pl.pallas_call(functools.partial(running_kernel, first), out_shape=jax.Sh...  29.8 us
    ppermute x13, waiting for transfers between devices, hop(): lax.ppermute(value, 'grp', [(g, flipped(g, axis)) for g in range(lax.axis...  19.7 us
    pallas_call x6, Pallas kernels, lists_call(): pl.pallas_call(kernel, out_shape=tuple((chunks_of(room) for room in rooms...  16 us
    ppermute x13, starting transfers between devices, hop(): lax.ppermute(value, 'grp', [(g, flipped(g, axis)) for g in range(lax.axis...  12.6 us
    pallas_call x1, Pallas kernels, land_rows(): pl.pallas_call(functools.partial(land_kernel, len(contexts)), out_shape=(...  11.1 us
    pallas_call x2, Pallas kernels, plan_call(): pl.pallas_call(kernel, out_shape=tuple((jax.ShapeDtypeStruct((r, 128), jn...  8.21 us
    pallas_call x3, Pallas kernels, before_lists(): pl.pallas_call(functools.partial(before_kernel, phase), out_shape=tuple((...  7.88 us
    ppermute x4, starting transfers between devices, hop(): lax.ppermute(value, 'tp', [(t, t ^ 1) for t in range(lax.axis_size('tp'))])  5.22 us
  transfers between devices with their start and end apart: 17, of which 10 were waited for; matrix products, arithmetic and copies ran while one was open for 3% of the time, Pallas kernels for 45%

profile of v3, /device:TPU:16, one launch (start us, length us, event | category | flops | bytes accessed | tf_op | source)
XLA Modules:
  0.0 125.7 jit_solution(7189197932490130191)
XLA Ops:
  0.8 0.7 copy-done
  1.5 1.7 %first_plan.1.table_ref = s32[8,128]{1,0:T(8,128)S(1)} custom-call(s32[3]{0:T(128)S(1)} %pad_add_fusion.where_ref, s32[1,256]{1,0:T(1,128)} %bitcast.506, s32[1,256]{1,0:T(1,128)} %bitcast.509, s32[8,64]{1,0:T(8,128)S(1)} %copy-done), custom_call_target="tpu_custom_call" | custom-call | bytes 4096 | tf_op jit(solution)/shard_map/first_plan/pallas_call | solution.py:254
  3.2 2.7 %own_lists.1 = (bf16[40,32,256]{2,1,0:T(8,128)(2,1)S(1)}, bf16[40,32,256]{2,1,0:T(8,128)(2,1)S(1)}, bf16[48,32,256]{2,1,0:T(8,128)(2,1)S(1)}, bf16[36,32,256]{2,1,0:T(8,128)(2,1)S(1)}) custom-call(s32[8,128]{1,0:T(8,128)S(1)} %first_plan.1.table_ref, bf16[256,32,256]{2,1,0:T(8,128)(2,1)} %bitcast.475), custom_call_target="tpu_custom_call" | custom-call | bytes 4096 | tf_op jit(solution)/shard_map/own_lists/pallas_call | solution.py:333
  5.9 1.0 copy.52
  7.0 0.8 copy.35
  7.8 0.1 reshape_squeeze.10.pages_ref
  7.9 0.8 reshape_squeeze.11.lens_ref
  8.7 3.0 %first_lists.1 = (bf16[40,32,256]{2,1,0:T(8,128)(2,1)S(1)}, bf16[40,32,256]{2,1,0:T(8,128)(2,1)S(1)}, bf16[48,32,256]{2,1,0:T(8,128)(2,1)S(1)}, bf16[36,32,256]{2,1,0:T(8,128)(2,1)S(1)}) custom-call(s32[8,128]{1,0:T(8,128)S(1)} %first_plan.1.table_ref, bf16[256,32,256]{2,1,0:T(8,128)(2,1)} %collective-permute-done.1.other_ref, ...), custom_call_target="tpu_custom_call" | custom-call | bytes 4096 | tf_op jit(solution)/shard_map/first_lists/pallas_call | solution.py:333
  11.7 0.5 collective-permute-start.4
  12.2 1.5 %collective-permute-start.2 = (bf16[40,32,256]{2,1,0:T(8,128)(2,1)S(1)}, bf16[40,32,256]{2,1,0:T(8,128)(2,1)S(1)}, u32[]{:S(2)}, u32[]{:S(2)}) collective-permute-start(bf16[40,32,256]{2,1,0:T(8,128)(2,1)S(1)} %get-tuple-element.156), channel_id=1, source_target_pairs={{0,16},{8,24},{16,0},{24,8},{32,48},{40,56},{48,32},{56,40},{64,80... | collective-permute-start | bytes 1966088 | tf_op jit(solution)/shard_map/ppermute | solution.py:55
  13.7 1.1 collective-permute-start.3
  14.8 1.9 %collective-permute-start.5 = (bf16[36,32,256]{2,1,0:T(8,128)(2,1)S(1)}, bf16[36,32,256]{2,1,0:T(8,128)(2,1)S(1)}, u32[]{:S(2)}, u32[]{:S(2)}) collective-permute-start(bf16[36,32,256]{2,1,0:T(8,128)(2,1)S(1)} %get-tuple-element.159), channel_id=1, source_target_pairs={{0,1},{1,0},{2,3},{3,2},{4,5},{5,4},{6,7},{7,6},{8,9},{9,8},{10,11... | collective-permute-start | bytes 1769480 | tf_op jit(solution)/shard_map/ppermute | solution.py:54
  16.7 3.1 %kept_lists.1 = (bf16[52,32,256]{2,1,0:T(8,128)(2,1)S(1)}, bf16[52,32,256]{2,1,0:T(8,128)(2,1)S(1)}, bf16[64,32,256]{2,1,0:T(8,128)(2,1)S(1)}, bf16[40,32,256]{2,1,0:T(8,128)(2,1)S(1)}) custom-call(s32[8,128]{1,0:T(8,128)S(1)} %first_plan.1.table_ref, bf16[256,32,256]{2,1,0:T(8,128)(2,1)S(1)} %bitcast.476, bf16[256,32,256]{2,1,0:T(8,128)(2,1)} %collective-permute-done.1.other_ref), custom_call_target="tpu_custom_call" | custom-call | bytes 4096 | tf_op jit(solution)/shard_map/kept_lists/pallas_call | solution.py:333
  19.8 6.5 %plan.1 = (s32[16,128]{1,0:T(8,128)S(1)}, s32[72,128]{1,0:T(8,128)S(1)}) custom-call(s32[3]{0:T(128)S(1)} %pad_add_fusion.where_ref, s32[1,256]{1,0:T(1,128)S(1)} %bitcast.507, s32[1,256]{1,0:T(1,128)S(1)} %bitcast.510, s32[8,64]{1,0:T(8,128)S(1)} %copy-done.1), custom_call_target="tpu_custom_call" | custom-call | bytes 4096 | tf_op jit(solution)/shard_map/plan/pallas_call | solution.py:254
  26.4 1.9 %before_lists.3 = (bf16[48,32,256]{2,1,0:T(8,128)(2,1)S(1)}, bf16[44,32,256]{2,1,0:T(8,128)(2,1)S(1)}, bf16[48,32,256]{2,1,0:T(8,128)(2,1)S(1)}, bf16[48,32,256]{2,1,0:T(8,128)(2,1)S(1)}) custom-call(s32[16,128]{1,0:T(8,128)S(1)} %get-tuple-element.216.table_ref, bf16[52,32,256]{2,1,0:T(8,128)(2,1)S(1)} %get-tuple-element.163.rest_0_, ...), custom_call_target="tpu_custom_call" | custom-call | bytes 4096 | tf_op jit(solution)/shard_map/before_lists/pallas_call | solution.py:367
  28.3 1.6 %collective-permute-done.5.rest_7_.rest_10_.rest_13_ = bf16[36,32,256]{2,1,0:T(8,128)(2,1)S(1)} collective-permute-done((bf16[36,32,256]{2,1,0:T(8,128)(2,1)S(1)}, bf16[36,32,256]{2,1,0:T(8,128)(2,1)S(1)}, u32[]{:S(2)}, u32[]{:S(2)}) %collective-permute-start.5) | collective-permute-done | bytes 589856 | tf_op jit(solution)/shard_map/ppermute | solution.py:54
  30.0 0.3 collective-permute-done.3.rest_5_.rest_3_.rest_4_
  30.3 1.4 %collective-permute-done.4.rest_6_.rest_5_.rest_7_.rest_9_ = bf16[48,32,256]{2,1,0:T(8,128)(2,1)S(1)} collective-permute-done((bf16[48,32,256]{2,1,0:T(8,128)(2,1)S(1)}, bf16[48,32,256]{2,1,0:T(8,128)(2,1)S(1)}, u32[]{:S(2)}, u32[]{:S(2)}) %collective-permute-start.4) | collective-permute-done | bytes 786464 | tf_op jit(solution)/shard_map/ppermute | solution.py:55
  31.7 1.5 %after_lists.3 = (bf16[48,32,256]{2,1,0:T(8,128)(2,1)S(1)}, bf16[44,32,256]{2,1,0:T(8,128)(2,1)S(1)}, bf16[48,32,256]{2,1,0:T(8,128)(2,1)S(1)}, bf16[48,32,256]{2,1,0:T(8,128)(2,1)S(1)}) custom-call(s32[16,128]{1,0:T(8,128)S(1)} %get-tuple-element.216.table_ref, bf16[48,32,256]{2,1,0:T(8,128)(2,1)S(1)} %get-tuple-element.173.rest_0_, ...), custom_call_target="tpu_custom_call" | custom-call | bytes 4096 | tf_op jit(solution)/shard_map/after_lists/pallas_call | solution.py:333
  33.2 2.0 %collective-permute-start.6 = (bf16[48,32,256]{2,1,0:T(8,128)(2,1)S(1)}, bf16[48,32,256]{2,1,0:T(8,128)(2,1)S(1)}, u32[]{:S(2)}, u32[]{:S(2)}) collective-permute-start(bf16[48,32,256]{2,1,0:T(8,128)(2,1)S(1)} %get-tuple-element.181), channel_id=1, source_target_pairs={{0,1},{1,0},{2,3},{3,2},{4,5},{5,4},{6,7},{7,6},{8,9},{9,8},{10,11... | collective-permute-start | bytes 2359304 | tf_op jit(solution)/shard_map/ppermute | solution.py:54
  35.2 2.5 %collective-permute-start.8 = (bf16[48,32,256]{2,1,0:T(8,128)(2,1)S(1)}, bf16[48,32,256]{2,1,0:T(8,128)(2,1)S(1)}, u32[]{:S(2)}, u32[]{:S(2)}) collective-permute-start(bf16[48,32,256]{2,1,0:T(8,128)(2,1)S(1)} %get-tuple-element.183), channel_id=1, source_target_pairs={{0,32},{8,40},{16,48},{24,56},{32,0},{40,8},{48,16},{56,24},{64,96... | collective-permute-start | bytes 2359304 | tf_op jit(solution)/shard_map/ppermute | solution.py:55
  37.7 1.5 %collective-permute-start.9 = (bf16[48,32,256]{2,1,0:T(8,128)(2,1)S(1)}, bf16[48,32,256]{2,1,0:T(8,128)(2,1)S(1)}, u32[]{:S(2)}, u32[]{:S(2)}) collective-permute-start(bf16[48,32,256]{2,1,0:T(8,128)(2,1)S(1)} %get-tuple-element.184), channel_id=1, source_target_pairs={{0,16},{8,24},{16,0},{24,8},{32,48},{40,56},{48,32},{56,40},{64,80... | collective-permute-start | bytes 2359304 | tf_op jit(solution)/shard_map/ppermute | solution.py:55
  39.2 2.6 %before_lists.4 = (bf16[64,32,256]{2,1,0:T(8,128)(2,1)S(1)}, bf16[52,32,256]{2,1,0:T(8,128)(2,1)S(1)}, bf16[48,32,256]{2,1,0:T(8,128)(2,1)S(1)}, bf16[52,32,256]{2,1,0:T(8,128)(2,1)S(1)}) custom-call(s32[16,128]{1,0:T(8,128)S(1)} %get-tuple-element.216.table_ref, bf16[52,32,256]{2,1,0:T(8,128)(2,1)S(1)} %get-tuple-element.163.rest_0_, ...), custom_call_target="tpu_custom_call" | custom-call | bytes 4096 | tf_op jit(solution)/shard_map/before_lists/pallas_call | solution.py:367
  41.9 8.2 %running_rows.3.rest_0_ = bf16[16,2048]{1,0:T(8,128)(2,1)S(1)} custom-call(s32[1]{0:T(128)} %bitcast.158.half_ref, s32[768]{0:T(1024)S(1)} %reshape_squeeze.10.pages_ref, s32[128]{0:T(128)S(1)} %reshape_squeeze.11.lens_ref, bf16[80,16,128]{2,1,0:T(8,128)(2,1)S(1)} %bitcast.468, bf16[80,2,256]{2,1,0:T(2,128)(2,1)S(1)} %bitcast.485, ...), custom_call_target="tpu_custom_call" | custom-call | bytes 4096 | tf_op jit(solution)/shard_map/running_rows/pallas_call | solution.py:476
  50.1 6.0 %collective-permute-done.7.rest_5_.rest_6_ = bf16[44,32,256]{2,1,0:T(8,128)(2,1)S(1)} collective-permute-done((bf16[44,32,256]{2,1,0:T(8,128)(2,1)S(1)}, bf16[44,32,256]{2,1,0:T(8,128)(2,1)S(1)}, u32[]{:S(2)}, u32[]{:S(2)}) %collective-permute-start.7) | collective-permute-done | bytes 720928 | tf_op jit(solution)/shard_map/ppermute | solution.py:55
  56.1 0.2 collective-permute-done.9.rest_7_.rest_11_.rest_14_
  56.3 1.7 %after_lists.4 = (bf16[64,32,256]{2,1,0:T(8,128)(2,1)S(1)}, bf16[52,32,256]{2,1,0:T(8,128)(2,1)S(1)}, bf16[48,32,256]{2,1,0:T(8,128)(2,1)S(1)}, bf16[52,32,256]{2,1,0:T(8,128)(2,1)S(1)}) custom-call(s32[16,128]{1,0:T(8,128)S(1)} %get-tuple-element.216.table_ref, bf16[64,32,256]{2,1,0:T(8,128)(2,1)S(1)} %get-tuple-element.197.rest_0_, ...), custom_call_target="tpu_custom_call" | custom-call | bytes 4096 | tf_op jit(solution)/shard_map/after_lists/pallas_call | solution.py:333
  58.0 0.2 collective-permute-start.10
  58.1 0.5 collective-permute-start.11
  58.7 1.5 %collective-permute-start.13 = (bf16[52,32,256]{2,1,0:T(8,128)(2,1)S(1)}, bf16[52,32,256]{2,1,0:T(8,128)(2,1)S(1)}, u32[]{:S(2)}, u32[]{:S(2)}) collective-permute-start(bf16[52,32,256]{2,1,0:T(8,128)(2,1)S(1)} %get-tuple-element.208), channel_id=1, source_target_pairs={{0,32},{8,40},{16,48},{24,56},{32,0},{40,8},{48,16},{56,24},{64,96... | collective-permute-start | bytes 2555912 | tf_op jit(solution)/shard_map/ppermute | solution.py:55
  60.2 0.5 collective-permute-start.12
  60.7 3.3 %before_lists.5 = (bf16[72,32,256]{2,1,0:T(8,128)(2,1)S(1)}, bf16[72,32,256]{2,1,0:T(8,128)(2,1)S(1)}, bf16[68,32,256]{2,1,0:T(8,128)(2,1)S(1)}, bf16[60,32,256]{2,1,0:T(8,128)(2,1)S(1)}) custom-call(s32[16,128]{1,0:T(8,128)S(1)} %get-tuple-element.216.table_ref, bf16[52,32,256]{2,1,0:T(8,128)(2,1)S(1)} %get-tuple-element.163.rest_0_, ...), custom_call_target="tpu_custom_call" | custom-call | bytes 4096 | tf_op jit(solution)/shard_map/before_lists/pallas_call | solution.py:367
  64.0 13.4 %running_rows.4.rest_1_ = bf16[32,2048]{1,0:T(8,128)(2,1)S(1)} custom-call(s32[1]{0:T(128)} %bitcast.158.half_ref, s32[768]{0:T(1024)S(1)} %reshape_squeeze.10.pages_ref, s32[128]{0:T(128)S(1)} %reshape_squeeze.11.lens_ref, bf16[80,16,128]{2,1,0:T(8,128)(2,1)S(1)} %bitcast.469, bf16[80,2,256]{2,1,0:T(2,128)(2,1)S(1)} %bitcast.486, ...), custom_call_target="tpu_custom_call" | custom-call | bytes 4096 | tf_op jit(solution)/shard_map/running_rows/pallas_call | solution.py:476
  77.5 0.2 collective-permute-done.13.rest_7_.rest_15_
  77.7 3.6 %collective-permute-done.10.rest_4_.rest_3_ = bf16[64,32,256]{2,1,0:T(8,128)(2,1)S(1)} collective-permute-done((bf16[64,32,256]{2,1,0:T(8,128)(2,1)S(1)}, bf16[64,32,256]{2,1,0:T(8,128)(2,1)S(1)}, u32[]{:S(2)}, u32[]{:S(2)}) %collective-permute-start.10) | collective-permute-done | bytes 1048608 | tf_op jit(solution)/shard_map/ppermute | solution.py:55
  81.3 4.0 %after_lists.5 = (bf16[72,32,256]{2,1,0:T(8,128)(2,1)}, bf16[72,32,256]{2,1,0:T(8,128)(2,1)}, bf16[68,32,256]{2,1,0:T(8,128)(2,1)}, bf16[60,32,256]{2,1,0:T(8,128)(2,1)}) custom-call(s32[16,128]{1,0:T(8,128)S(1)} %get-tuple-element.216.table_ref, bf16[72,32,256]{2,1,0:T(8,128)(2,1)S(1)} %get-tuple-element.218.rest_0_, ...), custom_call_target="tpu_custom_call" | custom-call | bytes 4096 | tf_op jit(solution)/shard_map/after_lists/pallas_call | solution.py:333
  85.4 2.5 %collective-permute-start.14 = (bf16[72,32,256]{2,1,0:T(8,128)(2,1)}, bf16[72,32,256]{2,1,0:T(8,128)(2,1)S(1)}, u32[]{:S(2)}, u32[]{:S(2)}) collective-permute-start(bf16[72,32,256]{2,1,0:T(8,128)(2,1)} %get-tuple-element.226), channel_id=1, source_target_pairs={{0,32},{8,40},{16,48},{24,56},{32,0},{40,8},{48,16},{56,24},{64,96... | collective-permute-start | bytes 3538952 | tf_op jit(solution)/shard_map/ppermute | solution.py:55
  87.9 0.7 collective-permute-start.15
  88.6 0.8 collective-permute-start.16
  89.4 4.9 %early_rows.1.early_ref = bf16[16,2,16,32,256]{4,3,2,1,0:T(8,128)(2,1)S(1)} custom-call(s32[72,128]{1,0:T(8,128)S(1)} %get-tuple-element.230.land_ref, bf16[52,32,256]{2,1,0:T(8,128)(2,1)S(1)} %get-tuple-element.163.rest_0_, bf16[40,32,256]{2,1,0:T(8,128)(2,1)S(1)} %collective-permute-done.2.rest_4_.rest_1_, ...), custom_call_target="tpu_custom_call" | custom-call | bytes 4096 | tf_op jit(solution)/shard_map/early_rows/pallas_call | solution.py:529
  94.3 0.5 slice.796
  94.8 8.2 %running_rows.5.rest_2_ = bf16[16,2048]{1,0:T(8,128)(2,1)S(1)} custom-call(s32[1]{0:T(128)} %bitcast.158.half_ref, s32[768]{0:T(1024)S(1)} %reshape_squeeze.10.pages_ref, s32[128]{0:T(128)S(1)} %reshape_squeeze.11.lens_ref, bf16[80,16,128]{2,1,0:T(8,128)(2,1)S(1)} %bitcast.470, bf16[80,2,256]{2,1,0:T(2,128)(2,1)S(1)} %bitcast.487, ...), custom_call_target="tpu_custom_call" | custom-call | bytes 4096 | tf_op jit(solution)/shard_map/running_rows/pallas_call | solution.py:476
  103.0 7.3 %collective-permute-done.17.rest_6_ = bf16[60,32,256]{2,1,0:T(8,128)(2,1)} collective-permute-done((bf16[60,32,256]{2,1,0:T(8,128)(2,1)}, bf16[60,32,256]{2,1,0:T(8,128)(2,1)}, u32[]{:S(2)}, u32[]{:S(2)}) %collective-permute-start.17) | collective-permute-done | bytes 983072 | tf_op jit(solution)/shard_map/ppermute | solution.py:55
  110.3 2.0 %collective-permute-done.16.rest_5_ = bf16[68,32,256]{2,1,0:T(8,128)(2,1)} collective-permute-done((bf16[68,32,256]{2,1,0:T(8,128)(2,1)}, bf16[68,32,256]{2,1,0:T(8,128)(2,1)}, u32[]{:S(2)}, u32[]{:S(2)}) %collective-permute-start.16) | collective-permute-done | bytes 1114144 | tf_op jit(solution)/shard_map/ppermute | solution.py:54
  112.3 0.6 collective-permute-done.15.rest_4_
  113.0 11.1 %land_rows.1 = (bf16[80,2048]{1,0:T(8,128)(2,1)S(1)}, bf16[16,2,16,32,256]{4,3,2,1,0:T(8,128)(2,1)}) custom-call(s32[72,128]{1,0:T(8,128)S(1)} %get-tuple-element.230.land_ref, bf16[80,16,128]{2,1,0:T(8,128)(2,1)S(1)} %bitcast.471, bf16[80,2,256]{2,1,0:T(2,128)(2,1)S(1)} %bitcast.488, bf16[16,2,16,32,256]{4,3,2,1,0:T(8,128)(2,1)S(1)} %early_rows.1.early_ref, ...), custom_call_target="tpu_custom_call" | custom-call | bytes 4096 | tf_op jit(solution)/shard_map/land_rows/pallas_call | solution.py:633
  124.1 0.9 while.12
  125.0 0.7 copy-done.6
  (23 shorter events, 0.2 us)
Async XLA Ops:
  0.6 8.1 %collective-permute-start.1 = (bf16[256,32,256]{2,1,0:T(8,128)(2,1)}, bf16[256,32,256]{2,1,0:T(8,128)(2,1)}, u32[]{:S(2)}, u32[]{:S(2)}) collective-permute-start(bf16[256,32,256]{2,1,0:T(8,128)(2,1)} %bitcast.474), channel_id=1, source_target_pairs={{0,8},{8,0},{16,24},{24,16},{32,40},{40,32},{48,56},{56,48},{64,72... | collective-permute-start | bytes 12582920 | tf_op jit(solution)/shard_map/ppermute | solution.py:55
  0.8 0.7 copy-start
  5.9 13.9 %copy-start.1 = (s32[8,64]{1,0:T(8,128)S(1)}, s32[8,64]{1,0:T(8,128)}, u32[]{:S(2)}) copy-start(s32[8,64]{1,0:T(8,128)} %constant.173.clone.const_ref) | copy-start | bytes 6148
  5.9 13.9 %copy-start.4 = (s32[256]{0:T(256)S(1)}, s32[256]{0:T(256)}, u32[]{:S(2)}) copy-start(s32[256]{0:T(256)} %param.13) | copy-start | bytes 3076
  5.9 13.9 %copy-start.5 = (s32[256]{0:T(256)S(1)}, s32[256]{0:T(256)}, u32[]{:S(2)}) copy-start(s32[256]{0:T(256)} %param.14) | copy-start | bytes 3076
  8.7 8.0 %copy-start.2 = (bf16[16,1,512,256]{3,2,1,0:T(8,128)(2,1)S(1)}, bf16[16,1,512,256]{3,2,1,0:T(8,128)(2,1)}, u32[]{:S(2)}) copy-start(bf16[16,1,512,256]{3,2,1,0:T(8,128)(2,1)} %param.15) | copy-start | bytes 12582916
  11.7 20.0 %collective-permute-start.4 = (bf16[48,32,256]{2,1,0:T(8,128)(2,1)S(1)}, bf16[48,32,256]{2,1,0:T(8,128)(2,1)S(1)}, u32[]{:S(2)}, u32[]{:S(2)}) collective-permute-start(bf16[48,32,256]{2,1,0:T(8,128)(2,1)S(1)} %get-tuple-element.158), channel_id=1, source_target_pairs={{0,96},{8,104},{16,112},{24,120},{32,64},{40,72},{48,80},{56,88},{... | collective-permute-start | bytes 2359304 | tf_op jit(solution)/shard_map/ppermute | solution.py:55
  12.2 17.7 %collective-permute-start.2 = (bf16[40,32,256]{2,1,0:T(8,128)(2,1)S(1)}, bf16[40,32,256]{2,1,0:T(8,128)(2,1)S(1)}, u32[]{:S(2)}, u32[]{:S(2)}) collective-permute-start(bf16[40,32,256]{2,1,0:T(8,128)(2,1)S(1)} %get-tuple-element.156), channel_id=1, source_target_pairs={{0,16},{8,24},{16,0},{24,8},{32,48},{40,56},{48,32},{56,40},{64,80... | collective-permute-start | bytes 1966088 | tf_op jit(solution)/shard_map/ppermute | solution.py:55
  13.7 16.5 %collective-permute-start.3 = (bf16[40,32,256]{2,1,0:T(8,128)(2,1)S(1)}, bf16[40,32,256]{2,1,0:T(8,128)(2,1)S(1)}, u32[]{:S(2)}, u32[]{:S(2)}) collective-permute-start(bf16[40,32,256]{2,1,0:T(8,128)(2,1)S(1)} %get-tuple-element.157), channel_id=1, source_target_pairs={{0,32},{8,40},{16,48},{24,56},{32,0},{40,8},{48,16},{56,24},{64,96... | collective-permute-start | bytes 1966088 | tf_op jit(solution)/shard_map/ppermute | solution.py:55
  14.8 15.2 %collective-permute-start.5 = (bf16[36,32,256]{2,1,0:T(8,128)(2,1)S(1)}, bf16[36,32,256]{2,1,0:T(8,128)(2,1)S(1)}, u32[]{:S(2)}, u32[]{:S(2)}) collective-permute-start(bf16[36,32,256]{2,1,0:T(8,128)(2,1)S(1)} %get-tuple-element.159), channel_id=1, source_target_pairs={{0,1},{1,0},{2,3},{3,2},{4,5},{5,4},{6,7},{7,6},{8,9},{9,8},{10,11... | collective-permute-start | bytes 1769480 | tf_op jit(solution)/shard_map/ppermute | solution.py:54
  19.8 22.0 %copy-start.3 = (bf16[1,1,80,2,256]{4,3,2,1,0:T(2,128)(2,1)S(1)}, bf16[1,1,80,2,256]{4,3,2,1,0:T(2,128)(2,1)}, u32[]{:S(2)}) copy-start(bf16[1,1,80,2,256]{4,3,2,1,0:T(2,128)(2,1)} %param.20) | copy-start | bytes 245764
  33.2 22.9 %collective-permute-start.6 = (bf16[48,32,256]{2,1,0:T(8,128)(2,1)S(1)}, bf16[48,32,256]{2,1,0:T(8,128)(2,1)S(1)}, u32[]{:S(2)}, u32[]{:S(2)}) collective-permute-start(bf16[48,32,256]{2,1,0:T(8,128)(2,1)S(1)} %get-tuple-element.181), channel_id=1, source_target_pairs={{0,1},{1,0},{2,3},{3,2},{4,5},{5,4},{6,7},{7,6},{8,9},{9,8},{10,11... | collective-permute-start | bytes 2359304 | tf_op jit(solution)/shard_map/ppermute | solution.py:54
  35.2 20.9 %collective-permute-start.8 = (bf16[48,32,256]{2,1,0:T(8,128)(2,1)S(1)}, bf16[48,32,256]{2,1,0:T(8,128)(2,1)S(1)}, u32[]{:S(2)}, u32[]{:S(2)}) collective-permute-start(bf16[48,32,256]{2,1,0:T(8,128)(2,1)S(1)} %get-tuple-element.183), channel_id=1, source_target_pairs={{0,32},{8,40},{16,48},{24,56},{32,0},{40,8},{48,16},{56,24},{64,96... | collective-permute-start | bytes 2359304 | tf_op jit(solution)/shard_map/ppermute | solution.py:55
  37.7 18.6 %collective-permute-start.9 = (bf16[48,32,256]{2,1,0:T(8,128)(2,1)S(1)}, bf16[48,32,256]{2,1,0:T(8,128)(2,1)S(1)}, u32[]{:S(2)}, u32[]{:S(2)}) collective-permute-start(bf16[48,32,256]{2,1,0:T(8,128)(2,1)S(1)} %get-tuple-element.184), channel_id=1, source_target_pairs={{0,16},{8,24},{16,0},{24,8},{32,48},{40,56},{48,32},{56,40},{64,80... | collective-permute-start | bytes 2359304 | tf_op jit(solution)/shard_map/ppermute | solution.py:55
  39.2 16.9 %collective-permute-start.7 = (bf16[44,32,256]{2,1,0:T(8,128)(2,1)S(1)}, bf16[44,32,256]{2,1,0:T(8,128)(2,1)S(1)}, u32[]{:S(2)}, u32[]{:S(2)}) collective-permute-start(bf16[44,32,256]{2,1,0:T(8,128)(2,1)S(1)} %get-tuple-element.182), channel_id=1, source_target_pairs={{0,96},{8,104},{16,112},{24,120},{32,64},{40,72},{48,80},{56,88},{... | collective-permute-start | bytes 2162696 | tf_op jit(solution)/shard_map/ppermute | solution.py:55
  58.0 23.4 %collective-permute-start.10 = (bf16[64,32,256]{2,1,0:T(8,128)(2,1)S(1)}, bf16[64,32,256]{2,1,0:T(8,128)(2,1)S(1)}, u32[]{:S(2)}, u32[]{:S(2)}) collective-permute-start(bf16[64,32,256]{2,1,0:T(8,128)(2,1)S(1)} %get-tuple-element.205), channel_id=1, source_target_pairs={{0,96},{8,104},{16,112},{24,120},{32,64},{40,72},{48,80},{56,88},{... | collective-permute-start | bytes 3145736 | tf_op jit(solution)/shard_map/ppermute | solution.py:55
  58.1 19.3 %collective-permute-start.11 = (bf16[52,32,256]{2,1,0:T(8,128)(2,1)S(1)}, bf16[52,32,256]{2,1,0:T(8,128)(2,1)S(1)}, u32[]{:S(2)}, u32[]{:S(2)}) collective-permute-start(bf16[52,32,256]{2,1,0:T(8,128)(2,1)S(1)} %get-tuple-element.206), channel_id=1, source_target_pairs={{0,1},{1,0},{2,3},{3,2},{4,5},{5,4},{6,7},{7,6},{8,9},{9,8},{10,11... | collective-permute-start | bytes 2555912 | tf_op jit(solution)/shard_map/ppermute | solution.py:54
  58.7 19.0 %collective-permute-start.13 = (bf16[52,32,256]{2,1,0:T(8,128)(2,1)S(1)}, bf16[52,32,256]{2,1,0:T(8,128)(2,1)S(1)}, u32[]{:S(2)}, u32[]{:S(2)}) collective-permute-start(bf16[52,32,256]{2,1,0:T(8,128)(2,1)S(1)} %get-tuple-element.208), channel_id=1, source_target_pairs={{0,32},{8,40},{16,48},{24,56},{32,0},{40,8},{48,16},{56,24},{64,96... | collective-permute-start | bytes 2555912 | tf_op jit(solution)/shard_map/ppermute | solution.py:55
  60.2 17.3 %collective-permute-start.12 = (bf16[48,32,256]{2,1,0:T(8,128)(2,1)S(1)}, bf16[48,32,256]{2,1,0:T(8,128)(2,1)S(1)}, u32[]{:S(2)}, u32[]{:S(2)}) collective-permute-start(bf16[48,32,256]{2,1,0:T(8,128)(2,1)S(1)} %get-tuple-element.207), channel_id=1, source_target_pairs={{0,16},{8,24},{16,0},{24,8},{32,48},{40,56},{48,32},{56,40},{64,80... | collective-permute-start | bytes 2359304 | tf_op jit(solution)/shard_map/ppermute | solution.py:55
  85.4 27.0 %collective-permute-start.14 = (bf16[72,32,256]{2,1,0:T(8,128)(2,1)}, bf16[72,32,256]{2,1,0:T(8,128)(2,1)S(1)}, u32[]{:S(2)}, u32[]{:S(2)}) collective-permute-start(bf16[72,32,256]{2,1,0:T(8,128)(2,1)} %get-tuple-element.226), channel_id=1, source_target_pairs={{0,32},{8,40},{16,48},{24,56},{32,0},{40,8},{48,16},{56,24},{64,96... | collective-permute-start | bytes 3538952 | tf_op jit(solution)/shard_map/ppermute | solution.py:55
  87.9 25.1 %collective-permute-start.15 = (bf16[72,32,256]{2,1,0:T(8,128)(2,1)}, bf16[72,32,256]{2,1,0:T(8,128)(2,1)S(1)}, u32[]{:S(2)}, u32[]{:S(2)}) collective-permute-start(bf16[72,32,256]{2,1,0:T(8,128)(2,1)} %get-tuple-element.227), channel_id=1, source_target_pairs={{0,16},{8,24},{16,0},{24,8},{32,48},{40,56},{48,32},{56,40},{64,80... | collective-permute-start | bytes 3538952 | tf_op jit(solution)/shard_map/ppermute | solution.py:55
  88.6 23.7 %collective-permute-start.16 = (bf16[68,32,256]{2,1,0:T(8,128)(2,1)}, bf16[68,32,256]{2,1,0:T(8,128)(2,1)}, u32[]{:S(2)}, u32[]{:S(2)}) collective-permute-start(bf16[68,32,256]{2,1,0:T(8,128)(2,1)} %get-tuple-element.228), channel_id=1, source_target_pairs={{0,1},{1,0},{2,3},{3,2},{4,5},{5,4},{6,7},{7,6},{8,9},{9,8},{10,11... | collective-permute-start | bytes 3342344 | tf_op jit(solution)/shard_map/ppermute | solution.py:54
  89.4 20.9 %collective-permute-start.17 = (bf16[60,32,256]{2,1,0:T(8,128)(2,1)}, bf16[60,32,256]{2,1,0:T(8,128)(2,1)}, u32[]{:S(2)}, u32[]{:S(2)}) collective-permute-start(bf16[60,32,256]{2,1,0:T(8,128)(2,1)} %get-tuple-element.229), channel_id=1, source_target_pairs={{0,96},{8,104},{16,112},{24,120},{32,64},{40,72},{48,80},{56,88},{... | collective-permute-start | bytes 2949128 | tf_op jit(solution)/shard_map/ppermute | solution.py:55
  125.0 0.7 copy-start.6

commit v4 on v3

--- a/solution.py
+++ b/solution.py
@@ -543,27 +543,13 @@
     )(land, *boxes)
 
 
-LAND_RING = 8
-
-
 def land_kernel(given, land_ref, query_ref, own_ref, early_ref, *rest):
     contexts, rest = rest[:given], rest[given:]
     boxes, rest = rest[:4], rest[4:]
-    out_ref, landed_ref, block, result, handed, in_sems, sems, space, box_sems, out_sems = rest
+    out_ref, landed_ref, even, odd, result, handed, sems, space, box_sems, out_sems = rest
     slots = landed_ref.shape[0]
     first = out_ref.shape[0] - slots
-
-    def read(slot):
-        turn = slot % LAND_RING
-        return pltpu.make_async_copy(early_ref.at[slot], block.at[turn], in_sems.at[turn])
-
-    def write(slot):
-        turn = slot % LAND_RING
-        return pltpu.make_async_copy(block.at[turn], landed_ref.at[slot], sems.at[turn])
-
     copies = fetch([(box, space.at[pl.ds(LATE_BEGIN[q], box.shape[0])]) for q, box in enumerate(boxes)], box_sems)
-    for slot in range(4):
-        read(slot).start()
     done = 0
     pairs = []
     for context in contexts:
@@ -573,59 +559,71 @@
     for copy in copies:
         copy.wait()
 
-    def complete(slot):
-        turn = slot % LAND_RING
-        length = land_ref[LENGTH, slot]
-        for j in range(2):
-            for k in range(0, PROMPT_CHUNKS, 8):
-                held = []
-                for b in range(8):
-                    source = land_ref[LATE + PROMPT_CHUNKS * j + k + b, slot]
-                    held.append(jnp.where(source >= 0, space[jnp.maximum(source, 0)], block[turn, j, k + b]))
-                for b in range(8):
-                    block[turn, j, k + b] = held[b]
-        last = jnp.maximum(length - 1, 0) // CHUNK
-        row = last * CHUNK + lax.broadcasted_iota(jnp.int32, (CHUNK, 256), 0)
-        zero = jnp.zeros((CHUNK, 256), jnp.bfloat16)
-        for j in range(2):
-            block[turn, j, last] = jnp.where(row < length, block[turn, j, last], zero)
-
-    def body(pair, carry):
-        both = (2 * pair, 2 * pair + 1)
-
-        @pl.when(2 * pair + 4 < slots)
-        def _():
-            for slot in both:
-
-                @pl.when(slot + 4 >= LAND_RING)
-                def _():
-                    write(slot + 4).wait()
-
-                read(slot + 4).start()
-
-        for slot in both:
-            read(slot).wait()
-        for slot in both:
-            complete(slot)
-        for slot in both:
-            write(slot).start()
-        results = []
-        for slot in both:
-            blocks = [block[slot % LAND_RING, j].reshape(PROMPT_CHUNKS * CHUNK, 256) for j in range(2)]
-            results.append(
+    def write(pair, block, turn):
+        return pltpu.make_async_copy(block, landed_ref.at[pl.ds(2 * pair, 2)], sems.at[turn])
+
+    def complete(pair, block):
+        for r in range(2):
+            slot = 2 * pair + r
+            length = land_ref[LENGTH, slot]
+            for j in range(2):
+                for k in range(0, PROMPT_CHUNKS, 8):
+                    held = []
+                    for b in range(8):
+                        source = land_ref[LATE + PROMPT_CHUNKS * j + k + b, slot]
+                        before = early_ref[slot, j, k + b]
+                        held.append(jnp.where(source >= 0, space[jnp.maximum(source, 0)], before))
+                    for b in range(8):
+                        block[r, j, k + b] = held[b]
+            last = jnp.maximum(length - 1, 0) // CHUNK
+            row = last * CHUNK + lax.broadcasted_iota(jnp.int32, (CHUNK, 256), 0)
+            zero = jnp.zeros((CHUNK, 256), jnp.bfloat16)
+            for j in range(2):
+                block[r, j, last] = jnp.where(row < length, block[r, j, last], zero)
+
+    def attend(pair, block):
+        values = []
+        for r in range(2):
+            slot = 2 * pair + r
+            blocks = [block[r, j].reshape(PROMPT_CHUNKS * CHUNK, 256) for j in range(2)]
+            values.append(
                 attend_row(query_ref[first + slot], *blocks, own_ref[first + slot], land_ref[LENGTH, slot])
             )
-        for slot, value in zip(both, results):
-            result[pl.ds(16 * slot, 16)] = value
+        for r in range(2):
+            result[pl.ds(16 * (2 * pair + r), 16)] = values[r]
+
+    last = slots // 2 - 1
+    complete(0, even)
+    write(0, even, 0).start()
+
+    def body(step, carry):
+        pair = 2 * step
+
+        @pl.when(step > 0)
+        def _():
+            write(pair - 1, odd, 1).wait()
+
+        attend(pair, even)
+        complete(pair + 1, odd)
+        write(pair + 1, odd, 1).start()
+        write(pair, even, 0).wait()
+        attend(pair + 1, odd)
+        complete(pair + 2, even)
+        write(pair + 2, even, 0).start()
         return carry
 
-    lax.fori_loop(0, slots // 2, body, 0)
+    lax.fori_loop(0, last // 2, body, 0)
+    write(last - 2, odd, 1).wait()
+    attend(last - 1, even)
+    complete(last, odd)
+    write(last, odd, 1).start()
+    attend(last, odd)
     lay_rows(result, handed, 0, slots)
-    last = pltpu.make_async_copy(handed, out_ref.at[pl.ds(first, slots)], out_sems.at[len(contexts)])
-    last.start()
-    for slot in range(slots - LAND_RING, slots):
-        write(slot).wait()
-    for copy in decoded + [last]:
+    final = pltpu.make_async_copy(handed, out_ref.at[pl.ds(first, slots)], out_sems.at[len(contexts)])
+    final.start()
+    write(last - 1, even, 0).wait()
+    write(last, odd, 1).wait()
+    for copy in decoded + [final]:
         copy.wait()
 
 
@@ -636,14 +634,14 @@
             jax.ShapeDtypeStruct((queries.shape[0], 2048), jnp.bfloat16),
             jax.ShapeDtypeStruct(early.shape, jnp.bfloat16),
         ),
-        in_specs=[SMEM, VMEM, VMEM, ANY] + [VMEM] * len(contexts) + [ANY] * 4,
-        out_specs=(ANY, ANY),
+        in_specs=[SMEM, VMEM, VMEM, VMEM] + [VMEM] * len(contexts) + [ANY] * 4,
+        out_specs=(pl.BlockSpec(memory_space=pltpu.HBM),) * 2,
         scratch_shapes=[
-            pltpu.VMEM((LAND_RING,) + early.shape[1:], jnp.bfloat16),
+            pltpu.VMEM((2,) + early.shape[1:], jnp.bfloat16),
+            pltpu.VMEM((2,) + early.shape[1:], jnp.bfloat16),
             pltpu.VMEM((16 * early.shape[0], 128), jnp.float32),
             pltpu.VMEM((early.shape[0], 2048), jnp.bfloat16),
-            pltpu.SemaphoreType.DMA((LAND_RING,)),
-            pltpu.SemaphoreType.DMA((LAND_RING,)),
+            pltpu.SemaphoreType.DMA((2,)),
             pltpu.VMEM((LATE_BEGIN[4], CHUNK, 256), jnp.bfloat16),
             pltpu.SemaphoreType.DMA((4,)),
             pltpu.SemaphoreType.DMA((len(contexts) + 1,)),
@@ -672,14 +670,15 @@
     befores = before_lists(1, table, boxes)
     contexts = []
     done = 0
-    for phase, count in ((1, running // 4), (2, running // 2), (3, running // 4)):
+    for phase, count in ((1, running // 2), (2, running // 2), (3, 0)):
         table, sent, befores = lax.optimization_barrier((table, sent, befores))
         lists = lists_call(functools.partial(after_kernel, phase), "after_lists", ROOM[phase], table, *befores, *sent)
         boxes = [part + [box] for part, box in zip(boxes, sent)]
         sent = [hop(value, order[phase]) for value, order in zip(lists, ORDERS)]
         (ready, table, land), _ = lax.optimization_barrier(((half, table, land), lists))
-        contexts.append(running_rows(done, count, ready, pages, lens, queries, own, pool))
-        done += count
+        if count:
+            contexts.append(running_rows(done, count, ready, pages, lens, queries, own, pool))
+            done += count
         if phase < 3:
             befores = before_lists(phase + 1, table, boxes)
             table, _ = lax.optimization_barrier((table, contexts))

time: 126 us -> 124 us (0.984); the launches traced: 126 us -> 122 us
  Pallas kernels: 77.9 us -> 71.3 us
  waiting for transfers between devices: 23.4 us -> 25.1 us
    pallas_call x3 -> x2, Pallas kernels: 29.8 us -> 26.8 us  [running_rows(): pl.pallas_call(functools.partial(running_kernel, first), out_shape=jax.Sh...]
    pallas_call x6, Pallas kernels: 16 us -> 13.9 us  [lists_call(): pl.pallas_call(kernel, out_shape=tuple((chunks_of(room) for room in rooms...]
    ppermute x13, waiting for transfers between devices: 19.7 us -> 21.4 us  [hop(): lax.ppermute(value, 'grp', [(g, flipped(g, axis)) for g in range(lax.axis...]
    pallas_call x1, Pallas kernels: 11.1 us -> 9.5 us  [land_rows(): pl.pallas_call(functools.partial(land_kernel, len(contexts)), out_shape=(...]
    ppermute x13, starting transfers between devices: 12.6 us -> 14.3 us  [hop(): lax.ppermute(value, 'grp', [(g, flipped(g, axis)) for g in range(lax.axis...]
  transfers between devices with their start and end apart: 17 -> 17, of which waited for: 10 -> 10; matrix products, arithmetic and copies ran while one was open for 3% -> 3% of each run, Pallas kernels for 45% -> 44%
where the time goes in v4:
time: 124 us; the launch traced here: 122 us
  Pallas kernels  71.3 us (58%)
  waiting for transfers between devices  25.1 us (20%)
  starting transfers between devices  19 us (15%)
  local copies, waits for them, and re-layouts  4.67 us (4%)
    pallas_call x2, Pallas kernels, running_rows(): pl.pallas_call(functools.partial(running_kernel, first), out_shape=jax.Sh...  26.8 us
    ppermute x13, waiting for transfers between devices, hop(): lax.ppermute(value, 'grp', [(g, flipped(g, axis)) for g in range(lax.axis...  21.4 us
    ppermute x13, starting transfers between devices, hop(): lax.ppermute(value, 'grp', [(g, flipped(g, axis)) for g in range(lax.axis...  14.3 us
    pallas_call x6, Pallas kernels, lists_call(): pl.pallas_call(kernel, out_shape=tuple((chunks_of(room) for room in rooms...  13.9 us
    pallas_call x1, Pallas kernels, land_rows(): pl.pallas_call(functools.partial(land_kernel, len(contexts)), out_shape=(...  9.5 us
    pallas_call x2, Pallas kernels, plan_call(): pl.pallas_call(kernel, out_shape=tuple((jax.ShapeDtypeStruct((r, 128), jn...  8.21 us
    pallas_call x3, Pallas kernels, before_lists(): pl.pallas_call(functools.partial(before_kernel, phase), out_shape=tuple((...  7.88 us
    pallas_call x1, Pallas kernels, early_rows(): pl.pallas_call(early_kernel, out_shape=jax.ShapeDtypeStruct((slots, 2, PR...  4.92 us
  transfers between devices with their start and end apart: 17, of which 10 were waited for; matrix products, arithmetic and copies ran while one was open for 3% of the time, Pallas kernels for 44%

profile of v4, /device:TPU:16, one launch (start us, length us, event | category | flops | bytes accessed | tf_op | source)
XLA Modules:
  0.0 121.8 jit_solution(17487880798698832234)
XLA Ops:
  0.6 0.1 collective-permute-start.1
  0.8 0.7 copy-done
  1.5 1.7 %first_plan.1.table_ref = s32[8,128]{1,0:T(8,128)S(1)} custom-call(s32[3]{0:T(128)S(1)} %pad_add_fusion.where_ref, s32[1,256]{1,0:T(1,128)} %bitcast.503, s32[1,256]{1,0:T(1,128)} %bitcast.506, s32[8,64]{1,0:T(8,128)S(1)} %copy-done), custom_call_target="tpu_custom_call" | custom-call | bytes 4096 | tf_op jit(solution)/shard_map/first_plan/pallas_call | solution.py:254
  3.2 2.7 %own_lists.1 = (bf16[40,32,256]{2,1,0:T(8,128)(2,1)S(1)}, bf16[40,32,256]{2,1,0:T(8,128)(2,1)S(1)}, bf16[48,32,256]{2,1,0:T(8,128)(2,1)S(1)}, bf16[36,32,256]{2,1,0:T(8,128)(2,1)S(1)}) custom-call(s32[8,128]{1,0:T(8,128)S(1)} %first_plan.1.table_ref, bf16[256,32,256]{2,1,0:T(8,128)(2,1)} %bitcast.474), custom_call_target="tpu_custom_call" | custom-call | bytes 4096 | tf_op jit(solution)/shard_map/own_lists/pallas_call | solution.py:333
  5.9 1.0 copy.52
  7.0 0.8 copy.35
  7.8 0.1 reshape_squeeze.10.pages_ref
  7.9 0.8 reshape_squeeze.11.lens_ref
  8.7 3.0 %first_lists.1 = (bf16[40,32,256]{2,1,0:T(8,128)(2,1)S(1)}, bf16[40,32,256]{2,1,0:T(8,128)(2,1)S(1)}, bf16[48,32,256]{2,1,0:T(8,128)(2,1)S(1)}, bf16[36,32,256]{2,1,0:T(8,128)(2,1)S(1)}) custom-call(s32[8,128]{1,0:T(8,128)S(1)} %first_plan.1.table_ref, bf16[256,32,256]{2,1,0:T(8,128)(2,1)} %collective-permute-done.1.other_ref, ...), custom_call_target="tpu_custom_call" | custom-call | bytes 4096 | tf_op jit(solution)/shard_map/first_lists/pallas_call | solution.py:333
  11.7 0.5 collective-permute-start.4
  12.2 1.5 %collective-permute-start.2 = (bf16[40,32,256]{2,1,0:T(8,128)(2,1)S(1)}, bf16[40,32,256]{2,1,0:T(8,128)(2,1)S(1)}, u32[]{:S(2)}, u32[]{:S(2)}) collective-permute-start(bf16[40,32,256]{2,1,0:T(8,128)(2,1)S(1)} %get-tuple-element.155), channel_id=1, source_target_pairs={{0,16},{8,24},{16,0},{24,8},{32,48},{40,56},{48,32},{56,40},{64,80... | collective-permute-start | bytes 1966088 | tf_op jit(solution)/shard_map/ppermute | solution.py:55
  13.7 1.1 collective-permute-start.3
  14.8 1.9 %collective-permute-start.5 = (bf16[36,32,256]{2,1,0:T(8,128)(2,1)S(1)}, bf16[36,32,256]{2,1,0:T(8,128)(2,1)S(1)}, u32[]{:S(2)}, u32[]{:S(2)}) collective-permute-start(bf16[36,32,256]{2,1,0:T(8,128)(2,1)S(1)} %get-tuple-element.158), channel_id=1, source_target_pairs={{0,1},{1,0},{2,3},{3,2},{4,5},{5,4},{6,7},{7,6},{8,9},{9,8},{10,11... | collective-permute-start | bytes 1769480 | tf_op jit(solution)/shard_map/ppermute | solution.py:54
  16.7 3.1 %kept_lists.1 = (bf16[52,32,256]{2,1,0:T(8,128)(2,1)S(1)}, bf16[52,32,256]{2,1,0:T(8,128)(2,1)S(1)}, bf16[64,32,256]{2,1,0:T(8,128)(2,1)S(1)}, bf16[40,32,256]{2,1,0:T(8,128)(2,1)S(1)}) custom-call(s32[8,128]{1,0:T(8,128)S(1)} %first_plan.1.table_ref, bf16[256,32,256]{2,1,0:T(8,128)(2,1)S(1)} %bitcast.475, bf16[256,32,256]{2,1,0:T(8,128)(2,1)} %collective-permute-done.1.other_ref), custom_call_target="tpu_custom_call" | custom-call | bytes 4096 | tf_op jit(solution)/shard_map/kept_lists/pallas_call | solution.py:333
  19.8 6.5 %plan.1 = (s32[16,128]{1,0:T(8,128)S(1)}, s32[72,128]{1,0:T(8,128)S(1)}) custom-call(s32[3]{0:T(128)S(1)} %pad_add_fusion.where_ref, s32[1,256]{1,0:T(1,128)S(1)} %bitcast.504, s32[1,256]{1,0:T(1,128)S(1)} %bitcast.507, s32[8,64]{1,0:T(8,128)S(1)} %copy-done.1), custom_call_target="tpu_custom_call" | custom-call | bytes 4096 | tf_op jit(solution)/shard_map/plan/pallas_call | solution.py:254
  26.4 1.9 %before_lists.3 = (bf16[48,32,256]{2,1,0:T(8,128)(2,1)S(1)}, bf16[44,32,256]{2,1,0:T(8,128)(2,1)S(1)}, bf16[48,32,256]{2,1,0:T(8,128)(2,1)S(1)}, bf16[48,32,256]{2,1,0:T(8,128)(2,1)S(1)}) custom-call(s32[16,128]{1,0:T(8,128)S(1)} %get-tuple-element.215.table_ref, bf16[52,32,256]{2,1,0:T(8,128)(2,1)S(1)} %get-tuple-element.162.rest_0_, ...), custom_call_target="tpu_custom_call" | custom-call | bytes 4096 | tf_op jit(solution)/shard_map/before_lists/pallas_call | solution.py:367
  28.3 1.6 %collective-permute-done.5.rest_7_.rest_10_.rest_13_ = bf16[36,32,256]{2,1,0:T(8,128)(2,1)S(1)} collective-permute-done((bf16[36,32,256]{2,1,0:T(8,128)(2,1)S(1)}, bf16[36,32,256]{2,1,0:T(8,128)(2,1)S(1)}, u32[]{:S(2)}, u32[]{:S(2)}) %collective-permute-start.5) | collective-permute-done | bytes 589856 | tf_op jit(solution)/shard_map/ppermute | solution.py:54
  30.0 0.3 collective-permute-done.3.rest_5_.rest_3_.rest_4_
  30.3 1.4 %collective-permute-done.4.rest_6_.rest_5_.rest_7_.rest_9_ = bf16[48,32,256]{2,1,0:T(8,128)(2,1)S(1)} collective-permute-done((bf16[48,32,256]{2,1,0:T(8,128)(2,1)S(1)}, bf16[48,32,256]{2,1,0:T(8,128)(2,1)S(1)}, u32[]{:S(2)}, u32[]{:S(2)}) %collective-permute-start.4) | collective-permute-done | bytes 786464 | tf_op jit(solution)/shard_map/ppermute | solution.py:55
  31.7 1.5 %after_lists.3 = (bf16[48,32,256]{2,1,0:T(8,128)(2,1)S(1)}, bf16[44,32,256]{2,1,0:T(8,128)(2,1)S(1)}, bf16[48,32,256]{2,1,0:T(8,128)(2,1)S(1)}, bf16[48,32,256]{2,1,0:T(8,128)(2,1)S(1)}) custom-call(s32[16,128]{1,0:T(8,128)S(1)} %get-tuple-element.215.table_ref, bf16[48,32,256]{2,1,0:T(8,128)(2,1)S(1)} %get-tuple-element.172.rest_0_, ...), custom_call_target="tpu_custom_call" | custom-call | bytes 4096 | tf_op jit(solution)/shard_map/after_lists/pallas_call | solution.py:333
  33.2 2.0 %collective-permute-start.6 = (bf16[48,32,256]{2,1,0:T(8,128)(2,1)S(1)}, bf16[48,32,256]{2,1,0:T(8,128)(2,1)S(1)}, u32[]{:S(2)}, u32[]{:S(2)}) collective-permute-start(bf16[48,32,256]{2,1,0:T(8,128)(2,1)S(1)} %get-tuple-element.180), channel_id=1, source_target_pairs={{0,1},{1,0},{2,3},{3,2},{4,5},{5,4},{6,7},{7,6},{8,9},{9,8},{10,11... | collective-permute-start | bytes 2359304 | tf_op jit(solution)/shard_map/ppermute | solution.py:54
  35.2 2.5 %collective-permute-start.8 = (bf16[48,32,256]{2,1,0:T(8,128)(2,1)S(1)}, bf16[48,32,256]{2,1,0:T(8,128)(2,1)S(1)}, u32[]{:S(2)}, u32[]{:S(2)}) collective-permute-start(bf16[48,32,256]{2,1,0:T(8,128)(2,1)S(1)} %get-tuple-element.182), channel_id=1, source_target_pairs={{0,32},{8,40},{16,48},{24,56},{32,0},{40,8},{48,16},{56,24},{64,96... | collective-permute-start | bytes 2359304 | tf_op jit(solution)/shard_map/ppermute | solution.py:55
  37.7 1.5 %collective-permute-start.9 = (bf16[48,32,256]{2,1,0:T(8,128)(2,1)S(1)}, bf16[48,32,256]{2,1,0:T(8,128)(2,1)S(1)}, u32[]{:S(2)}, u32[]{:S(2)}) collective-permute-start(bf16[48,32,256]{2,1,0:T(8,128)(2,1)S(1)} %get-tuple-element.183), channel_id=1, source_target_pairs={{0,16},{8,24},{16,0},{24,8},{32,48},{40,56},{48,32},{56,40},{64,80... | collective-permute-start | bytes 2359304 | tf_op jit(solution)/shard_map/ppermute | solution.py:55
  39.2 2.6 %before_lists.4 = (bf16[64,32,256]{2,1,0:T(8,128)(2,1)S(1)}, bf16[52,32,256]{2,1,0:T(8,128)(2,1)S(1)}, bf16[48,32,256]{2,1,0:T(8,128)(2,1)S(1)}, bf16[52,32,256]{2,1,0:T(8,128)(2,1)S(1)}) custom-call(s32[16,128]{1,0:T(8,128)S(1)} %get-tuple-element.215.table_ref, bf16[52,32,256]{2,1,0:T(8,128)(2,1)S(1)} %get-tuple-element.162.rest_0_, ...), custom_call_target="tpu_custom_call" | custom-call | bytes 4096 | tf_op jit(solution)/shard_map/before_lists/pallas_call | solution.py:367
  41.9 13.5 %running_rows.2.rest_0_ = bf16[32,2048]{1,0:T(8,128)(2,1)S(1)} custom-call(s32[1]{0:T(128)} %bitcast.158.half_ref, s32[768]{0:T(1024)S(1)} %reshape_squeeze.10.pages_ref, s32[128]{0:T(128)S(1)} %reshape_squeeze.11.lens_ref, bf16[80,16,128]{2,1,0:T(8,128)(2,1)S(1)} %bitcast.468, bf16[80,2,256]{2,1,0:T(2,128)(2,1)S(1)} %bitcast.484, ...), custom_call_target="tpu_custom_call" | custom-call | bytes 4096 | tf_op jit(solution)/shard_map/running_rows/pallas_call | solution.py:476
  55.3 0.8 collective-permute-done.7.rest_5_.rest_6_
  56.1 0.2 collective-permute-done.9.rest_7_.rest_11_.rest_14_
  56.3 1.7 %after_lists.4 = (bf16[64,32,256]{2,1,0:T(8,128)(2,1)S(1)}, bf16[52,32,256]{2,1,0:T(8,128)(2,1)S(1)}, bf16[48,32,256]{2,1,0:T(8,128)(2,1)S(1)}, bf16[52,32,256]{2,1,0:T(8,128)(2,1)S(1)}) custom-call(s32[16,128]{1,0:T(8,128)S(1)} %get-tuple-element.215.table_ref, bf16[64,32,256]{2,1,0:T(8,128)(2,1)S(1)} %get-tuple-element.196.rest_0_, ...), custom_call_target="tpu_custom_call" | custom-call | bytes 4096 | tf_op jit(solution)/shard_map/after_lists/pallas_call | solution.py:333
  58.0 1.3 %collective-permute-start.10 = (bf16[64,32,256]{2,1,0:T(8,128)(2,1)S(1)}, bf16[64,32,256]{2,1,0:T(8,128)(2,1)S(1)}, u32[]{:S(2)}, u32[]{:S(2)}) collective-permute-start(bf16[64,32,256]{2,1,0:T(8,128)(2,1)S(1)} %get-tuple-element.204), channel_id=1, source_target_pairs={{0,96},{8,104},{16,112},{24,120},{32,64},{40,72},{48,80},{56,88},{... | collective-permute-start | bytes 3145736 | tf_op jit(solution)/shard_map/ppermute | solution.py:55
  59.2 1.2 %collective-permute-start.13 = (bf16[52,32,256]{2,1,0:T(8,128)(2,1)S(1)}, bf16[52,32,256]{2,1,0:T(8,128)(2,1)S(1)}, u32[]{:S(2)}, u32[]{:S(2)}) collective-permute-start(bf16[52,32,256]{2,1,0:T(8,128)(2,1)S(1)} %get-tuple-element.207), channel_id=1, source_target_pairs={{0,32},{8,40},{16,48},{24,56},{32,0},{40,8},{48,16},{56,24},{64,96... | collective-permute-start | bytes 2555912 | tf_op jit(solution)/shard_map/ppermute | solution.py:55
  60.5 0.6 collective-permute-start.12
  61.1 3.3 %before_lists.5 = (bf16[72,32,256]{2,1,0:T(8,128)(2,1)S(1)}, bf16[72,32,256]{2,1,0:T(8,128)(2,1)S(1)}, bf16[68,32,256]{2,1,0:T(8,128)(2,1)S(1)}, bf16[60,32,256]{2,1,0:T(8,128)(2,1)S(1)}) custom-call(s32[16,128]{1,0:T(8,128)S(1)} %get-tuple-element.215.table_ref, bf16[52,32,256]{2,1,0:T(8,128)(2,1)S(1)} %get-tuple-element.162.rest_0_, ...), custom_call_target="tpu_custom_call" | custom-call | bytes 4096 | tf_op jit(solution)/shard_map/before_lists/pallas_call | solution.py:367
  64.4 13.4 %running_rows.3.rest_1_ = bf16[32,2048]{1,0:T(8,128)(2,1)S(1)} custom-call(s32[1]{0:T(128)} %bitcast.158.half_ref, s32[768]{0:T(1024)S(1)} %reshape_squeeze.10.pages_ref, s32[128]{0:T(128)S(1)} %reshape_squeeze.11.lens_ref, bf16[80,16,128]{2,1,0:T(8,128)(2,1)S(1)} %bitcast.469, bf16[80,2,256]{2,1,0:T(2,128)(2,1)S(1)} %bitcast.485, ...), custom_call_target="tpu_custom_call" | custom-call | bytes 4096 | tf_op jit(solution)/shard_map/running_rows/pallas_call | solution.py:476
  77.8 0.8 collective-permute-done.12.rest_6_.rest_11_
  78.6 2.7 %collective-permute-done.10.rest_4_.rest_3_ = bf16[64,32,256]{2,1,0:T(8,128)(2,1)S(1)} collective-permute-done((bf16[64,32,256]{2,1,0:T(8,128)(2,1)S(1)}, bf16[64,32,256]{2,1,0:T(8,128)(2,1)S(1)}, u32[]{:S(2)}, u32[]{:S(2)}) %collective-permute-start.10) | collective-permute-done | bytes 1048608 | tf_op jit(solution)/shard_map/ppermute | solution.py:55
  81.3 1.9 %after_lists.5 = (bf16[72,32,256]{2,1,0:T(8,128)(2,1)S(1)}, bf16[72,32,256]{2,1,0:T(8,128)(2,1)S(1)}, bf16[68,32,256]{2,1,0:T(8,128)(2,1)S(1)}, bf16[60,32,256]{2,1,0:T(8,128)(2,1)S(1)}) custom-call(s32[16,128]{1,0:T(8,128)S(1)} %get-tuple-element.215.table_ref, bf16[72,32,256]{2,1,0:T(8,128)(2,1)S(1)} %get-tuple-element.217.rest_0_, ...), custom_call_target="tpu_custom_call" | custom-call | bytes 4096 | tf_op jit(solution)/shard_map/after_lists/pallas_call | solution.py:333
  83.2 2.6 %collective-permute-start.14 = (bf16[72,32,256]{2,1,0:T(8,128)(2,1)S(1)}, bf16[72,32,256]{2,1,0:T(8,128)(2,1)S(1)}, u32[]{:S(2)}, u32[]{:S(2)}) collective-permute-start(bf16[72,32,256]{2,1,0:T(8,128)(2,1)S(1)} %get-tuple-element.225), channel_id=1, source_target_pairs={{0,32},{8,40},{16,48},{24,56},{32,0},{40,8},{48,16},{56,24},{64,96... | collective-permute-start | bytes 3538952 | tf_op jit(solution)/shard_map/ppermute | solution.py:55
  85.9 0.7 collective-permute-start.15
  86.6 0.8 collective-permute-start.16
  87.4 0.7 collective-permute-start.17
  88.0 4.9 %early_rows.1.early_ref = bf16[16,2,16,32,256]{4,3,2,1,0:T(8,128)(2,1)S(1)} custom-call(s32[72,128]{1,0:T(8,128)S(1)} %get-tuple-element.229.land_ref, bf16[52,32,256]{2,1,0:T(8,128)(2,1)S(1)} %get-tuple-element.162.rest_0_, bf16[40,32,256]{2,1,0:T(8,128)(2,1)S(1)} %collective-permute-done.2.rest_4_.rest_1_, ...), custom_call_target="tpu_custom_call" | custom-call | bytes 4096 | tf_op jit(solution)/shard_map/early_rows/pallas_call | solution.py:529
  93.0 0.5 slice.796
  93.5 14.5 %collective-permute-done.17.rest_5_ = bf16[60,32,256]{2,1,0:T(8,128)(2,1)S(1)} collective-permute-done((bf16[60,32,256]{2,1,0:T(8,128)(2,1)S(1)}, bf16[60,32,256]{2,1,0:T(8,128)(2,1)S(1)}, u32[]{:S(2)}, u32[]{:S(2)}) %collective-permute-start.17) | collective-permute-done | bytes 983072 | tf_op jit(solution)/shard_map/ppermute | solution.py:55
  108.0 2.0 %collective-permute-done.16.rest_4_ = bf16[68,32,256]{2,1,0:T(8,128)(2,1)S(1)} collective-permute-done((bf16[68,32,256]{2,1,0:T(8,128)(2,1)S(1)}, bf16[68,32,256]{2,1,0:T(8,128)(2,1)S(1)}, u32[]{:S(2)}, u32[]{:S(2)}) %collective-permute-start.16) | collective-permute-done | bytes 1114144 | tf_op jit(solution)/shard_map/ppermute | solution.py:54
  110.0 0.7 collective-permute-done.15.rest_3_
  110.7 9.5 %land_rows.1 = (bf16[80,2048]{1,0:T(8,128)(2,1)S(1)}, bf16[16,2,16,32,256]{4,3,2,1,0:T(8,128)(2,1)}) custom-call(s32[72,128]{1,0:T(8,128)S(1)} %get-tuple-element.229.land_ref, bf16[80,16,128]{2,1,0:T(8,128)(2,1)S(1)} %bitcast.470, bf16[80,2,256]{2,1,0:T(2,128)(2,1)S(1)} %bitcast.486, bf16[16,2,16,32,256]{4,3,2,1,0:T(8,128)(2,1)S(1)} %early_rows.1.early_ref, ...), custom_call_target="tpu_custom_call" | custom-call | bytes 4096 | tf_op jit(solution)/shard_map/land_rows/pallas_call | solution.py:631
  120.2 0.9 while.12
  121.1 0.7 copy-done.6
  (22 shorter events, 0.2 us)
Async XLA Ops:
  0.6 8.1 %collective-permute-start.1 = (bf16[256,32,256]{2,1,0:T(8,128)(2,1)}, bf16[256,32,256]{2,1,0:T(8,128)(2,1)}, u32[]{:S(2)}, u32[]{:S(2)}) collective-permute-start(bf16[256,32,256]{2,1,0:T(8,128)(2,1)} %bitcast.473), channel_id=1, source_target_pairs={{0,8},{8,0},{16,24},{24,16},{32,40},{40,32},{48,56},{56,48},{64,72... | collective-permute-start | bytes 12582920 | tf_op jit(solution)/shard_map/ppermute | solution.py:55
  0.8 0.7 copy-start
  5.9 13.9 %copy-start.1 = (s32[8,64]{1,0:T(8,128)S(1)}, s32[8,64]{1,0:T(8,128)}, u32[]{:S(2)}) copy-start(s32[8,64]{1,0:T(8,128)} %constant.173.clone.const_ref) | copy-start | bytes 6148
  5.9 13.9 %copy-start.4 = (s32[256]{0:T(256)S(1)}, s32[256]{0:T(256)}, u32[]{:S(2)}) copy-start(s32[256]{0:T(256)} %param.13) | copy-start | bytes 3076
  5.9 13.9 %copy-start.5 = (s32[256]{0:T(256)S(1)}, s32[256]{0:T(256)}, u32[]{:S(2)}) copy-start(s32[256]{0:T(256)} %param.14) | copy-start | bytes 3076
  8.7 8.0 %copy-start.2 = (bf16[16,1,512,256]{3,2,1,0:T(8,128)(2,1)S(1)}, bf16[16,1,512,256]{3,2,1,0:T(8,128)(2,1)}, u32[]{:S(2)}) copy-start(bf16[16,1,512,256]{3,2,1,0:T(8,128)(2,1)} %param.15) | copy-start | bytes 12582916
  11.7 20.0 %collective-permute-start.4 = (bf16[48,32,256]{2,1,0:T(8,128)(2,1)S(1)}, bf16[48,32,256]{2,1,0:T(8,128)(2,1)S(1)}, u32[]{:S(2)}, u32[]{:S(2)}) collective-permute-start(bf16[48,32,256]{2,1,0:T(8,128)(2,1)S(1)} %get-tuple-element.157), channel_id=1, source_target_pairs={{0,96},{8,104},{16,112},{24,120},{32,64},{40,72},{48,80},{56,88},{... | collective-permute-start | bytes 2359304 | tf_op jit(solution)/shard_map/ppermute | solution.py:55
  12.2 17.7 %collective-permute-start.2 = (bf16[40,32,256]{2,1,0:T(8,128)(2,1)S(1)}, bf16[40,32,256]{2,1,0:T(8,128)(2,1)S(1)}, u32[]{:S(2)}, u32[]{:S(2)}) collective-permute-start(bf16[40,32,256]{2,1,0:T(8,128)(2,1)S(1)} %get-tuple-element.155), channel_id=1, source_target_pairs={{0,16},{8,24},{16,0},{24,8},{32,48},{40,56},{48,32},{56,40},{64,80... | collective-permute-start | bytes 1966088 | tf_op jit(solution)/shard_map/ppermute | solution.py:55
  13.7 16.5 %collective-permute-start.3 = (bf16[40,32,256]{2,1,0:T(8,128)(2,1)S(1)}, bf16[40,32,256]{2,1,0:T(8,128)(2,1)S(1)}, u32[]{:S(2)}, u32[]{:S(2)}) collective-permute-start(bf16[40,32,256]{2,1,0:T(8,128)(2,1)S(1)} %get-tuple-element.156), channel_id=1, source_target_pairs={{0,32},{8,40},{16,48},{24,56},{32,0},{40,8},{48,16},{56,24},{64,96... | collective-permute-start | bytes 1966088 | tf_op jit(solution)/shard_map/ppermute | solution.py:55
  14.8 15.2 %collective-permute-start.5 = (bf16[36,32,256]{2,1,0:T(8,128)(2,1)S(1)}, bf16[36,32,256]{2,1,0:T(8,128)(2,1)S(1)}, u32[]{:S(2)}, u32[]{:S(2)}) collective-permute-start(bf16[36,32,256]{2,1,0:T(8,128)(2,1)S(1)} %get-tuple-element.158), channel_id=1, source_target_pairs={{0,1},{1,0},{2,3},{3,2},{4,5},{5,4},{6,7},{7,6},{8,9},{9,8},{10,11... | collective-permute-start | bytes 1769480 | tf_op jit(solution)/shard_map/ppermute | solution.py:54
  19.8 22.0 %copy-start.3 = (bf16[1,1,80,2,256]{4,3,2,1,0:T(2,128)(2,1)S(1)}, bf16[1,1,80,2,256]{4,3,2,1,0:T(2,128)(2,1)}, u32[]{:S(2)}) copy-start(bf16[1,1,80,2,256]{4,3,2,1,0:T(2,128)(2,1)} %param.20) | copy-start | bytes 245764
  33.2 22.9 %collective-permute-start.6 = (bf16[48,32,256]{2,1,0:T(8,128)(2,1)S(1)}, bf16[48,32,256]{2,1,0:T(8,128)(2,1)S(1)}, u32[]{:S(2)}, u32[]{:S(2)}) collective-permute-start(bf16[48,32,256]{2,1,0:T(8,128)(2,1)S(1)} %get-tuple-element.180), channel_id=1, source_target_pairs={{0,1},{1,0},{2,3},{3,2},{4,5},{5,4},{6,7},{7,6},{8,9},{9,8},{10,11... | collective-permute-start | bytes 2359304 | tf_op jit(solution)/shard_map/ppermute | solution.py:54
  35.2 20.9 %collective-permute-start.8 = (bf16[48,32,256]{2,1,0:T(8,128)(2,1)S(1)}, bf16[48,32,256]{2,1,0:T(8,128)(2,1)S(1)}, u32[]{:S(2)}, u32[]{:S(2)}) collective-permute-start(bf16[48,32,256]{2,1,0:T(8,128)(2,1)S(1)} %get-tuple-element.182), channel_id=1, source_target_pairs={{0,32},{8,40},{16,48},{24,56},{32,0},{40,8},{48,16},{56,24},{64,96... | collective-permute-start | bytes 2359304 | tf_op jit(solution)/shard_map/ppermute | solution.py:55
  37.7 18.6 %collective-permute-start.9 = (bf16[48,32,256]{2,1,0:T(8,128)(2,1)S(1)}, bf16[48,32,256]{2,1,0:T(8,128)(2,1)S(1)}, u32[]{:S(2)}, u32[]{:S(2)}) collective-permute-start(bf16[48,32,256]{2,1,0:T(8,128)(2,1)S(1)} %get-tuple-element.183), channel_id=1, source_target_pairs={{0,16},{8,24},{16,0},{24,8},{32,48},{40,56},{48,32},{56,40},{64,80... | collective-permute-start | bytes 2359304 | tf_op jit(solution)/shard_map/ppermute | solution.py:55
  39.2 16.9 %collective-permute-start.7 = (bf16[44,32,256]{2,1,0:T(8,128)(2,1)S(1)}, bf16[44,32,256]{2,1,0:T(8,128)(2,1)S(1)}, u32[]{:S(2)}, u32[]{:S(2)}) collective-permute-start(bf16[44,32,256]{2,1,0:T(8,128)(2,1)S(1)} %get-tuple-element.181), channel_id=1, source_target_pairs={{0,96},{8,104},{16,112},{24,120},{32,64},{40,72},{48,80},{56,88},{... | collective-permute-start | bytes 2162696 | tf_op jit(solution)/shard_map/ppermute | solution.py:55
  58.0 23.4 %collective-permute-start.10 = (bf16[64,32,256]{2,1,0:T(8,128)(2,1)S(1)}, bf16[64,32,256]{2,1,0:T(8,128)(2,1)S(1)}, u32[]{:S(2)}, u32[]{:S(2)}) collective-permute-start(bf16[64,32,256]{2,1,0:T(8,128)(2,1)S(1)} %get-tuple-element.204), channel_id=1, source_target_pairs={{0,96},{8,104},{16,112},{24,120},{32,64},{40,72},{48,80},{56,88},{... | collective-permute-start | bytes 3145736 | tf_op jit(solution)/shard_map/ppermute | solution.py:55
  59.2 19.3 %collective-permute-start.11 = (bf16[52,32,256]{2,1,0:T(8,128)(2,1)S(1)}, bf16[52,32,256]{2,1,0:T(8,128)(2,1)S(1)}, u32[]{:S(2)}, u32[]{:S(2)}) collective-permute-start(bf16[52,32,256]{2,1,0:T(8,128)(2,1)S(1)} %get-tuple-element.205), channel_id=1, source_target_pairs={{0,1},{1,0},{2,3},{3,2},{4,5},{5,4},{6,7},{7,6},{8,9},{9,8},{10,11... | collective-permute-start | bytes 2555912 | tf_op jit(solution)/shard_map/ppermute | solution.py:54
  59.2 19.3 %collective-permute-start.13 = (bf16[52,32,256]{2,1,0:T(8,128)(2,1)S(1)}, bf16[52,32,256]{2,1,0:T(8,128)(2,1)S(1)}, u32[]{:S(2)}, u32[]{:S(2)}) collective-permute-start(bf16[52,32,256]{2,1,0:T(8,128)(2,1)S(1)} %get-tuple-element.207), channel_id=1, source_target_pairs={{0,32},{8,40},{16,48},{24,56},{32,0},{40,8},{48,16},{56,24},{64,96... | collective-permute-start | bytes 2555912 | tf_op jit(solution)/shard_map/ppermute | solution.py:55
  60.5 18.1 %collective-permute-start.12 = (bf16[48,32,256]{2,1,0:T(8,128)(2,1)S(1)}, bf16[48,32,256]{2,1,0:T(8,128)(2,1)S(1)}, u32[]{:S(2)}, u32[]{:S(2)}) collective-permute-start(bf16[48,32,256]{2,1,0:T(8,128)(2,1)S(1)} %get-tuple-element.206), channel_id=1, source_target_pairs={{0,16},{8,24},{16,0},{24,8},{32,48},{40,56},{48,32},{56,40},{64,80... | collective-permute-start | bytes 2359304 | tf_op jit(solution)/shard_map/ppermute | solution.py:55
  83.2 26.7 %collective-permute-start.14 = (bf16[72,32,256]{2,1,0:T(8,128)(2,1)S(1)}, bf16[72,32,256]{2,1,0:T(8,128)(2,1)S(1)}, u32[]{:S(2)}, u32[]{:S(2)}) collective-permute-start(bf16[72,32,256]{2,1,0:T(8,128)(2,1)S(1)} %get-tuple-element.225), channel_id=1, source_target_pairs={{0,32},{8,40},{16,48},{24,56},{32,0},{40,8},{48,16},{56,24},{64,96... | collective-permute-start | bytes 3538952 | tf_op jit(solution)/shard_map/ppermute | solution.py:55
  85.9 24.9 %collective-permute-start.15 = (bf16[72,32,256]{2,1,0:T(8,128)(2,1)S(1)}, bf16[72,32,256]{2,1,0:T(8,128)(2,1)S(1)}, u32[]{:S(2)}, u32[]{:S(2)}) collective-permute-start(bf16[72,32,256]{2,1,0:T(8,128)(2,1)S(1)} %get-tuple-element.226), channel_id=1, source_target_pairs={{0,16},{8,24},{16,0},{24,8},{32,48},{40,56},{48,32},{56,40},{64,80... | collective-permute-start | bytes 3538952 | tf_op jit(solution)/shard_map/ppermute | solution.py:55
  86.6 23.4 %collective-permute-start.16 = (bf16[68,32,256]{2,1,0:T(8,128)(2,1)S(1)}, bf16[68,32,256]{2,1,0:T(8,128)(2,1)S(1)}, u32[]{:S(2)}, u32[]{:S(2)}) collective-permute-start(bf16[68,32,256]{2,1,0:T(8,128)(2,1)S(1)} %get-tuple-element.227), channel_id=1, source_target_pairs={{0,1},{1,0},{2,3},{3,2},{4,5},{5,4},{6,7},{7,6},{8,9},{9,8},{10,11... | collective-permute-start | bytes 3342344 | tf_op jit(solution)/shard_map/ppermute | solution.py:54
  87.4 20.6 %collective-permute-start.17 = (bf16[60,32,256]{2,1,0:T(8,128)(2,1)S(1)}, bf16[60,32,256]{2,1,0:T(8,128)(2,1)S(1)}, u32[]{:S(2)}, u32[]{:S(2)}) collective-permute-start(bf16[60,32,256]{2,1,0:T(8,128)(2,1)S(1)} %get-tuple-element.228), channel_id=1, source_target_pairs={{0,96},{8,104},{16,112},{24,120},{32,64},{40,72},{48,80},{56,88},{... | collective-permute-start | bytes 2949128 | tf_op jit(solution)/shard_map/ppermute | solution.py:55
  121.1 0.7 copy-start.6

commit v5 on v4

--- a/solution.py
+++ b/solution.py
@@ -17,7 +17,7 @@
 ORDERS = ((X, Z, YB, YA), (YA, YB, Z, X), (YB, YA, X, Z), (Z, X, YA, YB))
 DEAL = (2, 0, 1, 3, 2, 0, 1, 2, 3, 0, 1, 2, 0, 1, 3, 2)
 SHARES = tuple(sum(1 << k for k, part in enumerate(DEAL) if part == q) for q in range(4))
-ROOM = ((40, 40, 48, 36), (48, 44, 48, 48), (64, 52, 48, 52), (72, 72, 68, 60))
+ROOM = ((38, 41, 47, 36), (44, 36, 50, 48), (64, 52, 47, 53), (72, 68, 63, 56))
 MIB = 1024 * 1024
 SMALL = 4096
 
@@ -112,7 +112,7 @@
 SENT, RECEIVED, SLOTS, HELD = 0, 16, 32, 36
 
 
-def first_plan_kernel(where_ref, targets_ref, lens_ref, const_ref, table_ref):
+def first_plan_kernel(where_ref, targets_ref, lens_ref, table_ref):
     me, group = where_ref[0], where_ref[2]
     local = lax.broadcasted_iota(jnp.int32, (32, 1), 0)
     prompt = 16 * (group & ~1) + local
@@ -120,8 +120,9 @@
     targets = jnp.sum(jnp.where(match, targets_ref[...], 0), axis=1, keepdims=True)
     lens = jnp.sum(jnp.where(match, lens_ref[...], 0), axis=1, keepdims=True)
     start, ways = ends_of(targets, prompt, (me >> 3) & 1)
-    bit, share = const_ref[1:2, :], const_ref[3:4, :]
     lane = lax.broadcasted_iota(jnp.int32, (1, 64), 1)
+    bit = sum(jnp.where(lane == q, ORDERS[q][0], 0) for q in range(4))
+    share = sum(jnp.where((lane == q) | (lane == HELD + q), SHARES[q], 0) for q in range(4))
     word = turned(share, (prompt * 5) & 15) & below((lens + (CHUNK - 1)) >> 5)
     goes = (lane < 4) & ((ways & bit) != 0) | (lane >= HELD) & (lane < HELD + 4)
     goes = goes & (start == me)
@@ -254,9 +255,9 @@
     return pl.pallas_call(
         kernel,
         out_shape=tuple(jax.ShapeDtypeStruct((r, 128), jnp.int32) for r in rows),
-        in_specs=[pl.BlockSpec(memory_space=pltpu.SMEM), vmem, vmem, vmem],
+        in_specs=[pl.BlockSpec(memory_space=pltpu.SMEM)] + [vmem] * (len(operands) - 1),
         out_specs=(vmem,) * len(rows),
-        compiler_params=pltpu.CompilerParams(vmem_limit_bytes=24 * MIB),
+        compiler_params=pltpu.CompilerParams(vmem_limit_bytes=12 * MIB),
         cost_estimate=cost(SMALL),
         name=name,
     )(*operands)
@@ -335,7 +336,7 @@
         out_shape=tuple(chunks_of(room) for room in rooms),
         in_specs=[SMEM] + [VMEM] * len(operands),
         out_specs=(VMEM,) * 4,
-        compiler_params=pltpu.CompilerParams(vmem_limit_bytes=28 * MIB),
+        compiler_params=pltpu.CompilerParams(vmem_limit_bytes=18 * MIB),
         cost_estimate=cost(SMALL),
         name=name,
     )(table, *operands)
@@ -428,8 +429,12 @@
 DEPTH = 4 * TOGETHER
 
 
-def running_kernel(first, half_ref, pages_ref, lens_ref, query_ref, own_ref, pool_ref, out_ref, held, result, sems):
-    rows = out_ref.shape[0]
+def running_kernel(first, rows, given, half_ref, pages_ref, lens_ref, query_ref, own_ref, pool_ref, *rest):
+    befores, outs, (held, result, sems) = rest[:given], rest[given:-3], rest[-3:]
+    begin_row = 0
+    for before in befores:
+        result[0 : before.shape[0]] = before[...]
+        begin_row = before.shape[0] // 16
     all_rows = lens_ref.shape[0] // 2
     max_pages = held.shape[1]
     start = half_ref[0] * all_rows + first
@@ -464,29 +469,37 @@
                 attend_row(query_ref[first + row], *blocks, own_ref[first + row], lens_ref[start + row])
             )
         for r in range(TOGETHER):
-            result[pl.ds((group * TOGETHER + r) * 16, 16)] = results[r]
+            result[pl.ds((begin_row + group * TOGETHER + r) * 16, 16)] = results[r]
         return carry
 
     lax.fori_loop(0, rows // TOGETHER, body, 0)
-    lay_rows(result, out_ref, 0, rows)
-
-
-def running_rows(first, count, half, pages, lens, queries, own, pool):
+    laid = outs[0].shape[0]
+    lay_rows(result, outs[0], 0, laid)
+    for rest_ref in outs[1:]:
+        rest_ref[...] = result[16 * laid :]
+
+
+def running_rows(first, count, befores, half, pages, lens, queries, own, pool):
+    total = count + sum(b.shape[0] for b in befores) // 16
+    left = total % 16
+    shapes = [jax.ShapeDtypeStruct((total - left, 2048), jnp.bfloat16)]
+    if left:
+        shapes.append(jax.ShapeDtypeStruct((16 * left, 128), jnp.float32))
     max_pages = pages.shape[0] // lens.shape[0]
     return pl.pallas_call(
-        functools.partial(running_kernel, first),
-        out_shape=jax.ShapeDtypeStruct((count, 2048), jnp.bfloat16),
-        in_specs=[SMEM, SMEM, SMEM, VMEM, VMEM, pl.BlockSpec(memory_space=pltpu.HBM)],
-        out_specs=VMEM,
+        functools.partial(running_kernel, first, count, len(befores)),
+        out_shape=tuple(shapes),
+        in_specs=[SMEM, SMEM, SMEM, VMEM, VMEM, ANY] + [VMEM] * len(befores),
+        out_specs=(VMEM,) * len(shapes),
         scratch_shapes=[
             pltpu.VMEM((DEPTH, max_pages) + pool.shape[1:], jnp.bfloat16),
-            pltpu.VMEM((count * 16, 128), jnp.float32),
+            pltpu.VMEM((total * 16, 128), jnp.float32),
             pltpu.SemaphoreType.DMA((DEPTH, max_pages)),
         ],
         compiler_params=pltpu.CompilerParams(vmem_limit_bytes=40 * MIB),
         cost_estimate=cost(SMALL),
         name="running_rows",
-    )(half, pages, lens, queries, own, pool)
+    )(half, pages, lens, queries, own, pool, *befores)
 
 
 RING = 4
@@ -657,7 +670,7 @@
     rows = queries.shape[0]
     pages, lens = pages.reshape(-1), lens.reshape(-1)
     other = hop(kv, CORE)
-    (table,) = plan_call(first_plan_kernel, "first_plan", (8,), *operands)
+    (table,) = plan_call(first_plan_kernel, "first_plan", (8,), *operands[:3])
     lists = lists_call(own_kernel, "own_lists", ROOM[0], table, kv)
     queries = queries.reshape(rows, 16, 128)
     lists, other, queries, pages, lens = lax.optimization_barrier((lists, other, queries, pages, lens))
@@ -668,16 +681,17 @@
     table, land = plan_call(plan_kernel, "plan", (16, 72), where, *operands[1:])
     boxes = [[k] for k in kept]
     befores = before_lists(1, table, boxes)
-    contexts = []
+    contexts, left = [], []
     done = 0
-    for phase, count in ((1, running // 2), (2, running // 2), (3, 0)):
+    for phase, count in ((1, running * 3 // 8), (2, running * 5 // 8), (3, 0)):
         table, sent, befores = lax.optimization_barrier((table, sent, befores))
         lists = lists_call(functools.partial(after_kernel, phase), "after_lists", ROOM[phase], table, *befores, *sent)
         boxes = [part + [box] for part, box in zip(boxes, sent)]
         sent = [hop(value, order[phase]) for value, order in zip(lists, ORDERS)]
         (ready, table, land), _ = lax.optimization_barrier(((half, table, land), lists))
         if count:
-            contexts.append(running_rows(done, count, ready, pages, lens, queries, own, pool))
+            context, *left = running_rows(done, count, left, ready, pages, lens, queries, own, pool)
+            contexts.append(context)
             done += count
         if phase < 3:
             befores = before_lists(phase + 1, table, boxes)

time: 124 us -> 120 us (0.968)
  waiting for transfers between devices: 25.1 us -> 19.2 us
  starting transfers between devices: 19 us -> 20.6 us
    ppermute x13, waiting for transfers between devices: 21.4 us -> 15.4 us  [hop(): lax.ppermute(value, 'grp', [(g, flipped(g, axis)) for g in range(lax.axis...]
    ppermute x4, starting transfers between devices: 4.71 us -> 7.04 us  [hop(): lax.ppermute(value, 'tp', [(t, t ^ 1) for t in range(lax.axis_size('tp'))])]
    unnamed x16 -> x14, local copies, waits for them, and re-layouts: 3.26 us -> 2.57 us
  transfers between devices with their start and end apart: 17 -> 17, of which waited for: 10 -> 9; matrix products, arithmetic and copies ran while one was open for 3% -> 3% of each run, Pallas kernels for 44% -> 47%
where the time goes in v5:
time: 120 us; the launch traced here: 118 us
  Pallas kernels  72.3 us (60%)
  starting transfers between devices  20.6 us (17%)
  waiting for transfers between devices  19.2 us (16%)
  local copies, waits for them, and re-layouts  3.98 us (3%)
    pallas_call x2, Pallas kernels, running_rows(): pl.pallas_call(functools.partial(running_kernel, first, count, len(before...  26.8 us
    ppermute x13, waiting for transfers between devices, hop(): lax.ppermute(value, 'grp', [(g, flipped(g, axis)) for g in range(lax.axis...  15.4 us
    pallas_call x6, Pallas kernels, lists_call(): pl.pallas_call(kernel, out_shape=tuple((chunks_of(room) for room in rooms...  13.7 us
    ppermute x13, starting transfers between devices, hop(): lax.ppermute(value, 'grp', [(g, flipped(g, axis)) for g in range(lax.axis...  13.6 us
    pallas_call x1, Pallas kernels, land_rows(): pl.pallas_call(functools.partial(land_kernel, len(contexts)), out_shape=(...  9.52 us
    pallas_call x3, Pallas kernels, before_lists(): pl.pallas_call(functools.partial(before_kernel, phase), out_shape=tuple((...  8.44 us
    pallas_call x2, Pallas kernels, plan_call(): pl.pallas_call(kernel, out_shape=tuple((jax.ShapeDtypeStruct((r, 128), jn...  8.21 us
    ppermute x4, starting transfers between devices, hop(): lax.ppermute(value, 'tp', [(t, t ^ 1) for t in range(lax.axis_size('tp'))])  7.04 us
  transfers between devices with their start and end apart: 17, of which 9 were waited for; matrix products, arithmetic and copies ran while one was open for 3% of the time, Pallas kernels for 47%

profile of v5, /device:TPU:16, one launch (start us, length us, event | category | flops | bytes accessed | tf_op | source)
XLA Modules:
  0.0 117.8 jit_solution(11791167035187731525)
XLA Ops:
  0.6 0.1 collective-permute-start.1
  0.7 0.1 pad_add_fusion.where_ref
  0.8 1.7 %first_plan.1.table_ref = s32[8,128]{1,0:T(8,128)S(1)} custom-call(s32[3]{0:T(128)S(1)} %pad_add_fusion.where_ref, s32[1,256]{1,0:T(1,128)} %bitcast.503, s32[1,256]{1,0:T(1,128)} %bitcast.506), custom_call_target="tpu_custom_call" | custom-call | bytes 4096 | tf_op jit(solution)/shard_map/first_plan/pallas_call | solution.py:255
  2.5 2.7 %own_lists.1 = (bf16[38,32,256]{2,1,0:T(8,128)(2,1)S(1)}, bf16[41,32,256]{2,1,0:T(8,128)(2,1)S(1)}, bf16[47,32,256]{2,1,0:T(8,128)(2,1)S(1)}, bf16[36,32,256]{2,1,0:T(8,128)(2,1)S(1)}) custom-call(s32[8,128]{1,0:T(8,128)S(1)} %first_plan.1.table_ref, bf16[256,32,256]{2,1,0:T(8,128)(2,1)} %bitcast.474), custom_call_target="tpu_custom_call" | custom-call | bytes 4096 | tf_op jit(solution)/shard_map/own_lists/pallas_call | solution.py:334
  5.2 1.0 copy.52
  6.3 0.8 copy.35
  7.1 0.1 reshape_squeeze.10.pages_ref
  7.2 0.8 reshape_squeeze.11.lens_ref
  8.0 0.2 collective-permute-done.1.other_ref
  8.2 3.0 %first_lists.1 = (bf16[38,32,256]{2,1,0:T(8,128)(2,1)S(1)}, bf16[41,32,256]{2,1,0:T(8,128)(2,1)S(1)}, bf16[47,32,256]{2,1,0:T(8,128)(2,1)S(1)}, bf16[36,32,256]{2,1,0:T(8,128)(2,1)S(1)}) custom-call(s32[8,128]{1,0:T(8,128)S(1)} %first_plan.1.table_ref, bf16[256,32,256]{2,1,0:T(8,128)(2,1)} %collective-permute-done.1.other_ref, ...), custom_call_target="tpu_custom_call" | custom-call | bytes 4096 | tf_op jit(solution)/shard_map/first_lists/pallas_call | solution.py:334
  11.2 0.5 collective-permute-start.4
  11.7 1.0 collective-permute-start.3
  12.7 1.6 %collective-permute-start.2 = (bf16[38,32,256]{2,1,0:T(8,128)(2,1)S(1)}, bf16[38,32,256]{2,1,0:T(8,128)(2,1)S(1)}, u32[]{:S(2)}, u32[]{:S(2)}) collective-permute-start(bf16[38,32,256]{2,1,0:T(8,128)(2,1)S(1)} %get-tuple-element.157), channel_id=1, source_target_pairs={{0,16},{8,24},{16,0},{24,8},{32,48},{40,56},{48,32},{56,40},{64,80... | collective-permute-start | bytes 1867784 | tf_op jit(solution)/shard_map/ppermute | solution.py:55
  14.3 1.9 %collective-permute-start.5 = (bf16[36,32,256]{2,1,0:T(8,128)(2,1)S(1)}, bf16[36,32,256]{2,1,0:T(8,128)(2,1)S(1)}, u32[]{:S(2)}, u32[]{:S(2)}) collective-permute-start(bf16[36,32,256]{2,1,0:T(8,128)(2,1)S(1)} %get-tuple-element.160), channel_id=1, source_target_pairs={{0,1},{1,0},{2,3},{3,2},{4,5},{5,4},{6,7},{7,6},{8,9},{9,8},{10,11... | collective-permute-start | bytes 1769480 | tf_op jit(solution)/shard_map/ppermute | solution.py:54
  16.2 3.1 %kept_lists.1 = (bf16[52,32,256]{2,1,0:T(8,128)(2,1)S(1)}, bf16[52,32,256]{2,1,0:T(8,128)(2,1)S(1)}, bf16[64,32,256]{2,1,0:T(8,128)(2,1)S(1)}, bf16[40,32,256]{2,1,0:T(8,128)(2,1)S(1)}) custom-call(s32[8,128]{1,0:T(8,128)S(1)} %first_plan.1.table_ref, bf16[256,32,256]{2,1,0:T(8,128)(2,1)S(1)} %bitcast.475, bf16[256,32,256]{2,1,0:T(8,128)(2,1)} %collective-permute-done.1.other_ref), custom_call_target="tpu_custom_call" | custom-call | bytes 4096 | tf_op jit(solution)/shard_map/kept_lists/pallas_call | solution.py:334
  19.3 6.5 %plan.1 = (s32[16,128]{1,0:T(8,128)S(1)}, s32[72,128]{1,0:T(8,128)S(1)}) custom-call(s32[3]{0:T(128)S(1)} %pad_add_fusion.where_ref, s32[1,256]{1,0:T(1,128)S(1)} %bitcast.504, s32[1,256]{1,0:T(1,128)S(1)} %bitcast.507, s32[8,64]{1,0:T(8,128)S(1)} %copy-done), custom_call_target="tpu_custom_call" | custom-call | bytes 4096 | tf_op jit(solution)/shard_map/plan/pallas_call | solution.py:255
  25.9 1.9 %before_lists.3 = (bf16[44,32,256]{2,1,0:T(8,128)(2,1)S(1)}, bf16[36,32,256]{2,1,0:T(8,128)(2,1)S(1)}, bf16[50,32,256]{2,1,0:T(8,128)(2,1)S(1)}, bf16[48,32,256]{2,1,0:T(8,128)(2,1)S(1)}) custom-call(s32[16,128]{1,0:T(8,128)S(1)} %get-tuple-element.219.table_ref, bf16[52,32,256]{2,1,0:T(8,128)(2,1)S(1)} %get-tuple-element.164.rest_0_, ...), custom_call_target="tpu_custom_call" | custom-call | bytes 4096 | tf_op jit(solution)/shard_map/before_lists/pallas_call | solution.py:368
  27.8 1.4 %collective-permute-done.5.rest_7_.rest_10_.rest_13_ = bf16[36,32,256]{2,1,0:T(8,128)(2,1)S(1)} collective-permute-done((bf16[36,32,256]{2,1,0:T(8,128)(2,1)S(1)}, bf16[36,32,256]{2,1,0:T(8,128)(2,1)S(1)}, u32[]{:S(2)}, u32[]{:S(2)}) %collective-permute-start.5) | collective-permute-done | bytes 589856 | tf_op jit(solution)/shard_map/ppermute | solution.py:54
  29.2 1.4 %collective-permute-done.4.rest_6_.rest_5_.rest_7_.rest_9_ = bf16[47,32,256]{2,1,0:T(8,128)(2,1)S(1)} collective-permute-done((bf16[47,32,256]{2,1,0:T(8,128)(2,1)S(1)}, bf16[47,32,256]{2,1,0:T(8,128)(2,1)S(1)}, u32[]{:S(2)}, u32[]{:S(2)}) %collective-permute-start.4) | collective-permute-done | bytes 770080 | tf_op jit(solution)/shard_map/ppermute | solution.py:55
  30.6 1.5 %after_lists.3 = (bf16[44,32,256]{2,1,0:T(8,128)(2,1)S(1)}, bf16[36,32,256]{2,1,0:T(8,128)(2,1)S(1)}, bf16[50,32,256]{2,1,0:T(8,128)(2,1)S(1)}, bf16[48,32,256]{2,1,0:T(8,128)(2,1)S(1)}) custom-call(s32[16,128]{1,0:T(8,128)S(1)} %get-tuple-element.219.table_ref, bf16[44,32,256]{2,1,0:T(8,128)(2,1)S(1)} %get-tuple-element.174.rest_0_, ...), custom_call_target="tpu_custom_call" | custom-call | bytes 4096 | tf_op jit(solution)/shard_map/after_lists/pallas_call | solution.py:334
  32.1 2.6 %collective-permute-start.8 = (bf16[50,32,256]{2,1,0:T(8,128)(2,1)S(1)}, bf16[50,32,256]{2,1,0:T(8,128)(2,1)S(1)}, u32[]{:S(2)}, u32[]{:S(2)}) collective-permute-start(bf16[50,32,256]{2,1,0:T(8,128)(2,1)S(1)} %get-tuple-element.184), channel_id=1, source_target_pairs={{0,32},{8,40},{16,48},{24,56},{32,0},{40,8},{48,16},{56,24},{64,96... | collective-permute-start | bytes 2457608 | tf_op jit(solution)/shard_map/ppermute | solution.py:55
  34.6 1.5 %collective-permute-start.9 = (bf16[48,32,256]{2,1,0:T(8,128)(2,1)S(1)}, bf16[48,32,256]{2,1,0:T(8,128)(2,1)S(1)}, u32[]{:S(2)}, u32[]{:S(2)}) collective-permute-start(bf16[48,32,256]{2,1,0:T(8,128)(2,1)S(1)} %get-tuple-element.185), channel_id=1, source_target_pairs={{0,16},{8,24},{16,0},{24,8},{32,48},{40,56},{48,32},{56,40},{64,80... | collective-permute-start | bytes 2359304 | tf_op jit(solution)/shard_map/ppermute | solution.py:55
  36.1 1.9 %collective-permute-start.6 = (bf16[44,32,256]{2,1,0:T(8,128)(2,1)S(1)}, bf16[44,32,256]{2,1,0:T(8,128)(2,1)S(1)}, u32[]{:S(2)}, u32[]{:S(2)}) collective-permute-start(bf16[44,32,256]{2,1,0:T(8,128)(2,1)S(1)} %get-tuple-element.182), channel_id=1, source_target_pairs={{0,1},{1,0},{2,3},{3,2},{4,5},{5,4},{6,7},{7,6},{8,9},{9,8},{10,11... | collective-permute-start | bytes 2162696 | tf_op jit(solution)/shard_map/ppermute | solution.py:54
  38.1 2.9 %before_lists.4 = (bf16[64,32,256]{2,1,0:T(8,128)(2,1)S(1)}, bf16[52,32,256]{2,1,0:T(8,128)(2,1)S(1)}, bf16[47,32,256]{2,1,0:T(8,128)(2,1)S(1)}, bf16[53,32,256]{2,1,0:T(8,128)(2,1)S(1)}) custom-call(s32[16,128]{1,0:T(8,128)S(1)} %get-tuple-element.219.table_ref, bf16[52,32,256]{2,1,0:T(8,128)(2,1)S(1)} %get-tuple-element.164.rest_0_, ...), custom_call_target="tpu_custom_call" | custom-call | bytes 4096 | tf_op jit(solution)/shard_map/before_lists/pallas_call | solution.py:368
  41.0 10.7 %running_rows.2 = (bf16[16,2048]{1,0:T(8,128)(2,1)S(1)}, f32[128,128]{1,0:T(8,128)S(1)}) custom-call(s32[1]{0:T(128)} %bitcast.158.half_ref, s32[768]{0:T(1024)S(1)} %reshape_squeeze.10.pages_ref, s32[128]{0:T(128)S(1)} %reshape_squeeze.11.lens_ref, bf16[80,16,128]{2,1,0:T(8,128)(2,1)S(1)} %bitcast.468, bf16[80,2,256]{2,1,0:T(2,128)(2,1)S(1)} %bitcast.483, ...), custom_call_target="tpu_custom_call" | custom-call | bytes 4096 | tf_op jit(solution)/shard_map/running_rows/pallas_call | solution.py:489
  51.7 0.2 collective-permute-done.7.rest_5_.rest_6_
  51.9 1.3 %collective-permute-done.6.rest_4_.rest_2_ = bf16[44,32,256]{2,1,0:T(8,128)(2,1)S(1)} collective-permute-done((bf16[44,32,256]{2,1,0:T(8,128)(2,1)S(1)}, bf16[44,32,256]{2,1,0:T(8,128)(2,1)S(1)}, u32[]{:S(2)}, u32[]{:S(2)}) %collective-permute-start.6) | collective-permute-done | bytes 720928 | tf_op jit(solution)/shard_map/ppermute | solution.py:54
  53.2 0.0 collective-permute-done.9.rest_7_.rest_11_.rest_14_
  53.2 1.6 %after_lists.4 = (bf16[64,32,256]{2,1,0:T(8,128)(2,1)S(1)}, bf16[52,32,256]{2,1,0:T(8,128)(2,1)S(1)}, bf16[47,32,256]{2,1,0:T(8,128)(2,1)S(1)}, bf16[53,32,256]{2,1,0:T(8,128)(2,1)S(1)}) custom-call(s32[16,128]{1,0:T(8,128)S(1)} %get-tuple-element.219.table_ref, bf16[64,32,256]{2,1,0:T(8,128)(2,1)S(1)} %get-tuple-element.199.rest_0_, ...), custom_call_target="tpu_custom_call" | custom-call | bytes 4096 | tf_op jit(solution)/shard_map/after_lists/pallas_call | solution.py:334
  54.9 0.6 collective-permute-start.10
  55.5 1.5 %collective-permute-start.13 = (bf16[53,32,256]{2,1,0:T(8,128)(2,1)S(1)}, bf16[53,32,256]{2,1,0:T(8,128)(2,1)S(1)}, u32[]{:S(2)}, u32[]{:S(2)}) collective-permute-start(bf16[53,32,256]{2,1,0:T(8,128)(2,1)S(1)} %get-tuple-element.210), channel_id=1, source_target_pairs={{0,32},{8,40},{16,48},{24,56},{32,0},{40,8},{48,16},{56,24},{64,96... | collective-permute-start | bytes 2605064 | tf_op jit(solution)/shard_map/ppermute | solution.py:55
  56.9 1.3 %collective-permute-start.11 = (bf16[52,32,256]{2,1,0:T(8,128)(2,1)S(1)}, bf16[52,32,256]{2,1,0:T(8,128)(2,1)S(1)}, u32[]{:S(2)}, u32[]{:S(2)}) collective-permute-start(bf16[52,32,256]{2,1,0:T(8,128)(2,1)S(1)} %get-tuple-element.208), channel_id=1, source_target_pairs={{0,1},{1,0},{2,3},{3,2},{4,5},{5,4},{6,7},{7,6},{8,9},{9,8},{10,11... | collective-permute-start | bytes 2555912 | tf_op jit(solution)/shard_map/ppermute | solution.py:54
  58.2 1.5 %collective-permute-start.12 = (bf16[47,32,256]{2,1,0:T(8,128)(2,1)S(1)}, bf16[47,32,256]{2,1,0:T(8,128)(2,1)S(1)}, u32[]{:S(2)}, u32[]{:S(2)}) collective-permute-start(bf16[47,32,256]{2,1,0:T(8,128)(2,1)S(1)} %get-tuple-element.209), channel_id=1, source_target_pairs={{0,16},{8,24},{16,0},{24,8},{32,48},{40,56},{48,32},{56,40},{64,80... | collective-permute-start | bytes 2310152 | tf_op jit(solution)/shard_map/ppermute | solution.py:55
  59.7 3.7 %before_lists.5 = (bf16[72,32,256]{2,1,0:T(8,128)(2,1)S(1)}, bf16[68,32,256]{2,1,0:T(8,128)(2,1)S(1)}, bf16[63,32,256]{2,1,0:T(8,128)(2,1)S(1)}, bf16[56,32,256]{2,1,0:T(8,128)(2,1)S(1)}) custom-call(s32[16,128]{1,0:T(8,128)S(1)} %get-tuple-element.219.table_ref, bf16[52,32,256]{2,1,0:T(8,128)(2,1)S(1)} %get-tuple-element.164.rest_0_, ...), custom_call_target="tpu_custom_call" | custom-call | bytes 4096 | tf_op jit(solution)/shard_map/before_lists/pallas_call | solution.py:368
  63.4 16.0 %running_rows.3.rest_1_ = bf16[48,2048]{1,0:T(8,128)(2,1)S(1)} custom-call(s32[1]{0:T(128)} %bitcast.158.half_ref, s32[768]{0:T(1024)S(1)} %reshape_squeeze.10.pages_ref, s32[128]{0:T(128)S(1)} %reshape_squeeze.11.lens_ref, bf16[80,16,128]{2,1,0:T(8,128)(2,1)S(1)} %bitcast.469, bf16[80,2,256]{2,1,0:T(2,128)(2,1)S(1)} %bitcast.484, ...), custom_call_target="tpu_custom_call" | custom-call | bytes 4096 | tf_op jit(solution)/shard_map/running_rows/pallas_call | solution.py:489
  79.5 1.9 %after_lists.5 = (bf16[72,32,256]{2,1,0:T(8,128)(2,1)S(1)}, bf16[68,32,256]{2,1,0:T(8,128)(2,1)S(1)}, bf16[63,32,256]{2,1,0:T(8,128)(2,1)S(1)}, bf16[56,32,256]{2,1,0:T(8,128)(2,1)S(1)}) custom-call(s32[16,128]{1,0:T(8,128)S(1)} %get-tuple-element.219.table_ref, bf16[72,32,256]{2,1,0:T(8,128)(2,1)S(1)} %get-tuple-element.221.rest_0_, ...), custom_call_target="tpu_custom_call" | custom-call | bytes 4096 | tf_op jit(solution)/shard_map/after_lists/pallas_call | solution.py:334
  81.3 1.3 %collective-permute-start.14 = (bf16[72,32,256]{2,1,0:T(8,128)(2,1)S(1)}, bf16[72,32,256]{2,1,0:T(8,128)(2,1)S(1)}, u32[]{:S(2)}, u32[]{:S(2)}) collective-permute-start(bf16[72,32,256]{2,1,0:T(8,128)(2,1)S(1)} %get-tuple-element.229), channel_id=1, source_target_pairs={{0,32},{8,40},{16,48},{24,56},{32,0},{40,8},{48,16},{56,24},{64,96... | collective-permute-start | bytes 3538952 | tf_op jit(solution)/shard_map/ppermute | solution.py:55
  82.6 1.5 %collective-permute-start.15 = (bf16[68,32,256]{2,1,0:T(8,128)(2,1)S(1)}, bf16[68,32,256]{2,1,0:T(8,128)(2,1)S(1)}, u32[]{:S(2)}, u32[]{:S(2)}) collective-permute-start(bf16[68,32,256]{2,1,0:T(8,128)(2,1)S(1)} %get-tuple-element.230), channel_id=1, source_target_pairs={{0,16},{8,24},{16,0},{24,8},{32,48},{40,56},{48,32},{56,40},{64,80... | collective-permute-start | bytes 3342344 | tf_op jit(solution)/shard_map/ppermute | solution.py:55
  84.1 1.9 %collective-permute-start.16 = (bf16[63,32,256]{2,1,0:T(8,128)(2,1)S(1)}, bf16[63,32,256]{2,1,0:T(8,128)(2,1)S(1)}, u32[]{:S(2)}, u32[]{:S(2)}) collective-permute-start(bf16[63,32,256]{2,1,0:T(8,128)(2,1)S(1)} %get-tuple-element.231), channel_id=1, source_target_pairs={{0,1},{1,0},{2,3},{3,2},{4,5},{5,4},{6,7},{7,6},{8,9},{9,8},{10,11... | collective-permute-start | bytes 3096584 | tf_op jit(solution)/shard_map/ppermute | solution.py:54
  86.0 5.6 %early_rows.1.early_ref = bf16[16,2,16,32,256]{4,3,2,1,0:T(8,128)(2,1)S(1)} custom-call(s32[72,128]{1,0:T(8,128)S(1)} %get-tuple-element.233.land_ref, bf16[52,32,256]{2,1,0:T(8,128)(2,1)S(1)} %get-tuple-element.164.rest_0_, bf16[38,32,256]{2,1,0:T(8,128)(2,1)S(1)} %collective-permute-done.2.rest_4_.rest_1_, ...), custom_call_target="tpu_custom_call" | custom-call | bytes 4096 | tf_op jit(solution)/shard_map/early_rows/pallas_call | solution.py:542
  91.7 0.5 slice.796
  92.2 12.8 %collective-permute-done.17.rest_5_ = bf16[56,32,256]{2,1,0:T(8,128)(2,1)S(1)} collective-permute-done((bf16[56,32,256]{2,1,0:T(8,128)(2,1)S(1)}, bf16[56,32,256]{2,1,0:T(8,128)(2,1)S(1)}, u32[]{:S(2)}, u32[]{:S(2)}) %collective-permute-start.17) | collective-permute-done | bytes 917536 | tf_op jit(solution)/shard_map/ppermute | solution.py:55
  105.0 1.0 collective-permute-done.16.rest_4_
  106.0 0.4 collective-permute-done.15.rest_3_
  106.4 0.4 collective-permute-done.14.rest_2_
  106.8 9.5 %land_rows.1 = (bf16[80,2048]{1,0:T(8,128)(2,1)S(1)}, bf16[16,2,16,32,256]{4,3,2,1,0:T(8,128)(2,1)}) custom-call(s32[72,128]{1,0:T(8,128)S(1)} %get-tuple-element.233.land_ref, bf16[80,16,128]{2,1,0:T(8,128)(2,1)S(1)} %bitcast.470, bf16[80,2,256]{2,1,0:T(2,128)(2,1)S(1)} %bitcast.485, bf16[16,2,16,32,256]{4,3,2,1,0:T(8,128)(2,1)S(1)} %early_rows.1.early_ref, ...), custom_call_target="tpu_custom_call" | custom-call | bytes 4096 | tf_op jit(solution)/shard_map/land_rows/pallas_call | solution.py:644
  116.4 0.7 while.12
  117.0 0.7 copy-done.5
  (20 shorter events, 0.1 us)
Async XLA Ops:
  0.6 7.6 %collective-permute-start.1 = (bf16[256,32,256]{2,1,0:T(8,128)(2,1)}, bf16[256,32,256]{2,1,0:T(8,128)(2,1)}, u32[]{:S(2)}, u32[]{:S(2)}) collective-permute-start(bf16[256,32,256]{2,1,0:T(8,128)(2,1)} %bitcast.473), channel_id=1, source_target_pairs={{0,8},{8,0},{16,24},{24,16},{32,40},{40,32},{48,56},{56,48},{64,72... | collective-permute-start | bytes 12582920 | tf_op jit(solution)/shard_map/ppermute | solution.py:55
  5.2 14.1 %copy-start = (s32[8,64]{1,0:T(8,128)S(1)}, s32[8,64]{1,0:T(8,128)}, u32[]{:S(2)}) copy-start(s32[8,64]{1,0:T(8,128)} %constant.173.clone.const_ref) | copy-start | bytes 6148
  5.2 14.1 %copy-start.3 = (s32[256]{0:T(256)S(1)}, s32[256]{0:T(256)}, u32[]{:S(2)}) copy-start(s32[256]{0:T(256)} %param.13) | copy-start | bytes 3076
  5.2 14.1 %copy-start.4 = (s32[256]{0:T(256)S(1)}, s32[256]{0:T(256)}, u32[]{:S(2)}) copy-start(s32[256]{0:T(256)} %param.14) | copy-start | bytes 3076
  8.0 8.2 %copy-start.1 = (bf16[16,1,512,256]{3,2,1,0:T(8,128)(2,1)S(1)}, bf16[16,1,512,256]{3,2,1,0:T(8,128)(2,1)}, u32[]{:S(2)}) copy-start(bf16[16,1,512,256]{3,2,1,0:T(8,128)(2,1)} %param.15) | copy-start | bytes 12582916
  11.2 19.4 %collective-permute-start.4 = (bf16[47,32,256]{2,1,0:T(8,128)(2,1)S(1)}, bf16[47,32,256]{2,1,0:T(8,128)(2,1)S(1)}, u32[]{:S(2)}, u32[]{:S(2)}) collective-permute-start(bf16[47,32,256]{2,1,0:T(8,128)(2,1)S(1)} %get-tuple-element.159), channel_id=1, source_target_pairs={{0,96},{8,104},{16,112},{24,120},{32,64},{40,72},{48,80},{56,88},{... | collective-permute-start | bytes 2310152 | tf_op jit(solution)/shard_map/ppermute | solution.py:55
  11.7 17.5 %collective-permute-start.3 = (bf16[41,32,256]{2,1,0:T(8,128)(2,1)S(1)}, bf16[41,32,256]{2,1,0:T(8,128)(2,1)S(1)}, u32[]{:S(2)}, u32[]{:S(2)}) collective-permute-start(bf16[41,32,256]{2,1,0:T(8,128)(2,1)S(1)} %get-tuple-element.158), channel_id=1, source_target_pairs={{0,32},{8,40},{16,48},{24,56},{32,0},{40,8},{48,16},{56,24},{64,96... | collective-permute-start | bytes 2015240 | tf_op jit(solution)/shard_map/ppermute | solution.py:55
  12.7 16.5 %collective-permute-start.2 = (bf16[38,32,256]{2,1,0:T(8,128)(2,1)S(1)}, bf16[38,32,256]{2,1,0:T(8,128)(2,1)S(1)}, u32[]{:S(2)}, u32[]{:S(2)}) collective-permute-start(bf16[38,32,256]{2,1,0:T(8,128)(2,1)S(1)} %get-tuple-element.157), channel_id=1, source_target_pairs={{0,16},{8,24},{16,0},{24,8},{32,48},{40,56},{48,32},{56,40},{64,80... | collective-permute-start | bytes 1867784 | tf_op jit(solution)/shard_map/ppermute | solution.py:55
  14.3 14.9 %collective-permute-start.5 = (bf16[36,32,256]{2,1,0:T(8,128)(2,1)S(1)}, bf16[36,32,256]{2,1,0:T(8,128)(2,1)S(1)}, u32[]{:S(2)}, u32[]{:S(2)}) collective-permute-start(bf16[36,32,256]{2,1,0:T(8,128)(2,1)S(1)} %get-tuple-element.160), channel_id=1, source_target_pairs={{0,1},{1,0},{2,3},{3,2},{4,5},{5,4},{6,7},{7,6},{8,9},{9,8},{10,11... | collective-permute-start | bytes 1769480 | tf_op jit(solution)/shard_map/ppermute | solution.py:54
  19.3 21.6 %copy-start.2 = (bf16[1,1,80,2,256]{4,3,2,1,0:T(2,128)(2,1)S(1)}, bf16[1,1,80,2,256]{4,3,2,1,0:T(2,128)(2,1)}, u32[]{:S(2)}) copy-start(bf16[1,1,80,2,256]{4,3,2,1,0:T(2,128)(2,1)} %param.20) | copy-start | bytes 245764
  32.1 21.2 %collective-permute-start.8 = (bf16[50,32,256]{2,1,0:T(8,128)(2,1)S(1)}, bf16[50,32,256]{2,1,0:T(8,128)(2,1)S(1)}, u32[]{:S(2)}, u32[]{:S(2)}) collective-permute-start(bf16[50,32,256]{2,1,0:T(8,128)(2,1)S(1)} %get-tuple-element.184), channel_id=1, source_target_pairs={{0,32},{8,40},{16,48},{24,56},{32,0},{40,8},{48,16},{56,24},{64,96... | collective-permute-start | bytes 2457608 | tf_op jit(solution)/shard_map/ppermute | solution.py:55
  34.6 18.6 %collective-permute-start.9 = (bf16[48,32,256]{2,1,0:T(8,128)(2,1)S(1)}, bf16[48,32,256]{2,1,0:T(8,128)(2,1)S(1)}, u32[]{:S(2)}, u32[]{:S(2)}) collective-permute-start(bf16[48,32,256]{2,1,0:T(8,128)(2,1)S(1)} %get-tuple-element.185), channel_id=1, source_target_pairs={{0,16},{8,24},{16,0},{24,8},{32,48},{40,56},{48,32},{56,40},{64,80... | collective-permute-start | bytes 2359304 | tf_op jit(solution)/shard_map/ppermute | solution.py:55
  36.1 17.1 %collective-permute-start.6 = (bf16[44,32,256]{2,1,0:T(8,128)(2,1)S(1)}, bf16[44,32,256]{2,1,0:T(8,128)(2,1)S(1)}, u32[]{:S(2)}, u32[]{:S(2)}) collective-permute-start(bf16[44,32,256]{2,1,0:T(8,128)(2,1)S(1)} %get-tuple-element.182), channel_id=1, source_target_pairs={{0,1},{1,0},{2,3},{3,2},{4,5},{5,4},{6,7},{7,6},{8,9},{9,8},{10,11... | collective-permute-start | bytes 2162696 | tf_op jit(solution)/shard_map/ppermute | solution.py:54
  38.0 13.8 %collective-permute-start.7 = (bf16[36,32,256]{2,1,0:T(8,128)(2,1)S(1)}, bf16[36,32,256]{2,1,0:T(8,128)(2,1)S(1)}, u32[]{:S(2)}, u32[]{:S(2)}) collective-permute-start(bf16[36,32,256]{2,1,0:T(8,128)(2,1)S(1)} %get-tuple-element.183), channel_id=1, source_target_pairs={{0,96},{8,104},{16,112},{24,120},{32,64},{40,72},{48,80},{56,88},{... | collective-permute-start | bytes 1769480 | tf_op jit(solution)/shard_map/ppermute | solution.py:55
  54.9 24.6 %collective-permute-start.10 = (bf16[64,32,256]{2,1,0:T(8,128)(2,1)S(1)}, bf16[64,32,256]{2,1,0:T(8,128)(2,1)S(1)}, u32[]{:S(2)}, u32[]{:S(2)}) collective-permute-start(bf16[64,32,256]{2,1,0:T(8,128)(2,1)S(1)} %get-tuple-element.207), channel_id=1, source_target_pairs={{0,96},{8,104},{16,112},{24,120},{32,64},{40,72},{48,80},{56,88},{... | collective-permute-start | bytes 3145736 | tf_op jit(solution)/shard_map/ppermute | solution.py:55
  55.5 24.0 %collective-permute-start.13 = (bf16[53,32,256]{2,1,0:T(8,128)(2,1)S(1)}, bf16[53,32,256]{2,1,0:T(8,128)(2,1)S(1)}, u32[]{:S(2)}, u32[]{:S(2)}) collective-permute-start(bf16[53,32,256]{2,1,0:T(8,128)(2,1)S(1)} %get-tuple-element.210), channel_id=1, source_target_pairs={{0,32},{8,40},{16,48},{24,56},{32,0},{40,8},{48,16},{56,24},{64,96... | collective-permute-start | bytes 2605064 | tf_op jit(solution)/shard_map/ppermute | solution.py:55
  56.9 22.5 %collective-permute-start.11 = (bf16[52,32,256]{2,1,0:T(8,128)(2,1)S(1)}, bf16[52,32,256]{2,1,0:T(8,128)(2,1)S(1)}, u32[]{:S(2)}, u32[]{:S(2)}) collective-permute-start(bf16[52,32,256]{2,1,0:T(8,128)(2,1)S(1)} %get-tuple-element.208), channel_id=1, source_target_pairs={{0,1},{1,0},{2,3},{3,2},{4,5},{5,4},{6,7},{7,6},{8,9},{9,8},{10,11... | collective-permute-start | bytes 2555912 | tf_op jit(solution)/shard_map/ppermute | solution.py:54
  58.2 21.2 %collective-permute-start.12 = (bf16[47,32,256]{2,1,0:T(8,128)(2,1)S(1)}, bf16[47,32,256]{2,1,0:T(8,128)(2,1)S(1)}, u32[]{:S(2)}, u32[]{:S(2)}) collective-permute-start(bf16[47,32,256]{2,1,0:T(8,128)(2,1)S(1)} %get-tuple-element.209), channel_id=1, source_target_pairs={{0,16},{8,24},{16,0},{24,8},{32,48},{40,56},{48,32},{56,40},{64,80... | collective-permute-start | bytes 2310152 | tf_op jit(solution)/shard_map/ppermute | solution.py:55
  81.3 25.5 %collective-permute-start.14 = (bf16[72,32,256]{2,1,0:T(8,128)(2,1)S(1)}, bf16[72,32,256]{2,1,0:T(8,128)(2,1)S(1)}, u32[]{:S(2)}, u32[]{:S(2)}) collective-permute-start(bf16[72,32,256]{2,1,0:T(8,128)(2,1)S(1)} %get-tuple-element.229), channel_id=1, source_target_pairs={{0,32},{8,40},{16,48},{24,56},{32,0},{40,8},{48,16},{56,24},{64,96... | collective-permute-start | bytes 3538952 | tf_op jit(solution)/shard_map/ppermute | solution.py:55
  82.6 23.8 %collective-permute-start.15 = (bf16[68,32,256]{2,1,0:T(8,128)(2,1)S(1)}, bf16[68,32,256]{2,1,0:T(8,128)(2,1)S(1)}, u32[]{:S(2)}, u32[]{:S(2)}) collective-permute-start(bf16[68,32,256]{2,1,0:T(8,128)(2,1)S(1)} %get-tuple-element.230), channel_id=1, source_target_pairs={{0,16},{8,24},{16,0},{24,8},{32,48},{40,56},{48,32},{56,40},{64,80... | collective-permute-start | bytes 3342344 | tf_op jit(solution)/shard_map/ppermute | solution.py:55
  84.1 21.9 %collective-permute-start.16 = (bf16[63,32,256]{2,1,0:T(8,128)(2,1)S(1)}, bf16[63,32,256]{2,1,0:T(8,128)(2,1)S(1)}, u32[]{:S(2)}, u32[]{:S(2)}) collective-permute-start(bf16[63,32,256]{2,1,0:T(8,128)(2,1)S(1)} %get-tuple-element.231), channel_id=1, source_target_pairs={{0,1},{1,0},{2,3},{3,2},{4,5},{5,4},{6,7},{7,6},{8,9},{9,8},{10,11... | collective-permute-start | bytes 3096584 | tf_op jit(solution)/shard_map/ppermute | solution.py:54
  86.0 19.0 %collective-permute-start.17 = (bf16[56,32,256]{2,1,0:T(8,128)(2,1)S(1)}, bf16[56,32,256]{2,1,0:T(8,128)(2,1)S(1)}, u32[]{:S(2)}, u32[]{:S(2)}) collective-permute-start(bf16[56,32,256]{2,1,0:T(8,128)(2,1)S(1)} %get-tuple-element.232), channel_id=1, source_target_pairs={{0,96},{8,104},{16,112},{24,120},{32,64},{40,72},{48,80},{56,88},{... | collective-permute-start | bytes 2752520 | tf_op jit(solution)/shard_map/ppermute | solution.py:55
  117.0 0.7 copy-start.5
